TPU v7x, 256 devices: a whole 4x4x8 slice. The times are simulated.
256 devices in a mesh: blk: 64 (over x_lo, z, y), rep: 4 (over x_hi, core).
Axes of the slice: x: 4 (x_hi: 2, x_lo: 2; x = x_hi * 2 + x_lo), y: 4, z: 8, core: 2. Of those that a mesh axis runs over, the one named last changes fastest.
Arguments:
- image: bfloat16 [4, 8192, 1536], P('rep', 'blk'), may hold values from -8 to 8
- text: bfloat16 [4, 8192, 1536], P('rep', 'blk'), may hold values from -8 to 8
- log_scale: float32 [], replicated, may hold values from 2.3 to 3
- bias: float32 [], replicated, may hold values from -4 to -1
- head: bfloat16 [1536, 768], replicated, may hold values from -0.15625 to 0.15625
Outputs:
- loss: float32 [], replicated
- scale_grad: float32 [], replicated
- bias_grad: float32 [], replicated
- image_grad: bfloat16 [4, 8192, 1536], P('rep', 'blk')
- text_grad: bfloat16 [4, 8192, 1536], P('rep', 'blk')
- head_grad: float32 [1536, 768], P('blk')
All inputs are finite; a program needn't handle non-finite values.
Results may differ from a plain program's by a relative error of at most 0.0095.
Values may be sent and summed in bfloat16 or wider, within the bound.
No kernel may reach another device: no remote copies, remote signals or barrier semaphores. Data moves between devices by JAX's collectives and lax.ppermute only.
A program may use at most 128 MiB of HBM per device.

v0:
```python
import jax
import jax.numpy as jnp
from jax import lax
from jax.sharding import PartitionSpec as P


def contract_last(left, right):
    return lax.dot_general(
        left, right, (((1,), (1,)), ((), ())), preferred_element_type=jnp.float32
    )


def contract_first(left, right):
    return lax.dot_general(
        left, right, (((0,), (0,)), ((), ())), preferred_element_type=jnp.float32
    )


def project(data, head):
    proj = jnp.dot(data, head, preferred_element_type=jnp.float32)
    norm = jnp.sqrt(jnp.sum(proj * proj, axis=1, keepdims=True) + 1e-06)
    return (proj / norm, norm)


def backnorm(unit, norm, grad):
    return (grad - unit * jnp.sum(unit * grad, axis=1, keepdims=True)) / norm


def pair_block(left, piece, own_start, scale, bias):
    sims = contract_last(left, piece)
    logits = scale * sims + bias
    row_ids = own_start + jnp.arange(left.shape[0], dtype=jnp.int32)
    col_ids = jnp.arange(piece.shape[0], dtype=jnp.int32)
    sign = 2.0 * (row_ids[:, None] == col_ids[None, :]).astype(jnp.float32) - 1.0
    grads = -sign * jax.nn.sigmoid(-sign * logits)
    acc = jnp.dot(grads.astype(jnp.bfloat16), piece, preferred_element_type=jnp.float32)
    return (acc, jnp.sum(jax.nn.softplus(-sign * logits)), jnp.sum(grads * sims), jnp.sum(grads))


def per_device(image, text, log_scale, bias, head):
    xdata = image[0]
    ydata = text[0]
    rows = xdata.shape[0]
    scale = jnp.exp(log_scale)
    unit_img, norm_img = project(xdata, head)
    unit_txt, norm_txt = project(ydata, head)
    u_b = unit_img.astype(jnp.bfloat16)
    v_b = unit_txt.astype(jnp.bfloat16)
    own_start = lax.axis_index("blk") * rows
    acc, lsum, ssum, bsum = pair_block(
        u_b, lax.all_gather(v_b, "blk", axis=0, tiled=True), own_start, scale, bias
    )
    du, lsum, ssum, bsum = (acc, lsum, ssum, bsum)
    acc, unused_l, unused_s, unused_b = pair_block(
        v_b, lax.all_gather(u_b, "blk", axis=0, tiled=True), own_start, scale, bias
    )
    total_l, total_s, total_b = lax.psum((lsum, ssum, bsum), ("blk", "rep"))
    count = (
        float(rows * lax.axis_size("blk"))
        * float(rows * lax.axis_size("blk"))
        * float(lax.axis_size("rep"))
    )
    dimg_b = backnorm(unit_img, norm_img, scale * du).astype(jnp.bfloat16)
    dtxt_b = backnorm(unit_txt, norm_txt, scale * acc).astype(jnp.bfloat16)
    image_grad = contract_last(dimg_b, head).astype(jnp.bfloat16)[None]
    text_grad = contract_last(dtxt_b, head).astype(jnp.bfloat16)[None]
    local_full = contract_first(xdata, dimg_b) + contract_first(ydata, dtxt_b)
    summed = lax.psum(local_full.astype(jnp.bfloat16), "rep").astype(jnp.float32)
    head_grad = lax.psum_scatter(summed, "blk", scatter_dimension=0, tiled=True)
    return (
        total_l / count,
        scale * total_s / count,
        total_b / count,
        image_grad,
        text_grad,
        head_grad,
    )


def solution(mesh):
    placed = (P("rep", "blk", None), P("rep", "blk", None), P(), P(), P())
    return jax.shard_map(
        per_device,
        mesh=mesh,
        in_specs=placed,
        out_specs=(P(), P(), P(), P("rep", "blk", None), P("rep", "blk", None), P("blk", None)),
        check_vma=False,
    )
```

profile of v0, /device:TPU:4, one launch (start us, length us, event | category | flops | bytes accessed | tf_op | source)
XLA Modules:
  0.0 1084.9 jit_solution(8740629556179009276)
XLA Ops:
  7.2 0.0 copy-start
  7.2 0.0 all-gather.3.cloned.1.call-start
  7.2 1.6 copy-done
  8.8 1.6 multiply_reduce_fusion.3
  10.4 0.8 fusion.31
  11.2 0.0 all-gather.3.cloned.1.call-update
  11.2 0.0 all-gather.5.cloned.1.call-start
  11.3 0.0 copy-done.2
  11.3 0.6 multiply_reduce_fusion.4
  11.9 0.8 fusion.30
  12.6 0.0 all-gather.5.cloned.1.call-update
  12.7 0.0 all-reduce.3.cloned.1.call-start
  14.1 0.0 copy-start.6
  14.1 323.1 %all-gather.3.cloned.1.call-done = bf16[8192,768]{1,0:T(8,128)(2,1)} async-done(((bf16[128,768]{1,0:T(8,128)(2,1)}), bf16[8192,768]{1,0:T(8,128)(2,1)}) %all-gather.3.cloned.1.call-update) | async-done | bytes 12582928 | tf_op jit(solution)/shard_map/all_gather | solution.py:51
  337.2 12.1 %fusion.32 = (f32[]{:T(128)}, f32[]{:T(128)}, f32[]{:T(128)}, f32[128,8192]{1,0:T(8,128)S(1)}) fusion(f32[]{:T(128)S(6)} %copy.17, f32[]{:T(128)S(6)} %exp.13, s32[128]{0:T(128)S(1)} %iota_add_fusion, bf16[128,768]{1,0:T(8,128)(2,1)} %fusion.30, bf16[8192,768]{1,0:T(8,128)(2,1)} %all-gather.3.cloned.1.call-done), kind=kOutput, calls=%fused_computation.51 | convolution fusion | flops 1632632832 | bytes 16974356 | tf_op jit(solution)/shard_map/dot_general | solution.py:8
  349.3 0.0 copy-done.6
  349.3 3.2 multiply_reduce_fusion.2
  352.5 0.0 copy-start.4
  352.5 0.7 copy-done.4
  353.3 3.0 fusion.22
  356.3 304.4 %all-gather.5.cloned.1.call-done = bf16[8192,768]{1,0:T(8,128)(2,1)} async-done(((bf16[128,768]{1,0:T(8,128)(2,1)}), bf16[8192,768]{1,0:T(8,128)(2,1)}) %all-gather.5.cloned.1.call-update) | async-done | bytes 12582928 | tf_op jit(solution)/shard_map/all_gather | solution.py:55
  660.6 14.9 %multiply_reduce_fusion.1 = (f32[128]{0:T(128)S(1)}, f32[128,768]{1,0:T(8,128)}) fusion(f32[128,768]{1,0:T(8,128)S(1)} %get-tuple-element.27, f32[128]{0:T(128)S(1)} %add_sqrt_fusion, bf16[8192,768]{1,0:T(8,128)(2,1)} %all-gather.5.cloned.1.call-done, bf16[128,768]{1,0:T(8,128)(2,1)} %fusion.31, f32[]{:T(128)S(6)} %copy.17, f32[]{:T(128)S(6)} %exp.13, ...), kind=kOutput, calls=%fused_computation.35 | convolution fusion | flops 3234201600 | bytes 13567496 | tf_op jit(solution)/shard_map/dot_general | solution.py:36
  675.6 4.8 fusion.9
  680.3 0.0 all-reduce.3.cloned.1.call-update
  680.4 0.0 reduce-scatter.4.cloned.1.call-start
  680.4 63.4 %all-reduce.3.cloned.1.call-done = bf16[1536,768]{0,1:T(8,128)(2,1)} async-done(((bf16[1536,768]{0,1:T(8,128)(2,1)}), bf16[1536,768]{0,1:T(8,128)(2,1)}) %all-reduce.3.cloned.1.call-update) | async-done | bytes 2359312 | tf_op jit(solution)/shard_map/psum | solution.py:68
  743.9 4.5 copy.13
  748.4 0.0 reduce-scatter.4.cloned.1.call-update
  748.4 79.2 %all-reduce = (f32[]{:T(128)}, f32[]{:T(128)}, f32[]{:T(128)}) all-reduce(f32[]{:T(128)} %get-tuple-element.19, f32[]{:T(128)} %get-tuple-element.20, f32[]{:T(128)} %get-tuple-element.18), channel_id=1, replica_groups=mesh['blk'=64,'rep'=4] {'blk','rep'}, use_global_device_ids=true, to_apply=%region_3.4 | all-reduce | flops 3 | bytes 24 | tf_op jit(solution)/shard_map/psum | solution.py:57
  829.6 2.7 fusion.10
  832.3 1.7 fusion.11
  833.9 241.1 %reduce-scatter.4.cloned.1.call-done = f32[24,768]{1,0:T(8,128)} async-done(((f32[1536,768]{1,0:T(8,128)}), f32[24,768]{1,0:T(8,128)}) %reduce-scatter.4.cloned.1.call-update) | async-done | bytes 73744
  (10 shorter events, 0.0 us)
Async XLA Ops:
  7.2 1.7 copy-start
  7.2 4.1 copy-start.2
  7.2 330.0 %all-gather.3.cloned.1.call-start = ((), (), s32[]{:S(2)}) async-start(), calls=%async_computation.1 | async-start | bytes 12779520 | tf_op jit(solution)/shard_map/all_gather | solution.py:51
  11.2 649.4 %all-gather.5.cloned.1.call-start = ((), (), s32[]{:S(2)}) async-start(), calls=%async_computation.2 | async-start | bytes 12779520 | tf_op jit(solution)/shard_map/all_gather | solution.py:55
  12.7 731.2 %all-reduce.3.cloned.1.call-start = ((), (), s32[]{:S(2)}) async-start(), calls=%async_computation.3 | async-start | bytes 4718592 | tf_op jit(solution)/shard_map/psum | solution.py:68
  14.1 335.2 %copy-start.6 = (s32[128]{0:T(128)}, s32[128]{0:T(128)S(1)}, u32[]{:S(2)}) copy-start(s32[128]{0:T(128)S(1)} %iota_add_fusion) | copy-start | bytes 1540
  337.2 12.1 %copy-start.5 = (bf16[8192,768]{1,0:T(8,128)(2,1)S(1)}, bf16[8192,768]{1,0:T(8,128)(2,1)}, u32[]{:S(2)}) copy-start(bf16[8192,768]{1,0:T(8,128)(2,1)} %all-gather.3.cloned.1.call-done) | copy-start | bytes 37748740
  352.5 0.8 copy-start.4
  356.3 319.3 %copy-start.1 = (bf16[1,128,1536]{2,1,0:T(8,128)(2,1)S(1)}, bf16[1,128,1536]{2,1,0:T(8,128)(2,1)}, u32[]{:S(2)}) copy-start(bf16[1,128,1536]{2,1,0:T(8,128)(2,1)} %param.6) | copy-start | bytes 1179652
  680.4 394.7 %reduce-scatter.4.cloned.1.call-start = ((), (), s32[]{:S(2)}) async-start(), calls=%async_computation.4 | async-start | bytes 4792320
  748.4 83.9 %copy-start.3 = (f32[128,768]{1,0:T(8,128)S(1)}, f32[128,768]{1,0:T(8,128)}, u32[]{:S(2)}) copy-start(f32[128,768]{1,0:T(8,128)} %get-tuple-element.32) | copy-start | bytes 1179652
Sparse Core Ops, SparseCore 0:
  11.3 325.8 all-gather.2
  339.6 321.0 all-gather.4
  680.5 63.3 all-reduce.2
  748.5 326.4 reduce-scatter.3
where the time goes:
time: 1090 us; the launch traced here: 1080 us
  waiting for transfers between devices  932 us (86%)
  blocking collectives  79.2 us (7%)
  matrix products  44.4 us (4%)
  between operations  20.5 us (2%)
    all_gather x1, waiting for transfers between devices, per_device(): lax.all_gather(v_b, 'blk', axis=0, tiled=True)  323 us
    all_gather x1, waiting for transfers between devices, per_device(): lax.all_gather(u_b, 'blk', axis=0, tiled=True)  304 us
    unnamed x5, waiting for transfers between devices  241 us
    psum x1, blocking collectives, per_device(): total_l, total_s, total_b = lax.psum((lsum, ssum, bsum), ('blk', 'rep'))  79.2 us
    psum x1, waiting for transfers between devices, per_device(): lax.psum(local_full.astype(jnp.bfloat16), 'rep').astype(jnp.float32)  63.4 us
  transfers between devices with their start and end apart: 4, of which 4 were waited for; matrix products, arithmetic and copies ran while one was open for 2% of the time, Pallas kernels for 0%

commit v1 on v0

v1 whole, which is shorter than its diff:
```python
import functools

import jax
import jax.numpy as jnp
from jax import lax
from jax.experimental import pallas as pl
from jax.experimental.pallas import tpu as pltpu
from jax.sharding import Mesh, PartitionSpec as P

F32 = jnp.float32
BF16 = jnp.bfloat16
LOG2E = 1.4426950408889634
LN2 = 0.6931471805599453
VMEM_LIMIT = 50 * 1024 * 1024
R = 128
E = 768
D = 1536
H = E // 2

NT = (((1,), (1,)), ((), ()))
NN = (((1,), (0,)), ((), ()))
TN = (((0,), (0,)), ((), ()))


def dot(a, b, dims):
    return lax.dot_general(a, b, dims, preferred_element_type=F32)


def vmem_call(kernel, out_shape, scratch=(), smem_first=False, n_in=0, flops=0, nbytes=0):
    specs = [pl.BlockSpec(memory_space=pltpu.VMEM)] * n_in
    if smem_first:
        specs[0] = pl.BlockSpec(memory_space=pltpu.SMEM)
    return pl.pallas_call(
        kernel,
        out_shape=out_shape,
        in_specs=specs,
        out_specs=jax.tree.map(lambda _: pl.BlockSpec(memory_space=pltpu.VMEM), out_shape),
        scratch_shapes=list(scratch),
        compiler_params=pltpu.CompilerParams(vmem_limit_bytes=VMEM_LIMIT),
        cost_estimate=pl.CostEstimate(flops=flops, bytes_accessed=nbytes, transcendentals=0),
    )


def proj_kernel(x_ref, y_ref, head_ref, ui_ref, ni_ref, ub_ref, ut_ref, nt_ref, vb_ref):
    head = head_ref[...]
    for src, unit_ref, norm_ref, b_ref in (
        (y_ref, ut_ref, nt_ref, vb_ref),
        (x_ref, ui_ref, ni_ref, ub_ref),
    ):
        proj = dot(src[...], head, NN)
        norm = jnp.sqrt(jnp.sum(proj * proj, axis=1, keepdims=True) + 1e-06)
        unit = proj / norm
        unit_ref[...] = unit
        norm_ref[...] = norm
        b_ref[...] = unit.astype(BF16)


def project(x, y, head):
    unit = jax.ShapeDtypeStruct((R, E), F32)
    norm = jax.ShapeDtypeStruct((R, 1), F32)
    low = jax.ShapeDtypeStruct((R, E), BF16)
    return vmem_call(
        proj_kernel, (unit, norm, low, unit, norm, low), n_in=3,
        flops=4 * R * D * E, nbytes=2 * (2 * R * D + D * E),
    )(x, y, head)


SUB = 8
CB = 256
RB = 32


def pair_elementwise(s_ref, g_ref, rows, scale2, bias2, own):
    acc_m = jnp.zeros((SUB, CB), F32)
    acc_l = jnp.zeros((SUB, CB), F32)
    acc_s = jnp.zeros((SUB, CB), F32)
    acc_g = jnp.zeros((SUB, CB), F32)

    def fold(t):
        return jnp.sum(t.reshape(RB // SUB, SUB, CB), axis=0)

    for c in range(s_ref.shape[1] // CB):
        prod = jnp.ones((SUB, CB), F32)
        for r in range(rows // RB):
            s = s_ref[r * RB : (r + 1) * RB, c * CB : (c + 1) * CB]
            z = s * scale2 + bias2
            diag = own and c * CB < R
            if diag:
                row = r * RB + lax.broadcasted_iota(jnp.int32, (RB, CB), 0)
                col = c * CB + lax.broadcasted_iota(jnp.int32, (RB, CB), 1)
                mask = row == col
                z = jnp.where(mask, -z, z)
            t = jnp.exp2(-jnp.abs(z))
            one_t = 1.0 + t
            inv = 1.0 / one_t
            g = jnp.where(z >= 0.0, inv, t * inv)
            if diag:
                g = jnp.where(mask, -g, g)
            g_ref[r * RB : (r + 1) * RB, c * CB : (c + 1) * CB] = g.astype(BF16)
            acc_m = acc_m + fold(jnp.maximum(z, 0.0))
            acc_s = acc_s + fold(g * s)
            acc_g = acc_g + fold(g)
            for k in range(RB // SUB):
                prod = prod * one_t[k * SUB : (k + 1) * SUB]
        acc_l = acc_l + jnp.log(prod)
    return LN2 * acc_m + acc_l, acc_s, acc_g


def pair_kernel(chunks, first, scal_ref, *refs):
    n = sum(chunks)
    u_refs, refs = refs[:n], refs[n:]
    v_refs, refs = refs[:6], refs[6:]
    if first:
        du_ref, dv_ref, sums_ref, v_all, u_all, g_all, s_all = refs
    else:
        dv_in, du_ref, near_ref, far_ref, sums_ref, v_all, u_all, g_all, s_all = refs
    scale2 = scal_ref[0, 0]
    bias2 = scal_ref[0, 1]
    at = 0
    for ref in v_refs:
        v_all[at : at + ref.shape[0]] = ref[...]
        at += ref.shape[0]
    for i, ref in enumerate(u_refs):
        u_all[i * R : (i + 1) * R] = ref[...]
    v = v_all[...]
    tot = None
    at = 0
    for i, units in enumerate(chunks):
        rows = units * R
        s_all[i % 2, :rows] = dot(u_all[at : at + rows], v, NT)
        part = pair_elementwise(
            s_all.at[i % 2], g_all.at[pl.ds(at, rows)], rows, scale2, bias2, first and i == 0
        )
        tot = part if tot is None else tuple(a + b for a, b in zip(tot, part))
        du_ref[at : at + rows] = dot(g_all[at : at + rows], v, NN).astype(du_ref.dtype)
        at += rows
    dv = dot(g_all[...], u_all[...], TN)
    if first:
        dv_ref[...] = dv
    else:
        dv = dv + dv_in[...]
        near_ref[...] = dv[:E]
        far_ref[...] = dv[E:].astype(BF16)
    for i in range(3):
        sums_ref[i] = tot[i]


def pair(chunks, first, scal, us, vs, dv_in=None):
    n = sum(chunks)
    cols = 8 * R
    sums = jax.ShapeDtypeStruct((3, SUB, CB), F32)
    if first:
        out = (jax.ShapeDtypeStruct((n * R, E), F32), jax.ShapeDtypeStruct((cols, E), F32), sums)
        extra = ()
    else:
        out = (
            jax.ShapeDtypeStruct((n * R, E), BF16),
            jax.ShapeDtypeStruct((6 * R, E), F32),
            jax.ShapeDtypeStruct((2 * R, E), BF16),
            sums,
        )
        extra = (dv_in,)
    return vmem_call(
        functools.partial(pair_kernel, chunks, first), out,
        scratch=(
            pltpu.VMEM((cols, E), BF16),
            pltpu.VMEM((n * R, E), BF16),
            pltpu.VMEM((n * R, cols), BF16),
            pltpu.VMEM((2, max(chunks) * R, cols), F32),
        ),
        smem_first=True, n_in=1 + n + 6 + len(extra),
        flops=6 * n * R * cols * E, nbytes=4 * (n * R + cols) * E,
    )(scal, *us, *vs, *extra)


def back_kernel(
    scal_ref, ui_ref, ni_ref, du_ref, qa_ref, qb_ref, ut_ref, nt_ref, dv_ref, px_ref,
    di_ref, dt_ref, keep_ref, send_ref,
):
    scale = scal_ref[0, 0]
    low = scal_ref[0, 1] == 0.0
    du = scale * (du_ref[...] + qa_ref[...].astype(F32) + qb_ref[...].astype(F32))
    dv = scale * (dv_ref[...] + px_ref[...].astype(F32))
    for k, (unit_ref, norm_ref, grad, out_ref) in enumerate(
        ((ui_ref, ni_ref, du, di_ref), (ut_ref, nt_ref, dv, dt_ref))
    ):
        unit = unit_ref[...]
        d = (grad - unit * jnp.sum(unit * grad, axis=1, keepdims=True)) / norm_ref[...]
        out_ref[...] = d.astype(BF16)
        left, right = d[:, :H], d[:, H:]
        keep_ref[k * R : (k + 1) * R] = jnp.where(low, left, right).astype(BF16)
        send_ref[k * R : (k + 1) * R] = jnp.where(low, right, left).astype(BF16)


def back(scal, *args):
    low = jax.ShapeDtypeStruct((R, E), BF16)
    half = jax.ShapeDtypeStruct((2 * R, H), BF16)
    return vmem_call(
        back_kernel, (low, low, half, half), smem_first=True, n_in=10,
        flops=20 * R * E, nbytes=30 * R * E,
    )(scal, *args)


def input_grad_kernel(di_ref, dt_ref, head_ref, gi_ref, gt_ref):
    head = head_ref[...]
    gi_ref[...] = dot(di_ref[...], head, NT).astype(BF16)
    gt_ref[...] = dot(dt_ref[...], head, NT).astype(BF16)


def input_grad(di, dt, head):
    out = jax.ShapeDtypeStruct((R, D), BF16)
    return vmem_call(
        input_grad_kernel, (out, out), n_in=3, flops=4 * R * D * E, nbytes=2 * (4 * R * D + D * E)
    )(di, dt, head)


ZROWS = 24
PAD = 16


def head_grad_kernel(x_ref, y_ref, ox_ref, oy_ref, keep_ref, got_ref, extra_ref, out_ref, x_all, d_all):
    for i, ref in enumerate((x_ref, y_ref, ox_ref, oy_ref)):
        x_all[i * R : (i + 1) * R] = ref[...]
    d_all[: 2 * R] = keep_ref[...]
    d_all[2 * R :] = got_ref[...]
    d = d_all[...]
    for xl in range(2):
        full = dot(x_all[:, xl * E : (xl + 1) * E], d, TN)
        for y in range(4):
            for z in range(0, 8, 2):
                a = (z * 4 + y) * ZROWS
                b = ((z + 1) * 4 + y) * ZROWS
                both = jnp.concatenate([full[a : a + ZROWS], full[b : b + ZROWS]], axis=0)
                out_ref[xl * 4 + y, z * ZROWS : (z + 2) * ZROWS] = both.astype(BF16)
    for j in range(8):
        out_ref[j, 8 * ZROWS :] = extra_ref[...]


def head_grad_parts(x, y, ox, oy, keep, got, extra):
    return vmem_call(
        head_grad_kernel, jax.ShapeDtypeStruct((8, 8 * ZROWS + PAD, H), BF16),
        scratch=(pltpu.VMEM((4 * R, D), BF16), pltpu.VMEM((4 * R, H), BF16)),
        n_in=7, flops=8 * R * D * H, nbytes=2 * (4 * R * D + D * H),
    )(x, y, ox, oy, keep, got, extra)


def swap(axis):
    return lambda v: lax.ppermute(v, axis, [(0, 1), (1, 0)])


def ring(axis, n):
    even = [(i, i ^ 1) for i in range(n)]
    odd = [(i, (i + 1) % n if i % 2 else (i - 1) % n) for i in range(n)]
    return (lambda v: lax.ppermute(v, axis, even)), (lambda v: lax.ppermute(v, axis, odd))


def split3(t):
    hi = lax.reduce_precision(t, 8, 7)
    mid = lax.reduce_precision(t - hi, 8, 7)
    return hi, mid, t - hi - mid


def scalar_rows(t, rows):
    parts = jnp.stack(split3(t))
    return jnp.concatenate([parts, jnp.zeros((rows - 3, H), F32)]).astype(BF16)


def per_device(image, text, log_scale, bias, head):
    x = image[0]
    y = text[0]
    scale = jnp.exp(log_scale)
    core = lax.axis_index("c")
    z1, z2 = ring("z", 8)
    y1, y2 = ring("y", 4)
    xl = swap("xl")
    cc = swap("c")

    ui, ni, u, ut, nt, v = project(x, y, head)

    vx = xl(v)
    a1, b1 = z1(u), z2(u)
    w = jnp.concatenate([v, vx])
    wa, wb = y1(w), y2(w)
    a2, b2 = z1(b1), z2(a1)
    wfa, wfb = y1(wb[:R]), y2(wa[R:])
    a3, b3 = z1(b2), z2(a2)
    fa, fb = z1(b3[: R // 2]), z2(a3[R // 2 :])
    vs = (v, vx, wa, wb, wfa, wfb)
    ox, oy = cc(x), cc(y)

    scal = jnp.stack([scale * LOG2E, bias * LOG2E]).reshape(1, 2)
    du, dv, sums1 = pair((1, 2, 2, 2), True, scal, (u, a1, b1, a2, b2, a3, b3), vs)
    far = jnp.concatenate([fa, fb])
    duf, dvn, dvf, sums2 = pair((1,), False, scal, (far,), vs, dv)

    ra, rb = z1(duf[: R // 2]), z2(duf[R // 2 :])
    sa, sb = y1(dvf[:R]), y2(dvf[R:])
    p = [du[i * R : (i + 1) * R] for i in range(7)]
    pad = jnp.zeros((R // 2, E), BF16)
    ra = jnp.concatenate([ra, pad]).astype(F32)
    rb = jnp.concatenate([pad, rb]).astype(F32)
    qa, qb = z1((p[5] + rb).astype(BF16)), z2((p[6] + ra).astype(BF16))
    pad = jnp.zeros((R, E), BF16)
    sa = jnp.concatenate([sa, pad]).astype(F32)
    sb = jnp.concatenate([pad, sb]).astype(F32)
    ta, tb = y1((dvn[2 * R : 4 * R] + sb).astype(BF16)), y2((dvn[4 * R : 6 * R] + sa).astype(BF16))
    qa, qb = z1((p[3] + qb).astype(BF16)), z2((p[4] + qa).astype(BF16))
    wsum = dvn[: 2 * R] + ta.astype(F32) + tb.astype(F32)
    px = xl(wsum[R:].astype(BF16))
    qa, qb = z1((p[1] + qb).astype(BF16)), z2((p[2] + qa).astype(BF16))

    sums = jnp.sum(sums1 + sums2, axis=(1, 2))
    extra = scalar_rows(jnp.zeros((H,), F32).at[:3].set(sums), PAD)

    scal2 = jnp.stack([scale, core.astype(F32)]).reshape(1, 2)
    di, dt, keep, send = back(scal2, ui, ni, p[0], qa, qb, ut, nt, wsum[:R], px)
    got = cc(send)
    gi, gt = input_grad(di, dt, head)

    parts = head_grad_parts(x, y, ox, oy, keep, got, extra)
    parts = lax.all_to_all(parts, ("xl", "y"), 0, 0, tiled=True)
    s = jnp.sum(parts.astype(F32), axis=0)
    t = jnp.sum(s[8 * ZROWS : 8 * ZROWS + 3], axis=0)
    rows = jnp.broadcast_to(scalar_rows(t, 8)[None], (8, 8, H))
    parts = jnp.concatenate([s[: 8 * ZROWS].reshape(8, ZROWS, H).astype(BF16), rows], axis=1)
    parts = lax.all_to_all(parts, "z", 0, 0, tiled=True)
    s = jnp.sum(parts.astype(F32), axis=0)
    s = s + swap("xh")(s)
    o = cc(s)
    hg = jnp.where(
        core == 0,
        jnp.concatenate([s[:ZROWS], o[:ZROWS]], axis=1),
        jnp.concatenate([o[:ZROWS], s[:ZROWS]], axis=1),
    )
    t = jnp.sum(s[ZROWS : ZROWS + 3, :3] + o[ZROWS : ZROWS + 3, :3], axis=0)
    count = float(4 * 8192) * 8192.0
    return t[0] / count, scale * t[1] / count, t[2] / count, gi[None], gt[None], hg


def solution(mesh):
    fine = Mesh(mesh.devices.reshape(2, 8, 4, 2, 2), ("xl", "z", "y", "xh", "c"))
    blk = ("xl", "z", "y")
    rep = ("xh", "c")
    data = P(rep, blk, None)
    return jax.shard_map(
        per_device,
        mesh=fine,
        in_specs=(data, data, P(), P(), P()),
        out_specs=(P(), P(), P(), data, data, P(blk, None)),
        check_vma=False,
    )
```

time: 1090 us -> 159 us (0.15)
  waiting for transfers between devices: 932 us -> 51.9 us
  blocking collectives: 79.2 us -> 15.5 us
  starting transfers between devices: 0.16 us -> 48.8 us
  matrix products: 44.4 us -> 0 us
  Pallas kernels: 0 us -> 20.1 us
  between operations: 20.5 us -> 7.62 us
    all_gather x2 -> x0, waiting for transfers between devices: 627 us -> none  [the longest x1 323 us: per_device(): lax.all_gather(v_b, 'blk', axis=0, tiled=True)]
    unnamed x5 -> x0, waiting for transfers between devices: 241 us -> none
    psum x1 -> x0, blocking collectives: 79.2 us -> none  [per_device(): total_l, total_s, total_b = lax.psum((lsum, ssum, bsum), ('blk', 'rep'))]
    psum x1 -> x0, waiting for transfers between devices: 63.4 us -> none  [per_device(): lax.psum(local_full.astype(jnp.bfloat16), 'rep').astype(jnp.float32)]
    dot_general x9 -> x0, matrix products: 44.4 us -> none  [the longest x2 18.2 us: pair_block(): jnp.dot(grads.astype(jnp.bfloat16), piece, preferred_element_type=jnp.flo...]
    ppermute x0 -> x31, starting transfers between devices: none -> 44.2 us  [the longest x12 33.6 us: ring(): lax.ppermute(v, axis, odd)]
    ppermute x0 -> x31, waiting for transfers between devices: none -> 34.4 us  [the longest x12 15.7 us: ring(): lax.ppermute(v, axis, even)]
    pallas_call x0 -> x6, Pallas kernels: none -> 20.1 us  [the longest x2 13.2 us: pair(): vmem_call(functools.partial(pair_kernel, chunks, first), out, scratch=(pl...]
  transfers between devices with their start and end apart: 4 -> 32, of which waited for: 4 -> 15; matrix products, arithmetic and copies ran while one was open for 2% -> 4% of each run, Pallas kernels for 0% -> 2%
where the time goes in v1:
time: 159 us; the launch traced here: 157 us
  waiting for transfers between devices  51.9 us (33%)
  starting transfers between devices  48.8 us (31%)
  Pallas kernels  20.1 us (13%)
  blocking collectives  15.5 us (10%)
  between operations  7.62 us (5%)
  other arithmetic  7.46 us (5%)
  local copies, waits for them, and re-layouts  5.4 us (3%)
    ppermute x12, starting transfers between devices, ring(): lax.ppermute(v, axis, odd)  33.6 us
    all_to_all x1, waiting for transfers between devices, per_device(): parts = lax.all_to_all(parts, ('xl', 'y'), 0, 0, tiled=True)  17.6 us
    ppermute x12, waiting for transfers between devices, ring(): lax.ppermute(v, axis, even)  15.7 us
    all_to_all x1, blocking collectives, per_device(): parts = lax.all_to_all(parts, 'z', 0, 0, tiled=True)  15.5 us
    pallas_call x2, Pallas kernels, pair(): vmem_call(functools.partial(pair_kernel, chunks, first), out, scratch=(pl...  13.2 us
    ppermute x12, waiting for transfers between devices, ring(): lax.ppermute(v, axis, odd)  11.3 us
    ppermute x7, waiting for transfers between devices, swap(): return lambda v: lax.ppermute(v, axis, [(0, 1), (1, 0)])  7.46 us
    ppermute x12, starting transfers between devices, ring(): lax.ppermute(v, axis, even)  6.81 us
  transfers between devices with their start and end apart: 32, of which 15 were waited for; matrix products, arithmetic and copies ran while one was open for 4% of the time, Pallas kernels for 2%

profile of v1, /device:TPU:4, one launch (start us, length us, event | category | flops | bytes accessed | tf_op | source)
XLA Modules:
  0.0 156.7 jit_solution(11045589569558182896)
XLA Ops:
  2.6 2.6 %shard_map.100 = (f32[128,768]{1,0:T(8,128)S(1)}, f32[128,1]{1,0:T(8,128)S(1)}, bf16[128,768]{1,0:T(8,128)(2,1)S(1)}, f32[128,768]{1,0:T(8,128)S(1)}, f32[128,1]...) custom-call(bf16[128,1536]{1,0:T(8,128)(2,1)S(1)} %bitcast.16, bf16[128,1536]{1,0:T(8,128)(2,1)S(1)} %bitcast.19, ...), custom_call_target="tpu_custom_call" | custom-call | flops 603979776 | bytes 3145728 | tf_op jit(solution)/shard_map/pallas_call | solution.py:62
  6.5 1.9 %collective-permute-start.2 = (bf16[128,768]{1,0:T(8,128)(2,1)S(1)}, bf16[128,768]{1,0:T(8,128)(2,1)S(1)}, u32[]{:S(2)}, u32[]{:S(2)}) collective-permute-start(bf16[128,768]{1,0:T(8,128)(2,1)S(1)} %get-tuple-element.39.refs_0_), channel_id=1, source_target_pairs={{0,16},{16,0},{32,48},{48,32},{64,80},{80,64},{96,112},{112,96},{1... | collective-permute-start | bytes 589832 | tf_op jit(solution)/shard_map/ppermute | solution.py:254
  8.4 4.9 %collective-permute-start.3 = (bf16[128,768]{1,0:T(8,128)(2,1)S(1)}, bf16[128,768]{1,0:T(8,128)(2,1)S(1)}, u32[]{:S(2)}, u32[]{:S(2)}) collective-permute-start(bf16[128,768]{1,0:T(8,128)(2,1)S(1)} %get-tuple-element.39.refs_0_), channel_id=1, source_target_pairs={{0,112},{16,32},{32,16},{48,64},{64,48},{80,96},{96,80},{112,0},{1... | collective-permute-start | bytes 589832 | tf_op jit(solution)/shard_map/ppermute | solution.py:254
  14.7 3.0 %collective-permute-start.10 = (bf16[256,768]{1,0:T(8,128)(2,1)}, bf16[256,768]{1,0:T(8,128)(2,1)S(1)}, u32[]{:S(2)}, u32[]{:S(2)}) collective-permute-start(bf16[256,768]{1,0:T(8,128)(2,1)} %constant_dynamic-update-slice_fusion), channel_id=1, source_target_pairs={{0,12},{4,8},{8,4},{12,0},{1,13},{5,9},{9,5},{13,1},{2,14},{6,10},... | collective-permute-start | bytes 1179656 | tf_op jit(solution)/shard_map/ppermute | solution.py:254
  17.9 4.7 %collective-permute-start.5 = (bf16[128,768]{1,0:T(8,128)(2,1)S(1)}, bf16[128,768]{1,0:T(8,128)(2,1)}, u32[]{:S(2)}, u32[]{:S(2)}) collective-permute-start(bf16[128,768]{1,0:T(8,128)(2,1)S(1)} %collective-permute-done.2.refs_1_), channel_id=1, source_target_pairs={{0,112},{16,32},{32,16},{48,64},{64,48},{80,96},{96,80},{112,0},{1... | collective-permute-start | bytes 589832 | tf_op jit(solution)/shard_map/ppermute | solution.py:254
  23.5 3.7 %collective-permute-start.7 = (bf16[128,768]{1,0:T(8,128)(2,1)S(1)}, bf16[128,768]{1,0:T(8,128)(2,1)S(1)}, u32[]{:S(2)}, u32[]{:S(2)}) collective-permute-start(bf16[128,768]{1,0:T(8,128)(2,1)S(1)} %collective-permute-done.4.refs_3_), channel_id=1, source_target_pairs={{0,112},{16,32},{32,16},{48,64},{64,48},{80,96},{96,80},{112,0},{1... | collective-permute-start | bytes 589832 | tf_op jit(solution)/shard_map/ppermute | solution.py:254
  28.7 2.0 %collective-permute-start.11 = (bf16[128,768]{1,0:T(8,128)(2,1)S(1)}, bf16[128,768]{1,0:T(8,128)(2,1)S(1)}, u32[]{:S(2)}, u32[]{:S(2)}) collective-permute-start(bf16[128,768]{1,0:T(8,128)(2,1)S(1)} %slice.131), channel_id=1, source_target_pairs={{0,4},{4,0},{8,12},{12,8},{1,5},{5,1},{9,13},{13,9},{2,6},{6,2},{1... | collective-permute-start | bytes 589832 | tf_op jit(solution)/shard_map/ppermute | solution.py:254
  30.7 1.5 collective-permute-start.12
  32.2 1.5 collective-permute-start.13
  34.2 3.4 %collective-permute-start.14 = (bf16[64,768]{1,0:T(8,128)(2,1)S(1)}, bf16[64,768]{1,0:T(8,128)(2,1)S(1)}, u32[]{:S(2)}, u32[]{:S(2)}) collective-permute-start(bf16[64,768]{1,0:T(8,128)(2,1)S(1)} %slice.134), channel_id=1, source_target_pairs={{0,112},{16,32},{32,16},{48,64},{64,48},{80,96},{96,80},{112,0},{1... | collective-permute-start | bytes 294920 | tf_op jit(solution)/shard_map/ppermute | solution.py:254
  37.6 2.7 %collective-permute-done.14 = bf16[64,768]{1,0:T(8,128)(2,1)S(1)} collective-permute-done((bf16[64,768]{1,0:T(8,128)(2,1)S(1)}, bf16[64,768]{1,0:T(8,128)(2,1)S(1)}, u32[]{:S(2)}, u32[]{:S(2)}) %collective-permute-start.14) | collective-permute-done | bytes 98336 | tf_op jit(solution)/shard_map/ppermute | solution.py:254
  40.3 8.3 %shard_map.101 = (f32[896,768]{1,0:T(8,128)}, f32[1024,768]{1,0:T(8,128)}, f32[3,8,256]{2,1,0:T(8,128)S(1)}) custom-call(f32[1,2]{1,0:T(1,128)S(1)} %maximum_bitcast_fusion.1.scal_ref, bf16[128,768]{1,0:T(8,128)(2,1)S(1)} %get-tuple-element.39.refs_0_, bf16[128,768]{1,0:T(8,128)(2,1)S(1)} %collective-permute-done.2.refs_1_, ...), custom_call_target="tpu_custom_call" | custom-call | flops 4227858432 | bytes 5898240 | tf_op jit(solution)/shard_map/pallas_call | solution.py:163
  48.6 4.9 %shard_map.102 = (bf16[128,768]{1,0:T(8,128)(2,1)S(1)}, f32[768,768]{1,0:T(8,128)}, bf16[256,768]{1,0:T(8,128)(2,1)S(1)}, f32[3,8,256]{2,1,0:T(8,128)S(1)}) custom-call(f32[1,2]{1,0:T(1,128)S(1)} %maximum_bitcast_fusion.1.scal_ref, bf16[128,768]{1,0:T(8,128)(2,1)S(1)} %pad_maximum_fusion.refs_0_, bf16[128,768]{1,0:T(8,128)(2,1)S(1)} %get-tuple-element.40.refs_7_.refs_1_, ...), custom_call_target="tpu_custom_call" | custom-call | flops 603979776 | bytes 3538944 | tf_op jit(solution)/shard_map/pallas_call | solution.py:163
  53.6 4.6 %collective-permute-done.19 = bf16[64,768]{1,0:T(8,128)(2,1)S(1)} collective-permute-done((bf16[64,768]{1,0:T(8,128)(2,1)S(1)}, bf16[64,768]{1,0:T(8,128)(2,1)S(1)}, u32[]{:S(2)}, u32[]{:S(2)}) %collective-permute-start.19) | collective-permute-done | bytes 98336 | tf_op jit(solution)/shard_map/ppermute | solution.py:254
  58.3 3.2 %collective-permute-start.20 = (bf16[128,768]{1,0:T(8,128)(2,1)S(1)}, bf16[128,768]{1,0:T(8,128)(2,1)S(1)}, u32[]{:S(2)}, u32[]{:S(2)}) collective-permute-start(bf16[128,768]{1,0:T(8,128)(2,1)S(1)} %add_convert_fusion.4), channel_id=1, source_target_pairs={{0,112},{16,32},{32,16},{48,64},{64,48},{80,96},{96,80},{112,0},{1... | collective-permute-start | bytes 589832 | tf_op jit(solution)/shard_map/ppermute | solution.py:254
  61.6 3.6 %collective-permute-done.20 = bf16[128,768]{1,0:T(8,128)(2,1)S(1)} collective-permute-done((bf16[128,768]{1,0:T(8,128)(2,1)S(1)}, bf16[128,768]{1,0:T(8,128)(2,1)S(1)}, u32[]{:S(2)}, u32[]{:S(2)}) %collective-permute-start.20) | collective-permute-done | bytes 196640 | tf_op jit(solution)/shard_map/ppermute | solution.py:254
  65.4 2.2 %collective-permute-start.23 = (bf16[128,768]{1,0:T(8,128)(2,1)S(1)}, bf16[128,768]{1,0:T(8,128)(2,1)S(1)}, u32[]{:S(2)}, u32[]{:S(2)}) collective-permute-start(bf16[128,768]{1,0:T(8,128)(2,1)S(1)} %get-tuple-element.61), channel_id=1, source_target_pairs={{0,12},{4,8},{8,4},{12,0},{1,13},{5,9},{9,5},{13,1},{2,14},{6,10},... | collective-permute-start | bytes 589832 | tf_op jit(solution)/shard_map/ppermute | solution.py:254
  67.6 3.4 %collective-permute-done.21 = bf16[128,768]{1,0:T(8,128)(2,1)S(1)} collective-permute-done((bf16[128,768]{1,0:T(8,128)(2,1)S(1)}, bf16[128,768]{1,0:T(8,128)(2,1)S(1)}, u32[]{:S(2)}, u32[]{:S(2)}) %collective-permute-start.21) | collective-permute-done | bytes 196640 | tf_op jit(solution)/shard_map/ppermute | solution.py:254
  71.2 3.3 %collective-permute-done.23 = bf16[128,768]{1,0:T(8,128)(2,1)S(1)} collective-permute-done((bf16[128,768]{1,0:T(8,128)(2,1)S(1)}, bf16[128,768]{1,0:T(8,128)(2,1)S(1)}, u32[]{:S(2)}, u32[]{:S(2)}) %collective-permute-start.23) | collective-permute-done | bytes 196640 | tf_op jit(solution)/shard_map/ppermute | solution.py:254
  76.4 1.5 collective-permute-start.26
  78.6 2.7 %collective-permute-start.22 = (bf16[128,768]{1,0:T(8,128)(2,1)S(1)}, bf16[128,768]{1,0:T(8,128)(2,1)S(1)}, u32[]{:S(2)}, u32[]{:S(2)}) collective-permute-start(bf16[128,768]{1,0:T(8,128)(2,1)S(1)} %get-tuple-element.56), channel_id=1, source_target_pairs={{0,112},{16,32},{32,16},{48,64},{64,48},{80,96},{96,80},{112,0},{1... | collective-permute-start | bytes 589832 | tf_op jit(solution)/shard_map/ppermute | solution.py:254
  82.4 1.8 %collective-permute-done.24 = bf16[256,768]{1,0:T(8,128)(2,1)} collective-permute-done((bf16[256,768]{1,0:T(8,128)(2,1)}, bf16[256,768]{1,0:T(8,128)(2,1)}, u32[]{:S(2)}, u32[]{:S(2)}) %collective-permute-start.24) | collective-permute-done | bytes 393248 | tf_op jit(solution)/shard_map/ppermute | solution.py:254
  84.2 2.5 %collective-permute-start.17 = (bf16[128,768]{1,0:T(8,128)(2,1)S(1)}, bf16[128,768]{1,0:T(8,128)(2,1)S(1)}, u32[]{:S(2)}, u32[]{:S(2)}) collective-permute-start(bf16[128,768]{1,0:T(8,128)(2,1)S(1)} %add_convert_fusion.6), channel_id=1, source_target_pairs={{0,112},{16,32},{32,16},{48,64},{64,48},{80,96},{96,80},{112,0},{1... | collective-permute-start | bytes 589832 | tf_op jit(solution)/shard_map/ppermute | solution.py:254
  86.7 1.5 convert_add_fusion
  89.5 1.6 %collective-permute-done.17 = bf16[128,768]{1,0:T(8,128)(2,1)S(1)} collective-permute-done((bf16[128,768]{1,0:T(8,128)(2,1)S(1)}, bf16[128,768]{1,0:T(8,128)(2,1)S(1)}, u32[]{:S(2)}, u32[]{:S(2)}) %collective-permute-start.17) | collective-permute-done | bytes 196640 | tf_op jit(solution)/shard_map/ppermute | solution.py:254
  94.0 3.9 %collective-permute-done.18.qa_ref = bf16[128,768]{1,0:T(8,128)(2,1)S(1)} collective-permute-done((bf16[128,768]{1,0:T(8,128)(2,1)S(1)}, bf16[128,768]{1,0:T(8,128)(2,1)S(1)}, u32[]{:S(2)}, u32[]{:S(2)}) %collective-permute-start.18) | collective-permute-done | bytes 196640 | tf_op jit(solution)/shard_map/ppermute | solution.py:254
  102.5 4.6 %all-to-all-start = ((bf16[8,208,384]{2,1,0:T(8,128)(2,1)}), bf16[8,208,384]{2,1,0:T(8,128)(2,1)}, u32[]{:S(2)}, u32[]{:S(2)}) async-start(bf16[8,208,384]{2,1,0:T(8,128)(2,1)} %copy-done.1), calls=%async_computation | async-start | bytes 2555904 | tf_op jit(solution)/shard_map/all_to_all | solution.py:321
  107.2 17.6 %all-to-all-done = bf16[8,208,384]{2,1,0:T(8,128)(2,1)} async-done(((bf16[8,208,384]{2,1,0:T(8,128)(2,1)}), bf16[8,208,384]{2,1,0:T(8,128)(2,1)}, u32[]{:S(2)}, u32[]{:S(2)}) %all-to-all-start) | async-done | bytes 1277984 | tf_op jit(solution)/shard_map/all_to_all | solution.py:321
  124.7 1.5 convert_reduce_fusion
  126.4 15.5 %all_to_all.10 = bf16[8,32,384]{2,1,0:T(8,128)(2,1)S(1)} all-to-all(bf16[8,32,384]{2,1,0:T(8,128)(2,1)S(1)} %pad_maximum_fusion.1), channel_id=1, replica_groups=mesh['xl'=2,'z'=8,'y'=4,'xh'=2,'c'=2] {'z'}, dimensions={0} | all-to-all | bytes 393216 | tf_op jit(solution)/shard_map/all_to_all | solution.py:326
  142.5 5.1 %collective-permute-done.29 = f32[32,384]{1,0:T(8,128)S(1)} collective-permute-done((f32[32,384]{1,0:T(8,128)S(1)}, f32[32,384]{1,0:T(8,128)S(1)}, u32[]{:S(2)}, u32[]{:S(2)}) %collective-permute-start.29) | collective-permute-done | bytes 49184 | tf_op jit(solution)/shard_map/ppermute | solution.py:248
  147.7 2.4 %shard_map.105 = (bf16[128,1536]{1,0:T(8,128)(2,1)}, bf16[128,1536]{1,0:T(8,128)(2,1)}) custom-call(bf16[128,768]{1,0:T(8,128)(2,1)S(1)} %get-tuple-element.52.di_ref, bf16[128,768]{1,0:T(8,128)(2,1)S(1)} %get-tuple-element.53.dt_ref, bf16[1536,768]{1,0:T(8,128)(2,1)S(1)} %copy-done), custom_call_target="tpu_custom_call" | custom-call | flops 603979776 | bytes 3932160 | tf_op jit(solution)/shard_map/pallas_call | solution.py:212
  (99 shorter events, 21.4 us)
Async XLA Ops:
  5.2 8.8 %collective-permute-start.8 = (bf16[128,768]{1,0:T(8,128)(2,1)S(1)}, bf16[128,768]{1,0:T(8,128)(2,1)S(1)}, u32[]{:S(2)}, u32[]{:S(2)}) collective-permute-start(bf16[128,768]{1,0:T(8,128)(2,1)S(1)} %get-tuple-element.40.refs_7_.refs_1_), channel_id=1, source_target_pairs={{0,128},{128,0},{1,129},{129,1},{2,130},{130,2},{3,131},{131,3},{4... | collective-permute-start | bytes 589832 | tf_op jit(solution)/shard_map/ppermute | solution.py:248
  6.5 11.4 %collective-permute-start.2 = (bf16[128,768]{1,0:T(8,128)(2,1)S(1)}, bf16[128,768]{1,0:T(8,128)(2,1)S(1)}, u32[]{:S(2)}, u32[]{:S(2)}) collective-permute-start(bf16[128,768]{1,0:T(8,128)(2,1)S(1)} %get-tuple-element.39.refs_0_), channel_id=1, source_target_pairs={{0,16},{16,0},{32,48},{48,32},{64,80},{80,64},{96,112},{112,96},{1... | collective-permute-start | bytes 589832 | tf_op jit(solution)/shard_map/ppermute | solution.py:254
  8.4 9.5 %collective-permute-start.3 = (bf16[128,768]{1,0:T(8,128)(2,1)S(1)}, bf16[128,768]{1,0:T(8,128)(2,1)S(1)}, u32[]{:S(2)}, u32[]{:S(2)}) collective-permute-start(bf16[128,768]{1,0:T(8,128)(2,1)S(1)} %get-tuple-element.39.refs_0_), channel_id=1, source_target_pairs={{0,112},{16,32},{32,16},{48,64},{64,48},{80,96},{96,80},{112,0},{1... | collective-permute-start | bytes 589832 | tf_op jit(solution)/shard_map/ppermute | solution.py:254
  14.7 13.9 %collective-permute-start.10 = (bf16[256,768]{1,0:T(8,128)(2,1)}, bf16[256,768]{1,0:T(8,128)(2,1)S(1)}, u32[]{:S(2)}, u32[]{:S(2)}) collective-permute-start(bf16[256,768]{1,0:T(8,128)(2,1)} %constant_dynamic-update-slice_fusion), channel_id=1, source_target_pairs={{0,12},{4,8},{8,4},{12,0},{1,13},{5,9},{9,5},{13,1},{2,14},{6,10},... | collective-permute-start | bytes 1179656 | tf_op jit(solution)/shard_map/ppermute | solution.py:254
  17.7 12.9 %collective-permute-start.9 = (bf16[256,768]{1,0:T(8,128)(2,1)}, bf16[256,768]{1,0:T(8,128)(2,1)S(1)}, u32[]{:S(2)}, u32[]{:S(2)}) collective-permute-start(bf16[256,768]{1,0:T(8,128)(2,1)} %constant_dynamic-update-slice_fusion), channel_id=1, source_target_pairs={{0,4},{4,0},{8,12},{12,8},{1,5},{5,1},{9,13},{13,9},{2,6},{6,2},{1... | collective-permute-start | bytes 1179656 | tf_op jit(solution)/shard_map/ppermute | solution.py:254
  17.9 5.7 %collective-permute-start.4 = (bf16[128,768]{1,0:T(8,128)(2,1)S(1)}, bf16[128,768]{1,0:T(8,128)(2,1)S(1)}, u32[]{:S(2)}, u32[]{:S(2)}) collective-permute-start(bf16[128,768]{1,0:T(8,128)(2,1)S(1)} %collective-permute-done.3.refs_2_), channel_id=1, source_target_pairs={{0,16},{16,0},{32,48},{48,32},{64,80},{80,64},{96,112},{112,96},{1... | collective-permute-start | bytes 589832 | tf_op jit(solution)/shard_map/ppermute | solution.py:254
  17.9 9.4 %collective-permute-start.5 = (bf16[128,768]{1,0:T(8,128)(2,1)S(1)}, bf16[128,768]{1,0:T(8,128)(2,1)}, u32[]{:S(2)}, u32[]{:S(2)}) collective-permute-start(bf16[128,768]{1,0:T(8,128)(2,1)S(1)} %collective-permute-done.2.refs_1_), channel_id=1, source_target_pairs={{0,112},{16,32},{32,16},{48,64},{64,48},{80,96},{96,80},{112,0},{1... | collective-permute-start | bytes 589832 | tf_op jit(solution)/shard_map/ppermute | solution.py:254
  23.5 8.7 %collective-permute-start.7 = (bf16[128,768]{1,0:T(8,128)(2,1)S(1)}, bf16[128,768]{1,0:T(8,128)(2,1)S(1)}, u32[]{:S(2)}, u32[]{:S(2)}) collective-permute-start(bf16[128,768]{1,0:T(8,128)(2,1)S(1)} %collective-permute-done.4.refs_3_), channel_id=1, source_target_pairs={{0,112},{16,32},{32,16},{48,64},{64,48},{80,96},{96,80},{112,0},{1... | collective-permute-start | bytes 589832 | tf_op jit(solution)/shard_map/ppermute | solution.py:254
  27.3 6.8 %collective-permute-start.6 = (bf16[128,768]{1,0:T(8,128)(2,1)}, bf16[128,768]{1,0:T(8,128)(2,1)S(1)}, u32[]{:S(2)}, u32[]{:S(2)}) collective-permute-start(bf16[128,768]{1,0:T(8,128)(2,1)} %collective-permute-done.5.refs_4_), channel_id=1, source_target_pairs={{0,16},{16,0},{32,48},{48,32},{64,80},{80,64},{96,112},{112,96},{1... | collective-permute-start | bytes 589832 | tf_op jit(solution)/shard_map/ppermute | solution.py:254
  28.7 11.6 %collective-permute-start.11 = (bf16[128,768]{1,0:T(8,128)(2,1)S(1)}, bf16[128,768]{1,0:T(8,128)(2,1)S(1)}, u32[]{:S(2)}, u32[]{:S(2)}) collective-permute-start(bf16[128,768]{1,0:T(8,128)(2,1)S(1)} %slice.131), channel_id=1, source_target_pairs={{0,4},{4,0},{8,12},{12,8},{1,5},{5,1},{9,13},{13,9},{2,6},{6,2},{1... | collective-permute-start | bytes 589832 | tf_op jit(solution)/shard_map/ppermute | solution.py:254
  30.7 9.6 %collective-permute-start.12 = (bf16[128,768]{1,0:T(8,128)(2,1)S(1)}, bf16[128,768]{1,0:T(8,128)(2,1)S(1)}, u32[]{:S(2)}, u32[]{:S(2)}) collective-permute-start(bf16[128,768]{1,0:T(8,128)(2,1)S(1)} %slice.132), channel_id=1, source_target_pairs={{0,12},{4,8},{8,4},{12,0},{1,13},{5,9},{9,5},{13,1},{2,14},{6,10},... | collective-permute-start | bytes 589832 | tf_op jit(solution)/shard_map/ppermute | solution.py:254
  32.2 5.4 %collective-permute-start.13 = (bf16[64,768]{1,0:T(8,128)(2,1)S(1)}, bf16[64,768]{1,0:T(8,128)(2,1)S(1)}, u32[]{:S(2)}, u32[]{:S(2)}) collective-permute-start(bf16[64,768]{1,0:T(8,128)(2,1)S(1)} %slice.133), channel_id=1, source_target_pairs={{0,16},{16,0},{32,48},{48,32},{64,80},{80,64},{96,112},{112,96},{1... | collective-permute-start | bytes 294920 | tf_op jit(solution)/shard_map/ppermute | solution.py:254
  34.2 6.1 %collective-permute-start.14 = (bf16[64,768]{1,0:T(8,128)(2,1)S(1)}, bf16[64,768]{1,0:T(8,128)(2,1)S(1)}, u32[]{:S(2)}, u32[]{:S(2)}) collective-permute-start(bf16[64,768]{1,0:T(8,128)(2,1)S(1)} %slice.134), channel_id=1, source_target_pairs={{0,112},{16,32},{32,16},{48,64},{64,48},{80,96},{96,80},{112,0},{1... | collective-permute-start | bytes 294920 | tf_op jit(solution)/shard_map/ppermute | solution.py:254
  53.5 4.7 %collective-permute-start.19 = (bf16[64,768]{1,0:T(8,128)(2,1)S(1)}, bf16[64,768]{1,0:T(8,128)(2,1)S(1)}, u32[]{:S(2)}, u32[]{:S(2)}) collective-permute-start(bf16[64,768]{1,0:T(8,128)(2,1)S(1)} %get-tuple-element.63), channel_id=1, source_target_pairs={{0,16},{16,0},{32,48},{48,32},{64,80},{80,64},{96,112},{112,96},{1... | collective-permute-start | bytes 294920 | tf_op jit(solution)/shard_map/ppermute | solution.py:254
  58.3 7.0 %collective-permute-start.20 = (bf16[128,768]{1,0:T(8,128)(2,1)S(1)}, bf16[128,768]{1,0:T(8,128)(2,1)S(1)}, u32[]{:S(2)}, u32[]{:S(2)}) collective-permute-start(bf16[128,768]{1,0:T(8,128)(2,1)S(1)} %add_convert_fusion.4), channel_id=1, source_target_pairs={{0,112},{16,32},{32,16},{48,64},{64,48},{80,96},{96,80},{112,0},{1... | collective-permute-start | bytes 589832 | tf_op jit(solution)/shard_map/ppermute | solution.py:254
  61.4 6.2 %collective-permute-start.15 = (bf16[64,768]{1,0:T(8,128)(2,1)S(1)}, bf16[64,768]{1,0:T(8,128)(2,1)S(1)}, u32[]{:S(2)}, u32[]{:S(2)}) collective-permute-start(bf16[64,768]{1,0:T(8,128)(2,1)S(1)} %get-tuple-element.64), channel_id=1, source_target_pairs={{0,112},{16,32},{32,16},{48,64},{64,48},{80,96},{96,80},{112,0},{1... | collective-permute-start | bytes 294920 | tf_op jit(solution)/shard_map/ppermute | solution.py:254
  65.3 5.8 %collective-permute-start.21 = (bf16[128,768]{1,0:T(8,128)(2,1)S(1)}, bf16[128,768]{1,0:T(8,128)(2,1)S(1)}, u32[]{:S(2)}, u32[]{:S(2)}) collective-permute-start(bf16[128,768]{1,0:T(8,128)(2,1)S(1)} %add_convert_fusion.3), channel_id=1, source_target_pairs={{0,16},{16,0},{32,48},{48,32},{64,80},{80,64},{96,112},{112,96},{1... | collective-permute-start | bytes 589832 | tf_op jit(solution)/shard_map/ppermute | solution.py:254
  65.4 9.1 %collective-permute-start.23 = (bf16[128,768]{1,0:T(8,128)(2,1)S(1)}, bf16[128,768]{1,0:T(8,128)(2,1)S(1)}, u32[]{:S(2)}, u32[]{:S(2)}) collective-permute-start(bf16[128,768]{1,0:T(8,128)(2,1)S(1)} %get-tuple-element.61), channel_id=1, source_target_pairs={{0,12},{4,8},{8,4},{12,0},{1,13},{5,9},{9,5},{13,1},{2,14},{6,10},... | collective-permute-start | bytes 589832 | tf_op jit(solution)/shard_map/ppermute | solution.py:254
  67.6 7.5 %collective-permute-start.25 = (bf16[128,768]{1,0:T(8,128)(2,1)S(1)}, bf16[128,768]{1,0:T(8,128)(2,1)S(1)}, u32[]{:S(2)}, u32[]{:S(2)}) collective-permute-start(bf16[128,768]{1,0:T(8,128)(2,1)S(1)} %get-tuple-element.62), channel_id=1, source_target_pairs={{0,4},{4,0},{8,12},{12,8},{1,5},{5,1},{9,13},{13,9},{2,6},{6,2},{1... | collective-permute-start | bytes 589832 | tf_op jit(solution)/shard_map/ppermute | solution.py:254
  71.1 7.5 %collective-permute-start.16 = (bf16[128,768]{1,0:T(8,128)(2,1)S(1)}, bf16[128,768]{1,0:T(8,128)(2,1)}, u32[]{:S(2)}, u32[]{:S(2)}) collective-permute-start(bf16[128,768]{1,0:T(8,128)(2,1)S(1)} %get-tuple-element.57), channel_id=1, source_target_pairs={{0,16},{16,0},{32,48},{48,32},{64,80},{80,64},{96,112},{112,96},{1... | collective-permute-start | bytes 589832 | tf_op jit(solution)/shard_map/ppermute | solution.py:254
  76.1 8.1 %collective-permute-start.24 = (bf16[256,768]{1,0:T(8,128)(2,1)}, bf16[256,768]{1,0:T(8,128)(2,1)}, u32[]{:S(2)}, u32[]{:S(2)}) collective-permute-start(bf16[256,768]{1,0:T(8,128)(2,1)} %get-tuple-element.59), channel_id=1, source_target_pairs={{0,4},{4,0},{8,12},{12,8},{1,5},{5,1},{9,13},{13,9},{2,6},{6,2},{1... | collective-permute-start | bytes 1179656 | tf_op jit(solution)/shard_map/ppermute | solution.py:254
  76.4 10.3 %collective-permute-start.26 = (bf16[256,768]{1,0:T(8,128)(2,1)}, bf16[256,768]{1,0:T(8,128)(2,1)}, u32[]{:S(2)}, u32[]{:S(2)}) collective-permute-start(bf16[256,768]{1,0:T(8,128)(2,1)} %get-tuple-element.60), channel_id=1, source_target_pairs={{0,12},{4,8},{8,4},{12,0},{1,13},{5,9},{9,5},{13,1},{2,14},{6,10},... | collective-permute-start | bytes 1179656 | tf_op jit(solution)/shard_map/ppermute | solution.py:254
  77.9 21.1 %collective-permute-start = (bf16[128,1536]{1,0:T(8,128)(2,1)S(1)}, bf16[128,1536]{1,0:T(8,128)(2,1)S(1)}, u32[]{:S(2)}, u32[]{:S(2)}) collective-permute-start(bf16[128,1536]{1,0:T(8,128)(2,1)S(1)} %bitcast.17), channel_id=1, source_target_pairs={{0,1},{1,0},{2,3},{3,2},{4,5},{5,4},{6,7},{7,6},{8,9},{9,8},{10,11... | collective-permute-start | bytes 1179656 | tf_op jit(solution)/shard_map/ppermute | solution.py:248
  77.9 21.1 %collective-permute-start.1 = (bf16[128,1536]{1,0:T(8,128)(2,1)S(1)}, bf16[128,1536]{1,0:T(8,128)(2,1)S(1)}, u32[]{:S(2)}, u32[]{:S(2)}) collective-permute-start(bf16[128,1536]{1,0:T(8,128)(2,1)S(1)} %bitcast.20), channel_id=1, source_target_pairs={{0,1},{1,0},{2,3},{3,2},{4,5},{5,4},{6,7},{7,6},{8,9},{9,8},{10,11... | collective-permute-start | bytes 1179656 | tf_op jit(solution)/shard_map/ppermute | solution.py:248
  78.6 14.4 %collective-permute-start.22 = (bf16[128,768]{1,0:T(8,128)(2,1)S(1)}, bf16[128,768]{1,0:T(8,128)(2,1)S(1)}, u32[]{:S(2)}, u32[]{:S(2)}) collective-permute-start(bf16[128,768]{1,0:T(8,128)(2,1)S(1)} %get-tuple-element.56), channel_id=1, source_target_pairs={{0,112},{16,32},{32,16},{48,64},{64,48},{80,96},{96,80},{112,0},{1... | collective-permute-start | bytes 589832 | tf_op jit(solution)/shard_map/ppermute | solution.py:254
  84.2 6.9 %collective-permute-start.17 = (bf16[128,768]{1,0:T(8,128)(2,1)S(1)}, bf16[128,768]{1,0:T(8,128)(2,1)S(1)}, u32[]{:S(2)}, u32[]{:S(2)}) collective-permute-start(bf16[128,768]{1,0:T(8,128)(2,1)S(1)} %add_convert_fusion.6), channel_id=1, source_target_pairs={{0,112},{16,32},{32,16},{48,64},{64,48},{80,96},{96,80},{112,0},{1... | collective-permute-start | bytes 589832 | tf_op jit(solution)/shard_map/ppermute | solution.py:254
  88.3 5.8 %collective-permute-start.27 = (bf16[128,768]{1,0:T(8,128)(2,1)S(1)}, bf16[128,768]{1,0:T(8,128)(2,1)S(1)}, u32[]{:S(2)}, u32[]{:S(2)}) collective-permute-start(bf16[128,768]{1,0:T(8,128)(2,1)S(1)} %slice.159), channel_id=1, source_target_pairs={{0,128},{128,0},{1,129},{129,1},{2,130},{130,2},{3,131},{131,3},{4... | collective-permute-start | bytes 589832 | tf_op jit(solution)/shard_map/ppermute | solution.py:248
  92.2 5.8 %collective-permute-start.18 = (bf16[128,768]{1,0:T(8,128)(2,1)S(1)}, bf16[128,768]{1,0:T(8,128)(2,1)S(1)}, u32[]{:S(2)}, u32[]{:S(2)}) collective-permute-start(bf16[128,768]{1,0:T(8,128)(2,1)S(1)} %add_convert_fusion.5), channel_id=1, source_target_pairs={{0,16},{16,0},{32,48},{48,32},{64,80},{80,64},{96,112},{112,96},{1... | collective-permute-start | bytes 589832 | tf_op jit(solution)/shard_map/ppermute | solution.py:254
  98.9 1.5 collective-permute-start.28
  102.5 22.3 %all-to-all-start = ((bf16[8,208,384]{2,1,0:T(8,128)(2,1)}), bf16[8,208,384]{2,1,0:T(8,128)(2,1)}, u32[]{:S(2)}, u32[]{:S(2)}) async-start(bf16[8,208,384]{2,1,0:T(8,128)(2,1)} %copy-done.1), calls=%async_computation | async-start | bytes 2555904 | tf_op jit(solution)/shard_map/all_to_all | solution.py:321
  141.9 5.7 %collective-permute-start.29 = (f32[32,384]{1,0:T(8,128)S(1)}, f32[32,384]{1,0:T(8,128)S(1)}, u32[]{:S(2)}, u32[]{:S(2)}) collective-permute-start(f32[32,384]{1,0:T(8,128)S(1)} %convert_reduce_fusion.1), channel_id=1, source_target_pairs={{0,2},{2,0},{1,3},{3,1},{4,6},{6,4},{5,7},{7,5},{8,10},{10,8},{9,1... | collective-permute-start | bytes 147464 | tf_op jit(solution)/shard_map/ppermute | solution.py:248
  147.6 2.5 %collective-permute-start.30 = (f32[32,384]{1,0:T(8,128)S(1)}, f32[32,384]{1,0:T(8,128)S(1)}, u32[]{:S(2)}, u32[]{:S(2)}) collective-permute-start(f32[32,384]{1,0:T(8,128)S(1)} %add.62), channel_id=1, source_target_pairs={{0,1},{1,0},{2,3},{3,2},{4,5},{5,4},{6,7},{7,6},{8,9},{9,8},{10,11... | collective-permute-start | bytes 147464 | tf_op jit(solution)/shard_map/ppermute | solution.py:248
  (8 other events, 104.6 us)

commit v2 on v1

v2 whole, which is shorter than its diff:
```python
import functools
import math

import jax
import jax.numpy as jnp
from jax import lax
from jax.experimental import pallas as pl
from jax.experimental.pallas import tpu as pltpu
from jax.sharding import Mesh, PartitionSpec as P

F32 = jnp.float32
BF16 = jnp.bfloat16
LOG2E = 1.4426950408889634
LN2 = 0.6931471805599453
R = 128
E = 768
D = 1536
H = E // 2

NT = (((1,), (1,)), ((), ()))
NN = (((1,), (0,)), ((), ()))
TN = (((0,), (0,)), ((), ()))


def dot(a, b, dims):
    return lax.dot_general(a, b, dims, preferred_element_type=F32)


GRANT = 6 << 20
VM = pl.BlockSpec(memory_space=pltpu.VMEM)
SM = pl.BlockSpec(memory_space=pltpu.SMEM)
HB = pl.BlockSpec(memory_space=pltpu.HBM)
VP = pl.BlockSpec(memory_space=pltpu.VMEM, index_map=None)


def vmem_call(kernel, out_shape, scratch=(), smem=0, n_in=0, flops=0, nbytes=0, specs=None, out_specs=None):
    if specs is None:
        specs = [SM] * smem + [VM] * (n_in - smem)
    if out_specs is None:
        out_specs = jax.tree.map(lambda _: VM, out_shape)

    def place_out(t, spec):
        if spec is HB:
            return pltpu.HBM(t.shape, t.dtype)
        if spec is VP:
            return pltpu.VMEM(t.shape, t.dtype)
        return t

    def place_in(t, spec):
        if spec is HB:
            return pltpu.with_memory_space_constraint(t, pltpu.HBM)
        if spec is VP:
            return pltpu.with_memory_space_constraint(t, pltpu.VMEM)
        return t

    def call(*args):
        held = sum(t.size * jnp.dtype(t.dtype).itemsize for t in (*args, *jax.tree.leaves(out_shape)))
        held += sum(4 * math.prod(t.shape) for t in scratch)
        return pl.pallas_call(
            kernel,
            out_shape=jax.tree.map(place_out, out_shape, out_specs),
            in_specs=specs,
            out_specs=out_specs,
            scratch_shapes=list(scratch),
            compiler_params=pltpu.CompilerParams(vmem_limit_bytes=2 * held + GRANT),
            cost_estimate=pl.CostEstimate(flops=flops, bytes_accessed=nbytes, transcendentals=0),
        )(*(place_in(t, spec) for t, spec in zip(args, specs)))

    return call


PARTS = 3


def proj_kernel(copies, x_hbm, head_hbm, *refs):
    b_ref, unit_hbm, norm_hbm, x_v, head_v, unit_v, norm_v, low_v, in_sem, out_sem = refs[-10:]
    deep = D // PARTS
    get_x = pltpu.make_async_copy(x_hbm, x_v, in_sem.at[PARTS])
    get = [
        pltpu.make_async_copy(head_hbm.at[pl.ds(k * deep, deep)], head_v.at[pl.ds(k * deep, deep)], in_sem.at[k])
        for k in range(PARTS)
    ]
    get_x.start()
    for c in get:
        c.start()
    get_x.wait()
    proj = None
    for k, c in enumerate(get):
        c.wait()
        part = dot(x_v[:, k * deep : (k + 1) * deep], head_v[k * deep : (k + 1) * deep], NN)
        proj = part if proj is None else proj + part
    norm = jnp.sqrt(jnp.sum(proj * proj, axis=1, keepdims=True) + 1e-06)
    unit = proj / norm
    unit_v[...] = unit
    norm_v[...] = jnp.broadcast_to(norm, (R, 128))
    put = [
        pltpu.make_async_copy(unit_v, unit_hbm, out_sem.at[0]),
        pltpu.make_async_copy(norm_v, norm_hbm, out_sem.at[1]),
    ]
    for c in put:
        c.start()
    low = unit.astype(BF16)
    if copies == 1:
        b_ref[...] = low
    else:
        low_v[...] = low
        for k in range(copies):
            put.append(pltpu.make_async_copy(low_v, b_ref.at[pl.ds(k * R, R)], out_sem.at[2 + k]))
            put[-1].start()
    for c in put:
        c.wait()


def project(copies, x, head, after=()):
    return vmem_call(
        functools.partial(proj_kernel, copies),
        (
            jax.ShapeDtypeStruct((copies * R, E), BF16),
            jax.ShapeDtypeStruct((R, E), F32),
            jax.ShapeDtypeStruct((R, 128), F32),
        ),
        scratch=(
            pltpu.VMEM((R, D), BF16),
            pltpu.VMEM((D, E), BF16),
            pltpu.VMEM((R, E), F32),
            pltpu.VMEM((R, 128), F32),
            pltpu.VMEM((R, E), BF16),
            pltpu.SemaphoreType.DMA((PARTS + 1,)),
            pltpu.SemaphoreType.DMA((2 + copies,)),
        ),
        specs=[HB] * (2 + len(after)), out_specs=(HB if copies > 1 else VM, HB, HB),
        flops=2 * R * D * E, nbytes=2 * (R * D + D * E),
    )(x, head, *after)


SUB = 8
CB = 256
RB = 32


def pair_elementwise(s_ref, g_ref, rows, scale2, bias2, diag_at):
    acc_m = jnp.zeros((SUB, CB), F32)
    acc_l = jnp.zeros((SUB, CB), F32)
    acc_s = jnp.zeros((SUB, CB), F32)
    acc_g = jnp.zeros((SUB, CB), F32)

    def fold(t):
        return jnp.sum(t.reshape(RB // SUB, SUB, CB), axis=0)

    for c in range(s_ref.shape[1] // CB):
        prod = jnp.ones((SUB, CB), F32)
        for r in range(rows // RB):
            s = s_ref[r * RB : (r + 1) * RB, c * CB : (c + 1) * CB]
            z = s * scale2 + bias2
            if diag_at is not None:
                row = r * RB + lax.broadcasted_iota(jnp.int32, (RB, CB), 0)
                col = c * CB + lax.broadcasted_iota(jnp.int32, (RB, CB), 1)
                mask = row + diag_at == col
                z = jnp.where(mask, -z, z)
            t = jnp.exp2(-jnp.abs(z))
            one_t = 1.0 + t
            inv = 1.0 / one_t
            g = jnp.where(z >= 0.0, inv, t * inv)
            if diag_at is not None:
                g = jnp.where(mask, -g, g)
            g_ref[r * RB : (r + 1) * RB, c * CB : (c + 1) * CB] = g.astype(BF16)
            acc_m = acc_m + fold(jnp.maximum(z, 0.0))
            acc_s = acc_s + fold(g * s)
            acc_g = acc_g + fold(g)
            for k in range(RB // SUB):
                prod = prod * one_t[k * SUB : (k + 1) * SUB]
        acc_l = acc_l + jnp.log(prod)
    return LN2 * acc_m + acc_l, acc_s, acc_g


def pair_kernel(chunks, own, scal_ref, at_ref, v_ref, *refs):
    n = sum(len(c) for c in chunks)
    if not own:
        before_ref, refs = refs[0], refs[1:]
    u_refs, du_refs, (g_ref, sums_ref, u_all, s_all) = refs[:n], refs[n : 2 * n], refs[2 * n :]
    scale2 = scal_ref[0, 0]
    bias2 = scal_ref[0, 1]
    v = v_ref[...]
    tot = None
    at = 0
    for i, chunk in enumerate(chunks):
        rows = 0
        for k in chunk:
            u_all[i % 2, rows : rows + u_refs[k].shape[0]] = u_refs[k][...]
            rows += u_refs[k].shape[0]
        s_all[i % 2, :rows] = dot(u_all[i % 2, :rows], v, NT)
        part = pair_elementwise(
            s_all.at[i % 2], g_ref.at[pl.ds(at, rows)], rows, scale2, bias2,
            at_ref[0, 0] if own and i == 0 else None,
        )
        tot = part if tot is None else tuple(a + b for a, b in zip(tot, part))
        du = dot(g_ref[at : at + rows], v, NN)
        at += rows
        rows = 0
        for k in chunk:
            ref = du_refs[k]
            ref[...] = du[rows : rows + ref.shape[0]].astype(ref.dtype)
            rows += ref.shape[0]
    for i in range(3):
        sums_ref[i] = tot[i] if own else tot[i] + before_ref[i]


def pair(chunks, own, scal, at, v, us, dtype, before=()):
    rows = sum(u.shape[0] for u in us)
    most = max(sum(us[k].shape[0] for k in c) for c in chunks)
    cols = v.shape[0]
    out = (
        *(jax.ShapeDtypeStruct(u.shape, dtype) for u in us),
        jax.ShapeDtypeStruct((rows, cols), BF16),
        jax.ShapeDtypeStruct((3, SUB, CB), F32),
    )
    return vmem_call(
        functools.partial(pair_kernel, chunks, own), out,
        scratch=(pltpu.VMEM((2, most, E), BF16), pltpu.VMEM((2, most, cols), F32)),
        specs=[SM, SM] + [VM] * (1 + len(before) + len(us)), out_specs=(VP,) * (len(us) + 2),
        flops=4 * rows * cols * E, nbytes=4 * (rows + cols) * E,
    )(scal, at, v, *before, *us)


def cols_kernel(*refs):
    n = len(refs) - 6
    g1_ref, g2_ref, u_refs, (dv_hbm, u_all, dv_ref, sem) = refs[0], refs[1], refs[2 : 2 + n], refs[-4:]
    at = 0
    for ref in u_refs:
        u_all[at : at + ref.shape[0]] = ref[...]
        at += ref.shape[0]
    k = g1_ref.shape[0]
    cols = dv_ref.shape[0] // 2
    put = []
    for i in range(2):
        at = pl.ds(i * cols, cols)
        dv = dot(g1_ref[:, at], u_all[:k], TN) + dot(g2_ref[:, at], u_all[k:], TN)
        dv_ref[at] = dv.astype(BF16)
        put.append(pltpu.make_async_copy(dv_ref.at[at], dv_hbm.at[at], sem.at[i]))
        put[i].start()
    for c in put:
        c.wait()


def pair_cols(g1, g2, us):
    rows = g1.shape[0] + g2.shape[0]
    cols = g1.shape[1]
    return vmem_call(
        cols_kernel, jax.ShapeDtypeStruct((cols, E), BF16),
        scratch=(pltpu.VMEM((rows, E), BF16), pltpu.VMEM((cols, E), BF16), pltpu.SemaphoreType.DMA((2,))),
        specs=[VP, VP] + [VM] * len(us), out_specs=HB,
        flops=2 * rows * cols * E, nbytes=2 * (rows * cols + rows * E + cols * E),
    )(g1, g2, *us)


def step_kernel(pa_ref, pb_ref, ra_ref, rb_ref, a_ref, b_ref):
    half = ra_ref.shape[0]
    if half == R:
        a_ref[...] = (pa_ref[...] + rb_ref[...].astype(F32)).astype(BF16)
        b_ref[...] = (pb_ref[...] + ra_ref[...].astype(F32)).astype(BF16)
    else:
        a_ref[:half] = pa_ref[:half].astype(BF16)
        a_ref[half:] = (pa_ref[half:] + rb_ref[...].astype(F32)).astype(BF16)
        b_ref[:half] = (pb_ref[:half] + ra_ref[...].astype(F32)).astype(BF16)
        b_ref[half:] = pb_ref[half:].astype(BF16)


STEP_FLOPS = 8 * 10**9


def ring_step(pa, pb, ra, rb):
    low = jax.ShapeDtypeStruct((R, E), BF16)
    return vmem_call(step_kernel, (low, low), specs=[VP, VP, VM, VM], flops=STEP_FLOPS, nbytes=16 * R * E)(pa, pb, ra, rb)


def back_kernel(
    scal_ref, ui_hbm, ni_hbm, ut_hbm, nt_hbm, du_ref, qa_ref, qb_ref, dv_ref,
    di_ref, dt_ref, keep_ref, send_ref, ui_ref, ni_ref, ut_ref, nt_ref, sem,
):
    get = [
        pltpu.make_async_copy(src, dst, sem.at[k])
        for k, (src, dst) in enumerate(
            ((ui_hbm, ui_ref), (ni_hbm, ni_ref), (ut_hbm, ut_ref), (nt_hbm, nt_ref))
        )
    ]
    for c in get:
        c.start()
    scale = scal_ref[0, 0]
    low = scal_ref[0, 1] == 0.0
    du = scale * (du_ref[...] + qa_ref[...].astype(F32) + qb_ref[...].astype(F32))
    dv = dv_ref[:R].astype(F32)
    for j in range(1, 8):
        dv = dv + dv_ref[j * R : (j + 1) * R].astype(F32)
    dv = scale * dv
    for c in get:
        c.wait()
    for k, (unit_ref, norm_ref, grad, out_ref) in enumerate(
        ((ui_ref, ni_ref, du, di_ref), (ut_ref, nt_ref, dv, dt_ref))
    ):
        unit = unit_ref[...]
        d = (grad - unit * jnp.sum(unit * grad, axis=1, keepdims=True)) / norm_ref[:, :1]
        out_ref[...] = d.astype(BF16)
        left, right = d[:, :H], d[:, H:]
        keep_ref[k * R : (k + 1) * R] = jnp.where(low, left, right).astype(BF16)
        send_ref[k * R : (k + 1) * R] = jnp.where(low, right, left).astype(BF16)


def back(scal, *args):
    low = jax.ShapeDtypeStruct((R, E), BF16)
    half = jax.ShapeDtypeStruct((2 * R, H), BF16)
    return vmem_call(
        back_kernel, (low, low, half, half), specs=[SM] + [HB] * 4 + [VP] + [VM] * 3,
        scratch=(
            pltpu.VMEM((R, E), F32),
            pltpu.VMEM((R, 128), F32),
            pltpu.VMEM((R, E), F32),
            pltpu.VMEM((R, 128), F32),
            pltpu.SemaphoreType.DMA((4,)),
        ),
        flops=20 * R * E, nbytes=30 * R * E,
    )(scal, *args)


def input_grad_kernel(di_ref, dt_ref, head_ref, gi_ref, gt_ref, done_ref):
    head = head_ref[...]
    done_ref[...] = jnp.zeros((8, 128), F32)
    gi_ref[...] = dot(di_ref[...], head, NT).astype(BF16)
    gt_ref[...] = dot(dt_ref[...], head, NT).astype(BF16)


def input_grad(di, dt, head):
    out = jax.ShapeDtypeStruct((R, D), BF16)
    return vmem_call(
        input_grad_kernel, (out, out, jax.ShapeDtypeStruct((8, 128), F32)), n_in=3, flops=4 * R * D * E, nbytes=2 * (4 * R * D + D * E)
    )(di, dt, head)


ZROWS = 24
PAD = 16


def head_grad_kernel(x_hbm, y_hbm, ox_hbm, oy_hbm, keep_ref, got_ref, extra_ref, out_hbm, x_all, d_all, out_v, in_sem, out_sem):
    get = []
    for i, src in enumerate((x_hbm, y_hbm, ox_hbm, oy_hbm)):
        get.append(pltpu.make_async_copy(src, x_all.at[pl.ds(i * R, R)], in_sem.at[i]))
        get[i].start()
    d_all[: 2 * R] = keep_ref[...]
    d_all[2 * R :] = got_ref[...]
    for j in range(8):
        out_v[j, 8 * ZROWS :] = extra_ref[...]
    d = d_all[...]
    for c in get:
        c.wait()
    put = []
    for xl in range(2):
        full = dot(x_all[:, xl * E : (xl + 1) * E], d, TN)
        for y in range(4):
            for z in range(0, 8, 2):
                a = (z * 4 + y) * ZROWS
                b = ((z + 1) * 4 + y) * ZROWS
                both = jnp.concatenate([full[a : a + ZROWS], full[b : b + ZROWS]], axis=0)
                out_v[xl * 4 + y, z * ZROWS : (z + 2) * ZROWS] = both.astype(BF16)
        at = pl.ds(xl * 4, 4)
        put.append(pltpu.make_async_copy(out_v.at[at], out_hbm.at[at], out_sem.at[xl]))
        put[xl].start()
    for c in put:
        c.wait()


def head_grad_parts(x, y, ox, oy, keep, got, extra):
    shape = (8, 8 * ZROWS + PAD, H)
    return vmem_call(
        head_grad_kernel, jax.ShapeDtypeStruct(shape, BF16),
        scratch=(
            pltpu.VMEM((4 * R, D), BF16),
            pltpu.VMEM((4 * R, H), BF16),
            pltpu.VMEM(shape, BF16),
            pltpu.SemaphoreType.DMA((4,)),
            pltpu.SemaphoreType.DMA((2,)),
        ),
        specs=[HB] * 4 + [VM] * 3, out_specs=HB, flops=8 * R * D * H, nbytes=2 * (4 * R * D + D * H),
    )(x, y, ox, oy, keep, got, extra)


def sum_kernel(parts_ref, _, out_ref):
    s = parts_ref[0].astype(F32)
    for j in range(1, 8):
        s = s + parts_ref[j].astype(F32)
    t = jnp.sum(s[8 * ZROWS : 8 * ZROWS + 3], axis=0, keepdims=True)
    hi = t.astype(BF16).astype(F32)
    mid = (t - hi).astype(BF16).astype(F32)
    low = t - hi - mid
    row = lax.broadcasted_iota(jnp.int32, (8, H), 0)
    tail = jnp.where(row == 0, hi, jnp.where(row == 1, mid, jnp.where(row == 2, low, 0.0)))
    for z in range(8):
        out_ref[z] = jnp.concatenate([s[z * ZROWS : (z + 1) * ZROWS], tail], axis=0).astype(BF16)


def sum_parts(parts, after):
    return vmem_call(
        sum_kernel, jax.ShapeDtypeStruct((8, ZROWS + 8, H), BF16), n_in=2,
        flops=10 * parts.size, nbytes=2 * parts.size,
    )(parts, after)


def last_kernel(scal_ref, s_ref, r_ref, o_ref, hg_ref, l_ref, a_ref, b_ref):
    low = scal_ref[0, 1] == 0.0
    mine = s_ref[...] + r_ref[...]
    other = o_ref[...]
    left = jnp.where(low, mine, other)
    right = jnp.where(low, other, mine)
    hg_ref[:, :H] = left[:ZROWS]
    hg_ref[:, H:] = right[:ZROWS]
    t = jnp.sum((mine + other)[ZROWS : ZROWS + 3], axis=0, keepdims=True) * (1.0 / COUNT)
    l_ref[...] = t[:, 0:1]
    a_ref[...] = scal_ref[0, 0] * t[:, 1:2]
    b_ref[...] = t[:, 2:3]


COUNT = float(4 * 8192) * 8192.0


def last(scal, s, r, o):
    one = jax.ShapeDtypeStruct((1, 1), F32)
    return vmem_call(
        last_kernel, (jax.ShapeDtypeStruct((ZROWS, E), F32), one, one, one), smem=1, n_in=4,
        flops=ZROWS * E, nbytes=16 * ZROWS * E,
    )(scal, s, r, o)


def swap(axis):
    return lambda v: lax.ppermute(v, axis, [(0, 1), (1, 0)])


def ring(axis, n):
    even = [(i, i ^ 1) for i in range(n)]
    odd = [(i, (i + 1) % n if i % 2 else (i - 1) % n) for i in range(n)]
    return (lambda v: lax.ppermute(v, axis, even)), (lambda v: lax.ppermute(v, axis, odd))


def split3(t):
    hi = lax.reduce_precision(t, 8, 7)
    mid = lax.reduce_precision(t - hi, 8, 7)
    return hi, mid, t - hi - mid


def scalar_rows(t, rows):
    parts = jnp.stack(split3(t))
    return jnp.concatenate([parts, jnp.zeros((rows - 3, H), F32)]).astype(BF16)


def per_device(image, text, log_scale, bias, head):
    x = image[0]
    y = text[0]
    scale = jnp.exp(log_scale)
    core = lax.axis_index("c")
    z1, z2 = ring("z", 8)
    cc = swap("c")
    near = ("xl", "y")

    u, ui, ni = project(1, x, head)
    a1, b1 = z1(u), z2(u)
    v, ut, nt = project(8, y, head, (ni,))

    vs = lax.all_to_all(v, near, 0, 0, tiled=True)
    a2, b2 = z1(b1), z2(a1)
    a3, b3 = z1(b2), z2(a2)
    fa, fb = z1(b3[: R // 2]), z2(a3[R // 2 :])
    ox, oy = cc(x), cc(y)

    scal = jnp.stack([scale * LOG2E, bias * LOG2E]).reshape(1, 2)
    at = (lax.axis_index(near) * R).reshape(1, 1)
    us = (u, a1, b1, a2, b2, a3, b3)
    *p, g1, sums = pair(((0,), (1, 2), (3, 4), (5, 6)), True, scal, at, vs, us, F32)
    qa, qb, g2, sums = pair(((0, 1),), False, scal, at, vs, (fa, fb), BF16, (sums,))

    qa, qb = z1(qa), z2(qb)
    dv = lax.all_to_all(pair_cols(g1, g2, (*us, fa, fb)), near, 0, 0, tiled=True)
    for k in (5, 3, 1):
        qa, qb = ring_step(p[k], p[k + 1], qa, qb)
        qa, qb = z1(qa), z2(qb)

    sums = jnp.sum(sums, axis=(1, 2))
    extra = scalar_rows(jnp.zeros((H,), F32).at[:3].set(sums), PAD)

    scal2 = jnp.stack([scale, core.astype(F32)]).reshape(1, 2)
    di, dt, keep, send = back(scal2, ui, ni, ut, nt, p[0], qa, qb, dv)
    got = cc(send)
    gi, gt, done = input_grad(di, dt, head)

    parts = head_grad_parts(x, y, ox, oy, keep, got, extra)
    parts = lax.all_to_all(parts, ("xl", "y"), 0, 0, tiled=True)
    parts = lax.all_to_all(sum_parts(parts, done), "z", 0, 0, tiled=True)
    s = jnp.sum(parts.astype(F32), axis=0)
    r = swap("xh")(s)
    o = cc(s + r)
    hg, l, a, b = last(scal2, s, r, o)
    return l.reshape(()), a.reshape(()), b.reshape(()), gi[None], gt[None], hg


def solution(mesh):
    fine = Mesh(mesh.devices.reshape(2, 8, 4, 2, 2), ("xl", "z", "y", "xh", "c"))
    blk = ("xl", "z", "y")
    rep = ("xh", "c")
    data = P(rep, blk, None)
    return jax.shard_map(
        per_device,
        mesh=fine,
        in_specs=(data, data, P(), P(), P()),
        out_specs=(P(), P(), P(), data, data, P(blk, None)),
        check_vma=False,
    )
```

time: 159 us -> 144 us (0.906)
  Pallas kernels: 20.1 us -> 29 us
  other arithmetic: 7.46 us -> 0.38 us
  starting transfers between devices: 48.8 us -> 43.2 us
  between operations: 7.62 us -> 2.23 us
  waiting for transfers between devices: 51.9 us -> 47.9 us
  local copies, waits for them, and re-layouts: 5.4 us -> 3.71 us
    all_to_all x0 -> x2, starting transfers between devices: none -> 11.8 us  [the longest x1 6.71 us: per_device(): lax.all_to_all(pair_cols(g1, g2, (*us, fa, fb)), near, 0, 0, tiled=True)]
    ppermute x12 -> x8, starting transfers between devices: 33.6 us -> 22 us  [ring(): lax.ppermute(v, axis, odd)]
    pallas_call x6 -> x13, Pallas kernels: 20.1 us -> 29 us  [call(): pl.pallas_call(kernel, out_shape=jax.tree.map(place_out, out_shape, out_s...]
    ppermute x12 -> x8, starting transfers between devices: 6.81 us -> 1.99 us  [ring(): lax.ppermute(v, axis, even)]
    convert_element_type x6 -> x0, other arithmetic: 3.29 us -> none  [the longest x2 1.17 us: per_device(): qa, qb = (z1((p[3] + qb).astype(BF16)), z2((p[4] + qa).astype(BF16)))]
    ppermute x12 -> x8, waiting for transfers between devices: 15.7 us -> 13 us  [ring(): lax.ppermute(v, axis, even)]
    all_to_all x1, waiting for transfers between devices: 17.6 us -> 15.3 us  [per_device(): parts = lax.all_to_all(parts, ('xl', 'y'), 0, 0, tiled=True)]
    ppermute x7 -> x5, starting transfers between devices: 3.79 us -> 1.6 us  [swap(): return lambda v: lax.ppermute(v, axis, [(0, 1), (1, 0)])]
  transfers between devices with their start and end apart: 32 -> 24, of which waited for: 15 -> 16; matrix products, arithmetic and copies ran while one was open for 4% -> 1% of each run, Pallas kernels for 2% -> 10%
where the time goes in v2:
time: 144 us; the launch traced here: 142 us
  waiting for transfers between devices  47.9 us (33%)
  starting transfers between devices  43.2 us (30%)
  Pallas kernels  29 us (20%)
  blocking collectives  15.3 us (11%)
  local copies, waits for them, and re-layouts  3.71 us (3%)
  between operations  2.23 us (2%)
    pallas_call x13, Pallas kernels, call(): pl.pallas_call(kernel, out_shape=jax.tree.map(place_out, out_shape, out_s...  29 us
    ppermute x8, starting transfers between devices, ring(): lax.ppermute(v, axis, odd)  22 us
    all_to_all x1, waiting for transfers between devices, per_device(): parts = lax.all_to_all(parts, ('xl', 'y'), 0, 0, tiled=True)  15.3 us
    all_to_all x1, blocking collectives, per_device(): parts = lax.all_to_all(sum_parts(parts, done), 'z', 0, 0, tiled=True)  15.3 us
    ppermute x8, waiting for transfers between devices, ring(): lax.ppermute(v, axis, even)  13 us
    ppermute x8, waiting for transfers between devices, ring(): lax.ppermute(v, axis, odd)  12.2 us
    ppermute x5, waiting for transfers between devices, swap(): return lambda v: lax.ppermute(v, axis, [(0, 1), (1, 0)])  7.34 us
    all_to_all x1, starting transfers between devices, per_device(): lax.all_to_all(pair_cols(g1, g2, (*us, fa, fb)), near, 0, 0, tiled=True)  6.71 us
  transfers between devices with their start and end apart: 24, of which 16 were waited for; matrix products, arithmetic and copies ran while one was open for 1% of the time, Pallas kernels for 10%

profile of v2, /device:TPU:4, one launch (start us, length us, event | category | flops | bytes accessed | tf_op | source)
XLA Modules:
  0.0 141.7 jit_solution(18350838012191649738)
XLA Ops:
  0.6 3.0 %shard_map.100 = (bf16[128,768]{1,0:T(8,128)(2,1)S(1)}, f32[128,768]{1,0:T(8,128)}, f32[128,128]{1,0:T(8,128)}) custom-call(bf16[128,1536]{1,0:T(8,128)(2,1)} %bitcast.3.x_hbm, bf16[1536,768]{1,0:T(8,128)(2,1)} %head_ref.1), custom_call_target="tpu_custom_call" | custom-call | flops 301989888 | bytes 2752512 | tf_op jit(solution)/shard_map/pallas_call | solution.py:59
  3.7 3.7 %shard_map.101 = (bf16[1024,768]{1,0:T(8,128)(2,1)}, f32[128,768]{1,0:T(8,128)}, f32[128,128]{1,0:T(8,128)}) custom-call(bf16[128,1536]{1,0:T(8,128)(2,1)} %bitcast.4.x_hbm.y_hbm, bf16[1536,768]{1,0:T(8,128)(2,1)} %head_ref.1, f32[128,128]{1,0:T(8,128)} %get-tuple-element.55.refs_0_.ni_hbm), custom_call_target="tpu_custom_call" | custom-call | flops 301989888 | bytes 2752512 | tf_op jit(solution)/shard_map/pallas_call | solution.py:59
  7.3 5.1 %all-to-all-start = ((bf16[8,128,768]{2,1,0:T(8,128)(2,1)}), bf16[8,128,768]{2,1,0:T(8,128)(2,1)S(1)}, u32[]{:S(2)}, u32[]{:S(2)}) async-start(bf16[8,128,768]{2,1,0:T(8,128)(2,1)} %bitcast.24), calls=%async_computation | async-start | bytes 3145728 | tf_op jit(solution)/shard_map/all_to_all | solution.py:465
  12.5 5.9 %collective-permute-start.3 = (bf16[128,768]{1,0:T(8,128)(2,1)S(1)}, bf16[128,768]{1,0:T(8,128)(2,1)S(1)}, u32[]{:S(2)}, u32[]{:S(2)}) collective-permute-start(bf16[128,768]{1,0:T(8,128)(2,1)S(1)} %get-tuple-element.59.refs_0_.refs_2_), channel_id=1, source_target_pairs={{0,112},{16,32},{32,16},{48,64},{64,48},{80,96},{96,80},{112,0},{1... | collective-permute-start | bytes 589832 | tf_op jit(solution)/shard_map/ppermute | solution.py:438
  18.3 4.6 %collective-permute-done.3.refs_2_.refs_4_ = bf16[128,768]{1,0:T(8,128)(2,1)S(1)} collective-permute-done((bf16[128,768]{1,0:T(8,128)(2,1)S(1)}, bf16[128,768]{1,0:T(8,128)(2,1)S(1)}, u32[]{:S(2)}, u32[]{:S(2)}) %collective-permute-start.3) | collective-permute-done | bytes 196640 | tf_op jit(solution)/shard_map/ppermute | solution.py:438
  22.9 1.5 %collective-permute-done.2.refs_1_.refs_3_ = bf16[128,768]{1,0:T(8,128)(2,1)S(1)} collective-permute-done((bf16[128,768]{1,0:T(8,128)(2,1)S(1)}, bf16[128,768]{1,0:T(8,128)(2,1)S(1)}, u32[]{:S(2)}, u32[]{:S(2)}) %collective-permute-start.2) | collective-permute-done | bytes 196640 | tf_op jit(solution)/shard_map/ppermute | solution.py:438
  24.4 1.5 %collective-permute-start.5 = (bf16[128,768]{1,0:T(8,128)(2,1)S(1)}, bf16[128,768]{1,0:T(8,128)(2,1)S(1)}, u32[]{:S(2)}, u32[]{:S(2)}) collective-permute-start(bf16[128,768]{1,0:T(8,128)(2,1)S(1)} %collective-permute-done.2.refs_1_.refs_3_), channel_id=1, source_target_pairs={{0,112},{16,32},{32,16},{48,64},{64,48},{80,96},{96,80},{112,0},{1... | collective-permute-start | bytes 589832 | tf_op jit(solution)/shard_map/ppermute | solution.py:438
  25.9 2.8 %collective-permute-done.4.refs_3_.refs_5_ = bf16[128,768]{1,0:T(8,128)(2,1)S(1)} collective-permute-done((bf16[128,768]{1,0:T(8,128)(2,1)S(1)}, bf16[128,768]{1,0:T(8,128)(2,1)S(1)}, u32[]{:S(2)}, u32[]{:S(2)}) %collective-permute-start.4) | collective-permute-done | bytes 196640 | tf_op jit(solution)/shard_map/ppermute | solution.py:438
  28.7 2.9 %collective-permute-start.7 = (bf16[128,768]{1,0:T(8,128)(2,1)S(1)}, bf16[128,768]{1,0:T(8,128)(2,1)S(1)}, u32[]{:S(2)}, u32[]{:S(2)}) collective-permute-start(bf16[128,768]{1,0:T(8,128)(2,1)S(1)} %collective-permute-done.4.refs_3_.refs_5_), channel_id=1, source_target_pairs={{0,112},{16,32},{32,16},{48,64},{64,48},{80,96},{96,80},{112,0},{1... | collective-permute-start | bytes 589832 | tf_op jit(solution)/shard_map/ppermute | solution.py:438
  33.4 2.2 %collective-permute-done.7.refs_6_.refs_8_ = bf16[128,768]{1,0:T(8,128)(2,1)S(1)} collective-permute-done((bf16[128,768]{1,0:T(8,128)(2,1)S(1)}, bf16[128,768]{1,0:T(8,128)(2,1)S(1)}, u32[]{:S(2)}, u32[]{:S(2)}) %collective-permute-start.7) | collective-permute-done | bytes 196640 | tf_op jit(solution)/shard_map/ppermute | solution.py:438
  35.7 3.0 %collective-permute-done.6.refs_5_.refs_7_ = bf16[128,768]{1,0:T(8,128)(2,1)S(1)} collective-permute-done((bf16[128,768]{1,0:T(8,128)(2,1)S(1)}, bf16[128,768]{1,0:T(8,128)(2,1)S(1)}, u32[]{:S(2)}, u32[]{:S(2)}) %collective-permute-start.6) | collective-permute-done | bytes 196640 | tf_op jit(solution)/shard_map/ppermute | solution.py:438
  40.8 4.8 %shard_map.102 = (f32[128,768]{1,0:T(8,128)S(1)}, f32[128,768]{1,0:T(8,128)S(1)}, f32[128,768]{1,0:T(8,128)S(1)}, f32[128,768]{1,0:T(8,128)S(1)}, f32[128,768]{1...) custom-call(f32[1,2]{1,0:T(1,128)S(1)} %maximum_bitcast_fusion.1.sca, ...), custom_call_target="tpu_custom_call" | custom-call | flops 2818572288 | bytes 5898240 | tf_op jit(solution)/shard_map/pallas_call | solution.py:59
  45.7 1.6 %shard_map.103 = (bf16[64,768]{1,0:T(8,128)(2,1)S(1)}, bf16[64,768]{1,0:T(8,128)(2,1)S(1)}, bf16[128,1024]{1,0:T(8,128)(2,1)S(1)}, f32[3,8,256]{2,1,0:T(8,128)S(1)}) custom-call(f32[1,2]{1,0:T(1,128)S(1)} %maximum_bitcast_fusion.1.scal_ref, s32[1,1]{1,0:T(1,128)} %bitcast.8.at_ref, bf16[1024,768]{1,0:T(8,128)(2,1)S(1)} %bitcast.21, ...), custom_call_target="tpu_custom_call" | custom-call | flops 402653184 | bytes 3538944 | tf_op jit(solution)/shard_map/pallas_call | solution.py:59
  48.0 2.9 %collective-permute-start.11 = (bf16[64,768]{1,0:T(8,128)(2,1)S(1)}, bf16[64,768]{1,0:T(8,128)(2,1)S(1)}, u32[]{:S(2)}, u32[]{:S(2)}) collective-permute-start(bf16[64,768]{1,0:T(8,128)(2,1)S(1)} %get-tuple-element.69), channel_id=1, source_target_pairs={{0,112},{16,32},{32,16},{48,64},{64,48},{80,96},{96,80},{112,0},{1... | collective-permute-start | bytes 294920 | tf_op jit(solution)/shard_map/ppermute | solution.py:438
  52.0 1.8 %collective-permute-done.11.rb_ref = bf16[64,768]{1,0:T(8,128)(2,1)S(1)} collective-permute-done((bf16[64,768]{1,0:T(8,128)(2,1)S(1)}, bf16[64,768]{1,0:T(8,128)(2,1)S(1)}, u32[]{:S(2)}, u32[]{:S(2)}) %collective-permute-start.11) | collective-permute-done | bytes 98336 | tf_op jit(solution)/shard_map/ppermute | solution.py:438
  55.0 3.1 %collective-permute-start.13 = (bf16[128,768]{1,0:T(8,128)(2,1)}, bf16[128,768]{1,0:T(8,128)(2,1)}, u32[]{:S(2)}, u32[]{:S(2)}) collective-permute-start(bf16[128,768]{1,0:T(8,128)(2,1)} %get-tuple-element.71), channel_id=1, source_target_pairs={{0,112},{16,32},{32,16},{48,64},{64,48},{80,96},{96,80},{112,0},{1... | collective-permute-start | bytes 589832 | tf_op jit(solution)/shard_map/ppermute | solution.py:438
  58.1 3.5 %shard_map.107 = bf16[1024,768]{1,0:T(8,128)(2,1)} custom-call(bf16[896,1024]{1,0:T(8,128)(2,1)S(1)} %get-tuple-element.76.refs_0_, bf16[128,1024]{1,0:T(8,128)(2,1)S(1)} %get-tuple-element.77.refs_1_, bf16[128,768]{1,0:T(8,128)(2,1)S(1)} %get-tuple-element.59.refs_0_.refs_2_, bf16[128,768]{1,0:T(8,128)(2,1)S(1)} %collective-permute-done.2.refs_1_.refs_3_, ...), custom_call_target="tpu_custom_call" | custom-call | flops 1610612736 | bytes 5242880 | tf_op jit(solution)/shard_map/pallas_call | solution.py:59
  61.6 6.7 %all-to-all-start.1 = ((bf16[8,128,768]{2,1,0:T(8,128)(2,1)}), bf16[8,128,768]{2,1,0:T(8,128)(2,1)S(1)}, u32[]{:S(2)}, u32[]{:S(2)}) async-start(bf16[8,128,768]{2,1,0:T(8,128)(2,1)} %bitcast.23), calls=%async_computation.1 | async-start | bytes 3145728 | tf_op jit(solution)/shard_map/all_to_all | solution.py:478
  70.6 2.7 %collective-permute-start.15 = (bf16[128,768]{1,0:T(8,128)(2,1)S(1)}, bf16[128,768]{1,0:T(8,128)(2,1)S(1)}, u32[]{:S(2)}, u32[]{:S(2)}) collective-permute-start(bf16[128,768]{1,0:T(8,128)(2,1)S(1)} %get-tuple-element.73), channel_id=1, source_target_pairs={{0,112},{16,32},{32,16},{48,64},{64,48},{80,96},{96,80},{112,0},{1... | collective-permute-start | bytes 589832 | tf_op jit(solution)/shard_map/ppermute | solution.py:438
  73.8 2.4 %collective-permute-done.14.ra_ref = bf16[128,768]{1,0:T(8,128)(2,1)S(1)} collective-permute-done((bf16[128,768]{1,0:T(8,128)(2,1)S(1)}, bf16[128,768]{1,0:T(8,128)(2,1)S(1)}, u32[]{:S(2)}, u32[]{:S(2)}) %collective-permute-start.14) | collective-permute-done | bytes 196640 | tf_op jit(solution)/shard_map/ppermute | solution.py:438
  79.4 2.5 %collective-permute-start.17 = (bf16[128,768]{1,0:T(8,128)(2,1)S(1)}, bf16[128,768]{1,0:T(8,128)(2,1)S(1)}, u32[]{:S(2)}, u32[]{:S(2)}) collective-permute-start(bf16[128,768]{1,0:T(8,128)(2,1)S(1)} %get-tuple-element.75), channel_id=1, source_target_pairs={{0,112},{16,32},{32,16},{48,64},{64,48},{80,96},{96,80},{112,0},{1... | collective-permute-start | bytes 589832 | tf_op jit(solution)/shard_map/ppermute | solution.py:438
  82.2 2.2 %collective-permute-done.16.qa_ref = bf16[128,768]{1,0:T(8,128)(2,1)S(1)} collective-permute-done((bf16[128,768]{1,0:T(8,128)(2,1)S(1)}, bf16[128,768]{1,0:T(8,128)(2,1)S(1)}, u32[]{:S(2)}, u32[]{:S(2)}) %collective-permute-start.16) | collective-permute-done | bytes 196640 | tf_op jit(solution)/shard_map/ppermute | solution.py:438
  84.4 1.9 %collective-permute-done.17.qb_ref = bf16[128,768]{1,0:T(8,128)(2,1)S(1)} collective-permute-done((bf16[128,768]{1,0:T(8,128)(2,1)S(1)}, bf16[128,768]{1,0:T(8,128)(2,1)S(1)}, u32[]{:S(2)}, u32[]{:S(2)}) %collective-permute-start.17) | collective-permute-done | bytes 196640 | tf_op jit(solution)/shard_map/ppermute | solution.py:438
  86.3 2.0 %shard_map.108 = (bf16[128,768]{1,0:T(8,128)(2,1)S(1)}, bf16[128,768]{1,0:T(8,128)(2,1)S(1)}, bf16[256,384]{1,0:T(8,128)(2,1)S(1)}, bf16[256,384]{1,0:T(8,128)(2,1)S(1)}) custom-call(f32[1,2]{1,0:T(1,128)S(1)} %maximum_bitcast_fusion.scal_ref, f32[128,768]{1,0:T(8,128)} %get-tuple-element.54.ui_hbm, f32[128,128]{1,0:T(8,128)} %get-tuple-element.55.refs_0_.ni_hbm, ...), custom_call_target="tpu_custom_call" | custom-call | flops 1966080 | bytes 2949120 | tf_op jit(solution)/shard_map/pallas_call | solution.py:59
  88.5 1.3 collective-permute-done.18.got_ref
  89.9 3.3 %shard_map.109 = bf16[8,208,384]{2,1,0:T(8,128)(2,1)} custom-call(bf16[128,1536]{1,0:T(8,128)(2,1)} %bitcast.3.x_hbm, bf16[128,1536]{1,0:T(8,128)(2,1)} %bitcast.4.x_hbm.y_hbm, bf16[128,1536]{1,0:T(8,128)(2,1)} %collective-permute-done.ox_hbm, bf16[128,1536]{1,0:T(8,128)(2,1)} %collective-permute-done.1.oy_hbm, ...), custom_call_target="tpu_custom_call" | custom-call | flops 603979776 | bytes 2752512 | tf_op jit(solution)/shard_map/pallas_call | solution.py:59
  93.2 5.8 %all-to-all-start.2 = ((bf16[8,208,384]{2,1,0:T(8,128)(2,1)}), bf16[8,208,384]{2,1,0:T(8,128)(2,1)}, u32[]{:S(2)}, u32[]{:S(2)}) async-start(bf16[8,208,384]{2,1,0:T(8,128)(2,1)} %shard_map.109), calls=%async_computation.2 | async-start | bytes 2555904 | tf_op jit(solution)/shard_map/all_to_all | solution.py:492
  99.0 2.4 %shard_map.110 = (bf16[128,1536]{1,0:T(8,128)(2,1)}, bf16[128,1536]{1,0:T(8,128)(2,1)}, f32[8,128]{1,0:T(8,128)S(1)}) custom-call(bf16[128,768]{1,0:T(8,128)(2,1)S(1)} %get-tuple-element.81.di_ref, bf16[128,768]{1,0:T(8,128)(2,1)S(1)} %get-tuple-element.82.dt_ref, bf16[1536,768]{1,0:T(8,128)(2,1)S(1)} %copy-done), custom_call_target="tpu_custom_call" | custom-call | flops 603979776 | bytes 3932160 | tf_op jit(solution)/shard_map/pallas_call | solution.py:59
  101.4 15.3 %all-to-all-done.2.parts_ref = bf16[8,208,384]{2,1,0:T(8,128)(2,1)} async-done(((bf16[8,208,384]{2,1,0:T(8,128)(2,1)}), bf16[8,208,384]{2,1,0:T(8,128)(2,1)}, u32[]{:S(2)}, u32[]{:S(2)}) %all-to-all-start.2) | async-done | bytes 1277984 | tf_op jit(solution)/shard_map/all_to_all | solution.py:492
  116.7 1.5 %shard_map.111 = bf16[8,32,384]{2,1,0:T(8,128)(2,1)S(1)} custom-call(bf16[8,208,384]{2,1,0:T(8,128)(2,1)} %all-to-all-done.2.parts_ref, f32[8,128]{1,0:T(8,128)S(1)} %get-tuple-element.83._), custom_call_target="tpu_custom_call" | custom-call | flops 6389760 | bytes 1277952 | tf_op jit(solution)/shard_map/pallas_call | solution.py:59
  118.2 15.3 %all_to_all.32 = bf16[8,32,384]{2,1,0:T(8,128)(2,1)S(1)} all-to-all(bf16[8,32,384]{2,1,0:T(8,128)(2,1)S(1)} %shard_map.111), channel_id=1, replica_groups=mesh['xl'=2,'z'=8,'y'=4,'xh'=2,'c'=2] {'z'}, dimensions={0} | all-to-all | bytes 393216 | tf_op jit(solution)/shard_map/all_to_all | solution.py:493
  134.4 4.8 %collective-permute-done.19.r_ref = f32[32,384]{1,0:T(8,128)S(1)} collective-permute-done((f32[32,384]{1,0:T(8,128)S(1)}, f32[32,384]{1,0:T(8,128)S(1)}, u32[]{:S(2)}, u32[]{:S(2)}) %collective-permute-start.19) | collective-permute-done | bytes 49184 | tf_op jit(solution)/shard_map/ppermute | solution.py:432
  (68 shorter events, 15.6 us)
Async XLA Ops:
  7.3 32.6 %all-to-all-start = ((bf16[8,128,768]{2,1,0:T(8,128)(2,1)}), bf16[8,128,768]{2,1,0:T(8,128)(2,1)S(1)}, u32[]{:S(2)}, u32[]{:S(2)}) async-start(bf16[8,128,768]{2,1,0:T(8,128)(2,1)} %bitcast.24), calls=%async_computation | async-start | bytes 3145728 | tf_op jit(solution)/shard_map/all_to_all | solution.py:465
  12.5 10.5 %collective-permute-start.3 = (bf16[128,768]{1,0:T(8,128)(2,1)S(1)}, bf16[128,768]{1,0:T(8,128)(2,1)S(1)}, u32[]{:S(2)}, u32[]{:S(2)}) collective-permute-start(bf16[128,768]{1,0:T(8,128)(2,1)S(1)} %get-tuple-element.59.refs_0_.refs_2_), channel_id=1, source_target_pairs={{0,112},{16,32},{32,16},{48,64},{64,48},{80,96},{96,80},{112,0},{1... | collective-permute-start | bytes 589832 | tf_op jit(solution)/shard_map/ppermute | solution.py:438
  18.3 6.1 %collective-permute-start.2 = (bf16[128,768]{1,0:T(8,128)(2,1)S(1)}, bf16[128,768]{1,0:T(8,128)(2,1)S(1)}, u32[]{:S(2)}, u32[]{:S(2)}) collective-permute-start(bf16[128,768]{1,0:T(8,128)(2,1)S(1)} %get-tuple-element.59.refs_0_.refs_2_), channel_id=1, source_target_pairs={{0,16},{16,0},{32,48},{48,32},{64,80},{80,64},{96,112},{112,96},{1... | collective-permute-start | bytes 589832 | tf_op jit(solution)/shard_map/ppermute | solution.py:438
  22.9 5.8 %collective-permute-start.4 = (bf16[128,768]{1,0:T(8,128)(2,1)S(1)}, bf16[128,768]{1,0:T(8,128)(2,1)S(1)}, u32[]{:S(2)}, u32[]{:S(2)}) collective-permute-start(bf16[128,768]{1,0:T(8,128)(2,1)S(1)} %collective-permute-done.3.refs_2_.refs_4_), channel_id=1, source_target_pairs={{0,16},{16,0},{32,48},{48,32},{64,80},{80,64},{96,112},{112,96},{1... | collective-permute-start | bytes 589832 | tf_op jit(solution)/shard_map/ppermute | solution.py:438
  24.4 7.6 %collective-permute-start.5 = (bf16[128,768]{1,0:T(8,128)(2,1)S(1)}, bf16[128,768]{1,0:T(8,128)(2,1)S(1)}, u32[]{:S(2)}, u32[]{:S(2)}) collective-permute-start(bf16[128,768]{1,0:T(8,128)(2,1)S(1)} %collective-permute-done.2.refs_1_.refs_3_), channel_id=1, source_target_pairs={{0,112},{16,32},{32,16},{48,64},{64,48},{80,96},{96,80},{112,0},{1... | collective-permute-start | bytes 589832 | tf_op jit(solution)/shard_map/ppermute | solution.py:438
  28.7 6.9 %collective-permute-start.7 = (bf16[128,768]{1,0:T(8,128)(2,1)S(1)}, bf16[128,768]{1,0:T(8,128)(2,1)S(1)}, u32[]{:S(2)}, u32[]{:S(2)}) collective-permute-start(bf16[128,768]{1,0:T(8,128)(2,1)S(1)} %collective-permute-done.4.refs_3_.refs_5_), channel_id=1, source_target_pairs={{0,112},{16,32},{32,16},{48,64},{64,48},{80,96},{96,80},{112,0},{1... | collective-permute-start | bytes 589832 | tf_op jit(solution)/shard_map/ppermute | solution.py:438
  32.0 7.9 %copy-start.1 = (bf16[128,768]{1,0:T(8,128)(2,1)}, bf16[128,768]{1,0:T(8,128)(2,1)S(1)}, u32[]{:S(2)}) copy-start(bf16[128,768]{1,0:T(8,128)(2,1)S(1)} %collective-permute-done.5.refs_4_.refs_6_) | copy-start | bytes 589828
  32.0 6.7 %collective-permute-start.6 = (bf16[128,768]{1,0:T(8,128)(2,1)S(1)}, bf16[128,768]{1,0:T(8,128)(2,1)S(1)}, u32[]{:S(2)}, u32[]{:S(2)}) collective-permute-start(bf16[128,768]{1,0:T(8,128)(2,1)S(1)} %collective-permute-done.5.refs_4_.refs_6_), channel_id=1, source_target_pairs={{0,16},{16,0},{32,48},{48,32},{64,80},{80,64},{96,112},{112,96},{1... | collective-permute-start | bytes 589832 | tf_op jit(solution)/shard_map/ppermute | solution.py:438
  35.6 10.1 %collective-permute-start.8 = (bf16[64,768]{1,0:T(8,128)(2,1)S(1)}, bf16[64,768]{1,0:T(8,128)(2,1)S(1)}, u32[]{:S(2)}, u32[]{:S(2)}) collective-permute-start(bf16[64,768]{1,0:T(8,128)(2,1)S(1)} %slice.19), channel_id=1, source_target_pairs={{0,16},{16,0},{32,48},{48,32},{64,80},{80,64},{96,112},{112,96},{1... | collective-permute-start | bytes 294920 | tf_op jit(solution)/shard_map/ppermute | solution.py:438
  39.4 6.3 %collective-permute-start.9 = (bf16[64,768]{1,0:T(8,128)(2,1)}, bf16[64,768]{1,0:T(8,128)(2,1)S(1)}, u32[]{:S(2)}, u32[]{:S(2)}) collective-permute-start(bf16[64,768]{1,0:T(8,128)(2,1)} %slice.20), channel_id=1, source_target_pairs={{0,112},{16,32},{32,16},{48,64},{64,48},{80,96},{96,80},{112,0},{1... | collective-permute-start | bytes 294920 | tf_op jit(solution)/shard_map/ppermute | solution.py:438
  45.7 9.0 %copy-start.4 = (f32[128,768]{1,0:T(8,128)}, f32[128,768]{1,0:T(8,128)S(1)}, u32[]{:S(2)}) copy-start(f32[128,768]{1,0:T(8,128)S(1)} %get-tuple-element.61.pa_ref) | copy-start | bytes 1179652
  45.7 9.0 %copy-start.6 = (f32[128,768]{1,0:T(8,128)}, f32[128,768]{1,0:T(8,128)S(1)}, u32[]{:S(2)}) copy-start(f32[128,768]{1,0:T(8,128)S(1)} %get-tuple-element.62.pb_ref) | copy-start | bytes 1179652
  45.7 9.0 %copy-start.8 = (f32[128,768]{1,0:T(8,128)}, f32[128,768]{1,0:T(8,128)S(1)}, u32[]{:S(2)}) copy-start(f32[128,768]{1,0:T(8,128)S(1)} %get-tuple-element.63.pa_ref) | copy-start | bytes 1179652
  45.7 9.0 %copy-start.10 = (f32[128,768]{1,0:T(8,128)}, f32[128,768]{1,0:T(8,128)S(1)}, u32[]{:S(2)}) copy-start(f32[128,768]{1,0:T(8,128)S(1)} %get-tuple-element.64.pb_ref) | copy-start | bytes 1179652
  47.3 4.7 %collective-permute-start.10 = (bf16[64,768]{1,0:T(8,128)(2,1)S(1)}, bf16[64,768]{1,0:T(8,128)(2,1)S(1)}, u32[]{:S(2)}, u32[]{:S(2)}) collective-permute-start(bf16[64,768]{1,0:T(8,128)(2,1)S(1)} %get-tuple-element.68), channel_id=1, source_target_pairs={{0,16},{16,0},{32,48},{48,32},{64,80},{80,64},{96,112},{112,96},{1... | collective-permute-start | bytes 294920 | tf_op jit(solution)/shard_map/ppermute | solution.py:438
  48.0 5.8 %collective-permute-start.11 = (bf16[64,768]{1,0:T(8,128)(2,1)S(1)}, bf16[64,768]{1,0:T(8,128)(2,1)S(1)}, u32[]{:S(2)}, u32[]{:S(2)}) collective-permute-start(bf16[64,768]{1,0:T(8,128)(2,1)S(1)} %get-tuple-element.69), channel_id=1, source_target_pairs={{0,112},{16,32},{32,16},{48,64},{64,48},{80,96},{96,80},{112,0},{1... | collective-permute-start | bytes 294920 | tf_op jit(solution)/shard_map/ppermute | solution.py:438
  54.7 13.6 %collective-permute-start.12 = (bf16[128,768]{1,0:T(8,128)(2,1)}, bf16[128,768]{1,0:T(8,128)(2,1)}, u32[]{:S(2)}, u32[]{:S(2)}) collective-permute-start(bf16[128,768]{1,0:T(8,128)(2,1)} %get-tuple-element.70), channel_id=1, source_target_pairs={{0,16},{16,0},{32,48},{48,32},{64,80},{80,64},{96,112},{112,96},{1... | collective-permute-start | bytes 589832 | tf_op jit(solution)/shard_map/ppermute | solution.py:438
  55.0 13.3 %collective-permute-start.13 = (bf16[128,768]{1,0:T(8,128)(2,1)}, bf16[128,768]{1,0:T(8,128)(2,1)}, u32[]{:S(2)}, u32[]{:S(2)}) collective-permute-start(bf16[128,768]{1,0:T(8,128)(2,1)} %get-tuple-element.71), channel_id=1, source_target_pairs={{0,112},{16,32},{32,16},{48,64},{64,48},{80,96},{96,80},{112,0},{1... | collective-permute-start | bytes 589832 | tf_op jit(solution)/shard_map/ppermute | solution.py:438
  61.6 6.7 %copy-start.9 = (f32[128,768]{1,0:T(8,128)S(1)}, f32[128,768]{1,0:T(8,128)}, u32[]{:S(2)}) copy-start(f32[128,768]{1,0:T(8,128)} %copy-done.8) | copy-start | bytes 1179652
  61.6 24.7 %all-to-all-start.1 = ((bf16[8,128,768]{2,1,0:T(8,128)(2,1)}), bf16[8,128,768]{2,1,0:T(8,128)(2,1)S(1)}, u32[]{:S(2)}, u32[]{:S(2)}) async-start(bf16[8,128,768]{2,1,0:T(8,128)(2,1)} %bitcast.23), calls=%async_computation.1 | async-start | bytes 3145728 | tf_op jit(solution)/shard_map/all_to_all | solution.py:478
  69.3 8.2 %copy-start.5 = (f32[128,768]{1,0:T(8,128)S(1)}, f32[128,768]{1,0:T(8,128)}, u32[]{:S(2)}) copy-start(f32[128,768]{1,0:T(8,128)} %copy-done.4) | copy-start | bytes 1179652
  70.5 5.8 %collective-permute-start.14 = (bf16[128,768]{1,0:T(8,128)(2,1)S(1)}, bf16[128,768]{1,0:T(8,128)(2,1)S(1)}, u32[]{:S(2)}, u32[]{:S(2)}) collective-permute-start(bf16[128,768]{1,0:T(8,128)(2,1)S(1)} %get-tuple-element.72), channel_id=1, source_target_pairs={{0,16},{16,0},{32,48},{48,32},{64,80},{80,64},{96,112},{112,96},{1... | collective-permute-start | bytes 589832 | tf_op jit(solution)/shard_map/ppermute | solution.py:438
  70.6 7.0 %collective-permute-start.15 = (bf16[128,768]{1,0:T(8,128)(2,1)S(1)}, bf16[128,768]{1,0:T(8,128)(2,1)S(1)}, u32[]{:S(2)}, u32[]{:S(2)}) collective-permute-start(bf16[128,768]{1,0:T(8,128)(2,1)S(1)} %get-tuple-element.73), channel_id=1, source_target_pairs={{0,112},{16,32},{32,16},{48,64},{64,48},{80,96},{96,80},{112,0},{1... | collective-permute-start | bytes 589832 | tf_op jit(solution)/shard_map/ppermute | solution.py:438
  73.3 15.2 %collective-permute-start = (bf16[128,1536]{1,0:T(8,128)(2,1)}, bf16[128,1536]{1,0:T(8,128)(2,1)}, u32[]{:S(2)}, u32[]{:S(2)}) collective-permute-start(bf16[128,1536]{1,0:T(8,128)(2,1)} %bitcast.3.x_hbm), channel_id=1, source_target_pairs={{0,1},{1,0},{2,3},{3,2},{4,5},{5,4},{6,7},{7,6},{8,9},{9,8},{10,11... | collective-permute-start | bytes 1179656 | tf_op jit(solution)/shard_map/ppermute | solution.py:432
  73.3 15.2 %collective-permute-start.1 = (bf16[128,1536]{1,0:T(8,128)(2,1)}, bf16[128,1536]{1,0:T(8,128)(2,1)}, u32[]{:S(2)}, u32[]{:S(2)}) collective-permute-start(bf16[128,1536]{1,0:T(8,128)(2,1)} %bitcast.4.x_hbm.y_hbm), channel_id=1, source_target_pairs={{0,1},{1,0},{2,3},{3,2},{4,5},{5,4},{6,7},{7,6},{8,9},{9,8},{10,11... | collective-permute-start | bytes 1179656 | tf_op jit(solution)/shard_map/ppermute | solution.py:432
  78.6 5.8 %collective-permute-start.16 = (bf16[128,768]{1,0:T(8,128)(2,1)S(1)}, bf16[128,768]{1,0:T(8,128)(2,1)S(1)}, u32[]{:S(2)}, u32[]{:S(2)}) collective-permute-start(bf16[128,768]{1,0:T(8,128)(2,1)S(1)} %get-tuple-element.74), channel_id=1, source_target_pairs={{0,16},{16,0},{32,48},{48,32},{64,80},{80,64},{96,112},{112,96},{1... | collective-permute-start | bytes 589832 | tf_op jit(solution)/shard_map/ppermute | solution.py:438
  79.4 6.9 %collective-permute-start.17 = (bf16[128,768]{1,0:T(8,128)(2,1)S(1)}, bf16[128,768]{1,0:T(8,128)(2,1)S(1)}, u32[]{:S(2)}, u32[]{:S(2)}) collective-permute-start(bf16[128,768]{1,0:T(8,128)(2,1)S(1)} %get-tuple-element.75), channel_id=1, source_target_pairs={{0,112},{16,32},{32,16},{48,64},{64,48},{80,96},{96,80},{112,0},{1... | collective-permute-start | bytes 589832 | tf_op jit(solution)/shard_map/ppermute | solution.py:438
  88.3 1.5 %collective-permute-start.18 = (bf16[256,384]{1,0:T(8,128)(2,1)S(1)}, bf16[256,384]{1,0:T(8,128)(2,1)S(1)}, u32[]{:S(2)}, u32[]{:S(2)}) collective-permute-start(bf16[256,384]{1,0:T(8,128)(2,1)S(1)} %get-tuple-element.79), channel_id=1, source_target_pairs={{0,1},{1,0},{2,3},{3,2},{4,5},{5,4},{6,7},{7,6},{8,9},{9,8},{10,11... | collective-permute-start | bytes 589832 | tf_op jit(solution)/shard_map/ppermute | solution.py:432
  93.2 5.9 %copy-start = (bf16[1536,768]{1,0:T(8,128)(2,1)S(1)}, bf16[1536,768]{1,0:T(8,128)(2,1)}, u32[]{:S(2)}) copy-start(bf16[1536,768]{1,0:T(8,128)(2,1)} %head_ref.1) | copy-start | bytes 7077892
  93.2 23.5 %all-to-all-start.2 = ((bf16[8,208,384]{2,1,0:T(8,128)(2,1)}), bf16[8,208,384]{2,1,0:T(8,128)(2,1)}, u32[]{:S(2)}, u32[]{:S(2)}) async-start(bf16[8,208,384]{2,1,0:T(8,128)(2,1)} %shard_map.109), calls=%async_computation.2 | async-start | bytes 2555904 | tf_op jit(solution)/shard_map/all_to_all | solution.py:492
  133.5 5.7 %collective-permute-start.19 = (f32[32,384]{1,0:T(8,128)S(1)}, f32[32,384]{1,0:T(8,128)S(1)}, u32[]{:S(2)}, u32[]{:S(2)}) collective-permute-start(f32[32,384]{1,0:T(8,128)S(1)} %convert_reduce_fusion.s_ref), channel_id=1, source_target_pairs={{0,2},{2,0},{1,3},{3,1},{4,6},{6,4},{5,7},{7,5},{8,10},{10,8},{9,1... | collective-permute-start | bytes 147464 | tf_op jit(solution)/shard_map/ppermute | solution.py:432
  139.2 1.3 collective-permute-start.20
  (4 other events, 7.2 us)

commit v3 on v2

--- a/solution.py
+++ b/solution.py
@@ -72,65 +72,70 @@
 PARTS = 3
 
 
-def proj_kernel(copies, x_hbm, head_hbm, *refs):
-    b_ref, unit_hbm, norm_hbm, x_v, head_v, unit_v, norm_v, low_v, in_sem, out_sem = refs[-10:]
+def proj_kernel(
+    x_hbm, y_hbm, head_hbm, u_ref, v_hbm, ui_hbm, ni_hbm, ut_hbm, nt_hbm,
+    x_v, y_v, head_v, unit_v, norm_v, low_v, in_sem, out_sem,
+):
     deep = D // PARTS
     get_x = pltpu.make_async_copy(x_hbm, x_v, in_sem.at[PARTS])
+    get_y = pltpu.make_async_copy(y_hbm, y_v, in_sem.at[PARTS + 1])
     get = [
         pltpu.make_async_copy(head_hbm.at[pl.ds(k * deep, deep)], head_v.at[pl.ds(k * deep, deep)], in_sem.at[k])
         for k in range(PARTS)
     ]
-    get_x.start()
+    get_y.start()
     for c in get:
         c.start()
-    get_x.wait()
+    get_x.start()
+    put = []
+
+    def send(src, dst):
+        put.append(pltpu.make_async_copy(src, dst, out_sem.at[len(put)]))
+        put[-1].start()
+
+    def finish(k, proj, unit_hbm, norm_hbm):
+        norm = jnp.sqrt(jnp.sum(proj * proj, axis=1, keepdims=True) + 1e-06)
+        unit = proj / norm
+        unit_v[k] = unit
+        norm_v[k] = jnp.broadcast_to(norm, (R, 128))
+        send(unit_v.at[k], unit_hbm)
+        send(norm_v.at[k], norm_hbm)
+        return unit.astype(BF16)
+
+    get_y.wait()
     proj = None
     for k, c in enumerate(get):
         c.wait()
-        part = dot(x_v[:, k * deep : (k + 1) * deep], head_v[k * deep : (k + 1) * deep], NN)
+        part = dot(y_v[:, k * deep : (k + 1) * deep], head_v[k * deep : (k + 1) * deep], NN)
         proj = part if proj is None else proj + part
-    norm = jnp.sqrt(jnp.sum(proj * proj, axis=1, keepdims=True) + 1e-06)
-    unit = proj / norm
-    unit_v[...] = unit
-    norm_v[...] = jnp.broadcast_to(norm, (R, 128))
-    put = [
-        pltpu.make_async_copy(unit_v, unit_hbm, out_sem.at[0]),
-        pltpu.make_async_copy(norm_v, norm_hbm, out_sem.at[1]),
-    ]
-    for c in put:
-        c.start()
-    low = unit.astype(BF16)
-    if copies == 1:
-        b_ref[...] = low
-    else:
-        low_v[...] = low
-        for k in range(copies):
-            put.append(pltpu.make_async_copy(low_v, b_ref.at[pl.ds(k * R, R)], out_sem.at[2 + k]))
-            put[-1].start()
+    low_v[...] = finish(0, proj, ut_hbm, nt_hbm)
+    for k in range(8):
+        send(low_v, v_hbm.at[pl.ds(k * R, R)])
+    get_x.wait()
+    u_ref[...] = finish(1, dot(x_v[...], head_v[...], NN), ui_hbm, ni_hbm)
     for c in put:
         c.wait()
 
 
-def project(copies, x, head, after=()):
-    return vmem_call(
-        functools.partial(proj_kernel, copies),
-        (
-            jax.ShapeDtypeStruct((copies * R, E), BF16),
-            jax.ShapeDtypeStruct((R, E), F32),
-            jax.ShapeDtypeStruct((R, 128), F32),
-        ),
+def project(x, y, head):
+    unit = jax.ShapeDtypeStruct((R, E), F32)
+    norm = jax.ShapeDtypeStruct((R, 128), F32)
+    return vmem_call(
+        proj_kernel,
+        (jax.ShapeDtypeStruct((R, E), BF16), jax.ShapeDtypeStruct((8 * R, E), BF16), unit, norm, unit, norm),
         scratch=(
             pltpu.VMEM((R, D), BF16),
+            pltpu.VMEM((R, D), BF16),
             pltpu.VMEM((D, E), BF16),
-            pltpu.VMEM((R, E), F32),
-            pltpu.VMEM((R, 128), F32),
+            pltpu.VMEM((2, R, E), F32),
+            pltpu.VMEM((2, R, 128), F32),
             pltpu.VMEM((R, E), BF16),
-            pltpu.SemaphoreType.DMA((PARTS + 1,)),
-            pltpu.SemaphoreType.DMA((2 + copies,)),
+            pltpu.SemaphoreType.DMA((PARTS + 2,)),
+            pltpu.SemaphoreType.DMA((12,)),
         ),
-        specs=[HB] * (2 + len(after)), out_specs=(HB if copies > 1 else VM, HB, HB),
-        flops=2 * R * D * E, nbytes=2 * (R * D + D * E),
-    )(x, head, *after)
+        specs=[HB] * 3, out_specs=(VM, HB, HB, HB, HB, HB),
+        flops=4 * R * D * E, nbytes=2 * (2 * R * D + D * E),
+    )(x, y, head)
 
 
 SUB = 8
@@ -205,12 +210,12 @@
         sums_ref[i] = tot[i] if own else tot[i] + before_ref[i]
 
 
-def pair(chunks, own, scal, at, v, us, dtype, before=()):
+def pair(chunks, own, scal, at, v, us, before=()):
     rows = sum(u.shape[0] for u in us)
     most = max(sum(us[k].shape[0] for k in c) for c in chunks)
     cols = v.shape[0]
     out = (
-        *(jax.ShapeDtypeStruct(u.shape, dtype) for u in us),
+        *(jax.ShapeDtypeStruct(u.shape, BF16) for u in us),
         jax.ShapeDtypeStruct((rows, cols), BF16),
         jax.ShapeDtypeStruct((3, SUB, CB), F32),
     )
@@ -223,8 +228,9 @@
 
 
 def cols_kernel(*refs):
-    n = len(refs) - 6
-    g1_ref, g2_ref, u_refs, (dv_hbm, u_all, dv_ref, sem) = refs[0], refs[1], refs[2 : 2 + n], refs[-4:]
+    n = len(refs) - 7
+    g1_ref, g2_ref, u_refs, (dv_hbm, done_ref, u_all, dv_ref, sem) = refs[0], refs[1], refs[2 : 2 + n], refs[-5:]
+    done_ref[...] = jnp.zeros(done_ref.shape, F32)
     at = 0
     for ref in u_refs:
         u_all[at : at + ref.shape[0]] = ref[...]
@@ -246,54 +252,50 @@
     rows = g1.shape[0] + g2.shape[0]
     cols = g1.shape[1]
     return vmem_call(
-        cols_kernel, jax.ShapeDtypeStruct((cols, E), BF16),
+        cols_kernel, (jax.ShapeDtypeStruct((cols, E), BF16), jax.ShapeDtypeStruct((8, 128), F32)),
         scratch=(pltpu.VMEM((rows, E), BF16), pltpu.VMEM((cols, E), BF16), pltpu.SemaphoreType.DMA((2,))),
-        specs=[VP, VP] + [VM] * len(us), out_specs=HB,
+        specs=[VP, VP] + [VM] * len(us), out_specs=(HB, VM),
         flops=2 * rows * cols * E, nbytes=2 * (rows * cols + rows * E + cols * E),
     )(g1, g2, *us)
 
 
-def step_kernel(pa_ref, pb_ref, ra_ref, rb_ref, a_ref, b_ref):
-    half = ra_ref.shape[0]
-    if half == R:
-        a_ref[...] = (pa_ref[...] + rb_ref[...].astype(F32)).astype(BF16)
-        b_ref[...] = (pb_ref[...] + ra_ref[...].astype(F32)).astype(BF16)
-    else:
-        a_ref[:half] = pa_ref[:half].astype(BF16)
-        a_ref[half:] = (pa_ref[half:] + rb_ref[...].astype(F32)).astype(BF16)
-        b_ref[:half] = (pb_ref[:half] + ra_ref[...].astype(F32)).astype(BF16)
-        b_ref[half:] = pb_ref[half:].astype(BF16)
+def step_kernel(n, *refs):
+    for k in range(n):
+        refs[-n + k][...] = (refs[k][...].astype(F32) + refs[n + k][...].astype(F32)).astype(BF16)
 
 
 STEP_FLOPS = 8 * 10**9
 
 
-def ring_step(pa, pb, ra, rb):
-    low = jax.ShapeDtypeStruct((R, E), BF16)
-    return vmem_call(step_kernel, (low, low), specs=[VP, VP, VM, VM], flops=STEP_FLOPS, nbytes=16 * R * E)(pa, pb, ra, rb)
+def ring_step(own, got, after=()):
+    n = len(own)
+    return vmem_call(
+        functools.partial(step_kernel, n), (jax.ShapeDtypeStruct((R, E), BF16),) * n,
+        specs=[VP] * n + [VM] * (n + len(after)), flops=STEP_FLOPS, nbytes=12 * R * E,
+    )(*own, *got, *after)
 
 
 def back_kernel(
-    scal_ref, ui_hbm, ni_hbm, ut_hbm, nt_hbm, du_ref, qa_ref, qb_ref, dv_ref,
-    di_ref, dt_ref, keep_ref, send_ref, ui_ref, ni_ref, ut_ref, nt_ref, sem,
+    scal_ref, ui_hbm, ni_hbm, ut_hbm, nt_hbm, dv_hbm, du_ref, qa_ref, qb_ref,
+    di_ref, dt_ref, keep_ref, send_ref, ui_ref, ni_ref, ut_ref, nt_ref, dv_ref, sem,
 ):
     get = [
         pltpu.make_async_copy(src, dst, sem.at[k])
         for k, (src, dst) in enumerate(
-            ((ui_hbm, ui_ref), (ni_hbm, ni_ref), (ut_hbm, ut_ref), (nt_hbm, nt_ref))
+            ((dv_hbm, dv_ref), (ui_hbm, ui_ref), (ni_hbm, ni_ref), (ut_hbm, ut_ref), (nt_hbm, nt_ref))
         )
     ]
     for c in get:
         c.start()
     scale = scal_ref[0, 0]
     low = scal_ref[0, 1] == 0.0
-    du = scale * (du_ref[...] + qa_ref[...].astype(F32) + qb_ref[...].astype(F32))
+    du = scale * (du_ref[...].astype(F32) + qa_ref[...].astype(F32) + qb_ref[...].astype(F32))
+    for c in get:
+        c.wait()
     dv = dv_ref[:R].astype(F32)
     for j in range(1, 8):
         dv = dv + dv_ref[j * R : (j + 1) * R].astype(F32)
     dv = scale * dv
-    for c in get:
-        c.wait()
     for k, (unit_ref, norm_ref, grad, out_ref) in enumerate(
         ((ui_ref, ni_ref, du, di_ref), (ut_ref, nt_ref, dv, dt_ref))
     ):
@@ -309,13 +311,14 @@
     low = jax.ShapeDtypeStruct((R, E), BF16)
     half = jax.ShapeDtypeStruct((2 * R, H), BF16)
     return vmem_call(
-        back_kernel, (low, low, half, half), specs=[SM] + [HB] * 4 + [VP] + [VM] * 3,
+        back_kernel, (low, low, half, half), specs=[SM] + [HB] * 5 + [VP] + [VM] * 2,
         scratch=(
             pltpu.VMEM((R, E), F32),
             pltpu.VMEM((R, 128), F32),
             pltpu.VMEM((R, E), F32),
             pltpu.VMEM((R, 128), F32),
-            pltpu.SemaphoreType.DMA((4,)),
+            pltpu.VMEM((8 * R, E), BF16),
+            pltpu.SemaphoreType.DMA((5,)),
         ),
         flops=20 * R * E, nbytes=30 * R * E,
     )(scal, *args)
@@ -339,21 +342,34 @@
 PAD = 16
 
 
-def head_grad_kernel(x_hbm, y_hbm, ox_hbm, oy_hbm, keep_ref, got_ref, extra_ref, out_hbm, x_all, d_all, out_v, in_sem, out_sem):
+def turn_kernel(*refs):
+    hbm, (out_ref, x_all, sem) = refs[:4], refs[-3:]
     get = []
-    for i, src in enumerate((x_hbm, y_hbm, ox_hbm, oy_hbm)):
-        get.append(pltpu.make_async_copy(src, x_all.at[pl.ds(i * R, R)], in_sem.at[i]))
+    for i, src in enumerate(hbm):
+        get.append(pltpu.make_async_copy(src, x_all.at[pl.ds(i * R, R)], sem.at[i]))
         get[i].start()
+    for c in get:
+        c.wait()
+    out_ref[...] = x_all[...].T
+
+
+def turn(*data):
+    return vmem_call(
+        turn_kernel, jax.ShapeDtypeStruct((D, 4 * R), BF16),
+        scratch=(pltpu.VMEM((4 * R, D), BF16), pltpu.SemaphoreType.DMA((4,))),
+        specs=[HB] * 4, out_specs=VP, flops=4 * R * D, nbytes=16 * R * D,
+    )(*data)
+
+
+def head_grad_kernel(xt_ref, keep_ref, got_ref, extra_ref, out_hbm, d_all, out_v, out_sem):
     d_all[: 2 * R] = keep_ref[...]
     d_all[2 * R :] = got_ref[...]
     for j in range(8):
         out_v[j, 8 * ZROWS :] = extra_ref[...]
     d = d_all[...]
-    for c in get:
-        c.wait()
     put = []
     for xl in range(2):
-        full = dot(x_all[:, xl * E : (xl + 1) * E], d, TN)
+        full = dot(xt_ref[xl * E : (xl + 1) * E], d, NN)
         for y in range(4):
             for z in range(0, 8, 2):
                 a = (z * 4 + y) * ZROWS
@@ -367,19 +383,17 @@
         c.wait()
 
 
-def head_grad_parts(x, y, ox, oy, keep, got, extra):
+def head_grad_parts(xt, keep, got, extra):
     shape = (8, 8 * ZROWS + PAD, H)
     return vmem_call(
         head_grad_kernel, jax.ShapeDtypeStruct(shape, BF16),
         scratch=(
-            pltpu.VMEM((4 * R, D), BF16),
             pltpu.VMEM((4 * R, H), BF16),
             pltpu.VMEM(shape, BF16),
-            pltpu.SemaphoreType.DMA((4,)),
             pltpu.SemaphoreType.DMA((2,)),
         ),
-        specs=[HB] * 4 + [VM] * 3, out_specs=HB, flops=8 * R * D * H, nbytes=2 * (4 * R * D + D * H),
-    )(x, y, ox, oy, keep, got, extra)
+        specs=[VP] + [VM] * 3, out_specs=HB, flops=8 * R * D * H, nbytes=2 * (4 * R * D + D * H),
+    )(xt, keep, got, extra)
 
 
 def sum_kernel(parts_ref, _, out_ref):
@@ -458,37 +472,37 @@
     cc = swap("c")
     near = ("xl", "y")
 
-    u, ui, ni = project(1, x, head)
+    u, v, ui, ni, ut, nt = project(x, y, head)
+
     a1, b1 = z1(u), z2(u)
-    v, ut, nt = project(8, y, head, (ni,))
-
     vs = lax.all_to_all(v, near, 0, 0, tiled=True)
     a2, b2 = z1(b1), z2(a1)
     a3, b3 = z1(b2), z2(a2)
-    fa, fb = z1(b3[: R // 2]), z2(a3[R // 2 :])
-    ox, oy = cc(x), cc(y)
+    far = z1(b3)
+    xt = turn(x, y, cc(x), cc(y))
 
     scal = jnp.stack([scale * LOG2E, bias * LOG2E]).reshape(1, 2)
     at = (lax.axis_index(near) * R).reshape(1, 1)
     us = (u, a1, b1, a2, b2, a3, b3)
-    *p, g1, sums = pair(((0,), (1, 2), (3, 4), (5, 6)), True, scal, at, vs, us, F32)
-    qa, qb, g2, sums = pair(((0, 1),), False, scal, at, vs, (fa, fb), BF16, (sums,))
-
-    qa, qb = z1(qa), z2(qb)
-    dv = lax.all_to_all(pair_cols(g1, g2, (*us, fa, fb)), near, 0, 0, tiled=True)
-    for k in (5, 3, 1):
-        qa, qb = ring_step(p[k], p[k + 1], qa, qb)
-        qa, qb = z1(qa), z2(qb)
+    p0, pa1, pb1, pa2, pb2, pa3, pb3, g1, sums = pair(((0,), (1, 2), (3, 4), (5, 6)), True, scal, at, vs, us)
+    pf, g2, sums = pair(((0,),), False, scal, at, vs, (far,), (sums,))
+
+    dv, done = pair_cols(g1, g2, (*us, far))
+    (qa,) = ring_step((pb3,), (z1(pf),), (done,))
+    dv = lax.all_to_all(dv, near, 0, 0, tiled=True)
+    qa, qb = ring_step((pa2, pb2), (z2(qa), z1(pa3)))
+    qa, qb = ring_step((pb1, pa1), (z1(qa), z2(qb)))
+    qa, qb = z2(qa), z1(qb)
 
     sums = jnp.sum(sums, axis=(1, 2))
     extra = scalar_rows(jnp.zeros((H,), F32).at[:3].set(sums), PAD)
 
     scal2 = jnp.stack([scale, core.astype(F32)]).reshape(1, 2)
-    di, dt, keep, send = back(scal2, ui, ni, ut, nt, p[0], qa, qb, dv)
+    di, dt, keep, send = back(scal2, ui, ni, ut, nt, dv, p0, qa, qb)
     got = cc(send)
     gi, gt, done = input_grad(di, dt, head)
 
-    parts = head_grad_parts(x, y, ox, oy, keep, got, extra)
+    parts = head_grad_parts(xt, keep, got, extra)
     parts = lax.all_to_all(parts, ("xl", "y"), 0, 0, tiled=True)
     parts = lax.all_to_all(sum_parts(parts, done), "z", 0, 0, tiled=True)
     s = jnp.sum(parts.astype(F32), axis=0)

time: 144 us -> 131 us (0.910)
  starting transfers between devices: 43.2 us -> 39.7 us
  Pallas kernels: 29 us -> 25.9 us
  waiting for transfers between devices: 47.9 us -> 45.4 us
  blocking collectives: 15.3 us -> 13.5 us
  local copies, waits for them, and re-layouts: 3.71 us -> 2.23 us
    pallas_call x13, Pallas kernels: 29 us -> 25.9 us  [call(): pl.pallas_call(kernel, out_shape=jax.tree.map(place_out, out_shape, out_s...]
    ppermute x8 -> x6, starting transfers between devices: 22 us -> 19 us  [ring(): lax.ppermute(v, axis, odd)]
    ppermute x8 -> x6, waiting for transfers between devices: 12.2 us -> 10.2 us  [ring(): lax.ppermute(v, axis, odd)]
    all_to_all x1, blocking collectives: 15.3 us -> 13.5 us  [per_device(): parts = lax.all_to_all(sum_parts(parts, done), 'z', 0, 0, tiled=True)]
    all_to_all x1, starting transfers between devices: 6.71 us -> 5.03 us  [per_device(): dv = lax.all_to_all(dv, near, 0, 0, tiled=True)]
    unnamed x24 -> x28, local copies, waits for them, and re-layouts: 2.95 us -> 2.14 us
  transfers between devices with their start and end apart: 24 -> 22, of which waited for: 16 -> 15; matrix products, arithmetic and copies ran while one was open for 1% -> 0% of each run, Pallas kernels for 10% -> 10%
where the time goes in v3:
time: 131 us; the launch traced here: 129 us
  waiting for transfers between devices  45.4 us (35%)
  starting transfers between devices  39.7 us (30%)
  Pallas kernels  25.9 us (20%)
  blocking collectives  13.5 us (10%)
  local copies, waits for them, and re-layouts  2.23 us (2%)
  between operations  2.2 us (2%)
    pallas_call x13, Pallas kernels, call(): pl.pallas_call(kernel, out_shape=jax.tree.map(place_out, out_shape, out_s...  25.9 us
    ppermute x6, starting transfers between devices, ring(): lax.ppermute(v, axis, odd)  19 us
    all_to_all x1, waiting for transfers between devices, per_device(): parts = lax.all_to_all(parts, ('xl', 'y'), 0, 0, tiled=True)  15.3 us
    all_to_all x1, blocking collectives, per_device(): parts = lax.all_to_all(sum_parts(parts, done), 'z', 0, 0, tiled=True)  13.5 us
    ppermute x8, waiting for transfers between devices, ring(): lax.ppermute(v, axis, even)  12.5 us
    ppermute x6, waiting for transfers between devices, ring(): lax.ppermute(v, axis, odd)  10.2 us
    ppermute x5, waiting for transfers between devices, swap(): return lambda v: lax.ppermute(v, axis, [(0, 1), (1, 0)])  7.37 us
    all_to_all x1, starting transfers between devices, per_device(): parts = lax.all_to_all(parts, ('xl', 'y'), 0, 0, tiled=True)  6.68 us
  transfers between devices with their start and end apart: 22, of which 15 were waited for; matrix products, arithmetic and copies ran while one was open for 0% of the time, Pallas kernels for 10%

profile of v3, /device:TPU:4, one launch (start us, length us, event | category | flops | bytes accessed | tf_op | source)
XLA Modules:
  0.0 129.3 jit_solution(6356421763774499999)
XLA Ops:
  0.6 3.8 %shard_map.101 = (bf16[128,768]{1,0:T(8,128)(2,1)S(1)}, bf16[1024,768]{1,0:T(8,128)(2,1)}, f32[128,768]{1,0:T(8,128)}, f32[128,128]{1,0:T(8,128)}, f32[128,768]{1,0:T(8,128)}, /*index=5*/f32[128,128]{1,0:T(8,128)}) custom-call(bf16[128,1536]{1,0:T(8,128)(2,1)} %bitcast.22, bf16[128,1536]{1,0:T(8,128)(2,1)} %bitcast.25, bf16[1536,768]{1,0:T(8,128)(2,1)} %head_ref.1), custom_call_target="tpu_custom_call" | custom-call | flops 603979776 | bytes 3145728 | tf_op jit(solution)/shard_map/pallas_call | solution.py:59
  4.5 5.1 %all-to-all-start = ((bf16[8,128,768]{2,1,0:T(8,128)(2,1)}), bf16[8,128,768]{2,1,0:T(8,128)(2,1)S(1)}, u32[]{:S(2)}, u32[]{:S(2)}) async-start(bf16[8,128,768]{2,1,0:T(8,128)(2,1)} %bitcast.29), calls=%async_computation | async-start | bytes 3145728 | tf_op jit(solution)/shard_map/all_to_all | solution.py:478
  9.6 5.9 %collective-permute-start.3 = (bf16[128,768]{1,0:T(8,128)(2,1)S(1)}, bf16[128,768]{1,0:T(8,128)(2,1)S(1)}, u32[]{:S(2)}, u32[]{:S(2)}) collective-permute-start(bf16[128,768]{1,0:T(8,128)(2,1)S(1)} %get-tuple-element.58.refs_0_.refs_2_), channel_id=1, source_target_pairs={{0,112},{16,32},{32,16},{48,64},{64,48},{80,96},{96,80},{112,0},{1... | collective-permute-start | bytes 589832 | tf_op jit(solution)/shard_map/ppermute | solution.py:452
  15.4 4.6 %collective-permute-done.3.refs_2_.refs_4_ = bf16[128,768]{1,0:T(8,128)(2,1)S(1)} collective-permute-done((bf16[128,768]{1,0:T(8,128)(2,1)S(1)}, bf16[128,768]{1,0:T(8,128)(2,1)S(1)}, u32[]{:S(2)}, u32[]{:S(2)}) %collective-permute-start.3) | collective-permute-done | bytes 196640 | tf_op jit(solution)/shard_map/ppermute | solution.py:452
  20.0 1.5 %collective-permute-done.2.refs_1_.refs_3_ = bf16[128,768]{1,0:T(8,128)(2,1)S(1)} collective-permute-done((bf16[128,768]{1,0:T(8,128)(2,1)S(1)}, bf16[128,768]{1,0:T(8,128)(2,1)S(1)}, u32[]{:S(2)}, u32[]{:S(2)}) %collective-permute-start.2) | collective-permute-done | bytes 196640 | tf_op jit(solution)/shard_map/ppermute | solution.py:452
  21.5 1.5 %collective-permute-start.5 = (bf16[128,768]{1,0:T(8,128)(2,1)S(1)}, bf16[128,768]{1,0:T(8,128)(2,1)S(1)}, u32[]{:S(2)}, u32[]{:S(2)}) collective-permute-start(bf16[128,768]{1,0:T(8,128)(2,1)S(1)} %collective-permute-done.2.refs_1_.refs_3_), channel_id=1, source_target_pairs={{0,112},{16,32},{32,16},{48,64},{64,48},{80,96},{96,80},{112,0},{1... | collective-permute-start | bytes 589832 | tf_op jit(solution)/shard_map/ppermute | solution.py:452
  23.0 2.8 %collective-permute-done.4.refs_3_.refs_5_ = bf16[128,768]{1,0:T(8,128)(2,1)S(1)} collective-permute-done((bf16[128,768]{1,0:T(8,128)(2,1)S(1)}, bf16[128,768]{1,0:T(8,128)(2,1)S(1)}, u32[]{:S(2)}, u32[]{:S(2)}) %collective-permute-start.4) | collective-permute-done | bytes 196640 | tf_op jit(solution)/shard_map/ppermute | solution.py:452
  25.8 2.9 %collective-permute-start.7 = (bf16[128,768]{1,0:T(8,128)(2,1)S(1)}, bf16[128,768]{1,0:T(8,128)(2,1)S(1)}, u32[]{:S(2)}, u32[]{:S(2)}) collective-permute-start(bf16[128,768]{1,0:T(8,128)(2,1)S(1)} %collective-permute-done.4.refs_3_.refs_5_), channel_id=1, source_target_pairs={{0,112},{16,32},{32,16},{48,64},{64,48},{80,96},{96,80},{112,0},{1... | collective-permute-start | bytes 589832 | tf_op jit(solution)/shard_map/ppermute | solution.py:452
  30.5 2.2 %collective-permute-done.7.refs_6_.refs_8_ = bf16[128,768]{1,0:T(8,128)(2,1)S(1)} collective-permute-done((bf16[128,768]{1,0:T(8,128)(2,1)S(1)}, bf16[128,768]{1,0:T(8,128)(2,1)S(1)}, u32[]{:S(2)}, u32[]{:S(2)}) %collective-permute-start.7) | collective-permute-done | bytes 196640 | tf_op jit(solution)/shard_map/ppermute | solution.py:452
  32.7 3.9 %collective-permute-done.6.refs_5_.refs_7_ = bf16[128,768]{1,0:T(8,128)(2,1)S(1)} collective-permute-done((bf16[128,768]{1,0:T(8,128)(2,1)S(1)}, bf16[128,768]{1,0:T(8,128)(2,1)S(1)}, u32[]{:S(2)}, u32[]{:S(2)}) %collective-permute-start.6) | collective-permute-done | bytes 196640 | tf_op jit(solution)/shard_map/ppermute | solution.py:452
  36.6 5.4 %shard_map.102 = (bf16[128,768]{1,0:T(8,128)(2,1)S(1)}, bf16[128,768]{1,0:T(8,128)(2,1)S(1)}, bf16[128,768]{1,0:T(8,128)(2,1)S(1)}, bf16[128,768]{1,0:T(8,128)(2...) custom-call(f32[1,2]{1,0:T(1,128)S(1)} %maximum_bitcast_fusion.1.sca, ...), custom_call_target="tpu_custom_call" | custom-call | flops 2818572288 | bytes 5898240 | tf_op jit(solution)/shard_map/pallas_call | solution.py:59
  43.3 1.6 %shard_map.103 = (bf16[128,768]{1,0:T(8,128)(2,1)S(1)}, bf16[128,1024]{1,0:T(8,128)(2,1)S(1)}, f32[3,8,256]{2,1,0:T(8,128)S(1)}) custom-call(f32[1,2]{1,0:T(1,128)S(1)} %maximum_bitcast_fusion.1.scal_ref, s32[1,1]{1,0:T(1,128)} %bitcast.8.at_ref, bf16[1024,768]{1,0:T(8,128)(2,1)S(1)} %bitcast.21, f32[3,8,256]{2,1,0:T(8,128)S(1)} %get-tuple-element.60.refs_0_, ...), custom_call_target="tpu_custom_call" | custom-call | flops 402653184 | bytes 3538944 | tf_op jit(solution)/shard_map/pallas_call | solution.py:59
  45.0 2.0 %collective-permute-start.11 = (bf16[128,768]{1,0:T(8,128)(2,1)}, bf16[128,768]{1,0:T(8,128)(2,1)S(1)}, u32[]{:S(2)}, u32[]{:S(2)}) collective-permute-start(bf16[128,768]{1,0:T(8,128)(2,1)} %get-tuple-element.71), channel_id=1, source_target_pairs={{0,16},{16,0},{32,48},{48,32},{64,80},{80,64},{96,112},{112,96},{1... | collective-permute-start | bytes 589832 | tf_op jit(solution)/shard_map/ppermute | solution.py:452
  47.0 3.5 %shard_map.104 = (bf16[1024,768]{1,0:T(8,128)(2,1)}, f32[8,128]{1,0:T(8,128)S(1)}) custom-call(bf16[896,1024]{1,0:T(8,128)(2,1)S(1)} %get-tuple-element.59.refs_0_, bf16[128,1024]{1,0:T(8,128)(2,1)S(1)} %get-tuple-element.61.refs_1_, bf16[128,768]{1,0:T(8,128)(2,1)S(1)} %get-tuple-element.58.refs_0_.refs_2_, ...), custom_call_target="tpu_custom_call" | custom-call | flops 1610612736 | bytes 5242880 | tf_op jit(solution)/shard_map/pallas_call | solution.py:59
  50.7 2.2 %collective-permute-start.10 = (bf16[128,768]{1,0:T(8,128)(2,1)S(1)}, bf16[128,768]{1,0:T(8,128)(2,1)S(1)}, u32[]{:S(2)}, u32[]{:S(2)}) collective-permute-start(bf16[128,768]{1,0:T(8,128)(2,1)S(1)} %shard_map.105), channel_id=1, source_target_pairs={{0,112},{16,32},{32,16},{48,64},{64,48},{80,96},{96,80},{112,0},{1... | collective-permute-start | bytes 589832 | tf_op jit(solution)/shard_map/ppermute | solution.py:452
  53.0 5.0 %all-to-all-start.1 = ((bf16[8,128,768]{2,1,0:T(8,128)(2,1)}), bf16[8,128,768]{2,1,0:T(8,128)(2,1)}, u32[]{:S(2)}, u32[]{:S(2)}) async-start(bf16[8,128,768]{2,1,0:T(8,128)(2,1)} %bitcast.28), calls=%async_computation.1 | async-start | bytes 3145728 | tf_op jit(solution)/shard_map/all_to_all | solution.py:492
  58.4 2.7 %collective-permute-start.13 = (bf16[128,768]{1,0:T(8,128)(2,1)S(1)}, bf16[128,768]{1,0:T(8,128)(2,1)S(1)}, u32[]{:S(2)}, u32[]{:S(2)}) collective-permute-start(bf16[128,768]{1,0:T(8,128)(2,1)S(1)} %get-tuple-element.73), channel_id=1, source_target_pairs={{0,112},{16,32},{32,16},{48,64},{64,48},{80,96},{96,80},{112,0},{1... | collective-permute-start | bytes 589832 | tf_op jit(solution)/shard_map/ppermute | solution.py:452
  61.8 2.2 %collective-permute-done.12.refs_2_ = bf16[128,768]{1,0:T(8,128)(2,1)S(1)} collective-permute-done((bf16[128,768]{1,0:T(8,128)(2,1)S(1)}, bf16[128,768]{1,0:T(8,128)(2,1)S(1)}, u32[]{:S(2)}, u32[]{:S(2)}) %collective-permute-start.12) | collective-permute-done | bytes 196640 | tf_op jit(solution)/shard_map/ppermute | solution.py:452
  63.9 2.1 %collective-permute-done.13.refs_3_ = bf16[128,768]{1,0:T(8,128)(2,1)S(1)} collective-permute-done((bf16[128,768]{1,0:T(8,128)(2,1)S(1)}, bf16[128,768]{1,0:T(8,128)(2,1)S(1)}, u32[]{:S(2)}, u32[]{:S(2)}) %collective-permute-start.13) | collective-permute-done | bytes 196640 | tf_op jit(solution)/shard_map/ppermute | solution.py:452
  66.2 3.8 %collective-permute-start.14 = (bf16[128,768]{1,0:T(8,128)(2,1)S(1)}, bf16[128,768]{1,0:T(8,128)(2,1)S(1)}, u32[]{:S(2)}, u32[]{:S(2)}) collective-permute-start(bf16[128,768]{1,0:T(8,128)(2,1)S(1)} %get-tuple-element.74), channel_id=1, source_target_pairs={{0,112},{16,32},{32,16},{48,64},{64,48},{80,96},{96,80},{112,0},{1... | collective-permute-start | bytes 589832 | tf_op jit(solution)/shard_map/ppermute | solution.py:452
  70.8 1.8 %shard_map.100.xt_ref = bf16[1536,512]{1,0:T(8,128)(2,1)S(1)} custom-call(bf16[128,1536]{1,0:T(8,128)(2,1)} %bitcast.23, bf16[128,1536]{1,0:T(8,128)(2,1)} %bitcast.26, bf16[128,1536]{1,0:T(8,128)(2,1)} %copy-done.13, bf16[128,1536]{1,0:T(8,128)(2,1)} %collective-permute-done.1.refs_3_), custom_call_target="tpu_custom_call" | custom-call | flops 786432 | bytes 3145728 | tf_op jit(solution)/shard_map/pallas_call | solution.py:59
  73.6 2.0 %collective-permute-done.15.qb_ref = bf16[128,768]{1,0:T(8,128)(2,1)S(1)} collective-permute-done((bf16[128,768]{1,0:T(8,128)(2,1)S(1)}, bf16[128,768]{1,0:T(8,128)(2,1)S(1)}, u32[]{:S(2)}, u32[]{:S(2)}) %collective-permute-start.15) | collective-permute-done | bytes 196640 | tf_op jit(solution)/shard_map/ppermute | solution.py:452
  75.6 2.7 %shard_map.108 = (bf16[128,768]{1,0:T(8,128)(2,1)S(1)}, bf16[128,768]{1,0:T(8,128)(2,1)S(1)}, bf16[256,384]{1,0:T(8,128)(2,1)S(1)}, bf16[256,384]{1,0:T(8,128)(2,1)S(1)}) custom-call(f32[1,2]{1,0:T(1,128)S(1)} %maximum_bitcast_fusion.scal_ref, f32[128,768]{1,0:T(8,128)} %get-tuple-element.53.ui_hbm, f32[128,128]{1,0:T(8,128)} %get-tuple-element.54.ni_hbm, ...), custom_call_target="tpu_custom_call" | custom-call | flops 1966080 | bytes 2949120 | tf_op jit(solution)/shard_map/pallas_call | solution.py:59
  78.5 1.4 %collective-permute-done.16.got_ref = bf16[256,384]{1,0:T(8,128)(2,1)S(1)} collective-permute-done((bf16[256,384]{1,0:T(8,128)(2,1)S(1)}, bf16[256,384]{1,0:T(8,128)(2,1)S(1)}, u32[]{:S(2)}, u32[]{:S(2)}) %collective-permute-start.16) | collective-permute-done | bytes 196640 | tf_op jit(solution)/shard_map/ppermute | solution.py:446
  79.8 1.9 %shard_map.109 = bf16[8,208,384]{2,1,0:T(8,128)(2,1)} custom-call(bf16[1536,512]{1,0:T(8,128)(2,1)S(1)} %shard_map.100.xt_ref, bf16[256,384]{1,0:T(8,128)(2,1)S(1)} %get-tuple-element.76.keep_ref, bf16[256,384]{1,0:T(8,128)(2,1)S(1)} %collective-permute-done.16.got_ref, bf16[16,384]{1,0:T(8,128)(2,1)S(1)} %maximum_maximum_fusion.extra_ref), custom_call_target="tpu_custom_call" | custom-call | flops 603979776 | bytes 2752512 | tf_op jit(solution)/shard_map/pallas_call | solution.py:59
  81.7 6.7 %all-to-all-start.2 = ((bf16[8,208,384]{2,1,0:T(8,128)(2,1)}), bf16[8,208,384]{2,1,0:T(8,128)(2,1)}, u32[]{:S(2)}, u32[]{:S(2)}) async-start(bf16[8,208,384]{2,1,0:T(8,128)(2,1)} %shard_map.109), calls=%async_computation.2 | async-start | bytes 2555904 | tf_op jit(solution)/shard_map/all_to_all | solution.py:506
  88.4 2.4 %shard_map.110 = (bf16[128,1536]{1,0:T(8,128)(2,1)}, bf16[128,1536]{1,0:T(8,128)(2,1)}, f32[8,128]{1,0:T(8,128)S(1)}) custom-call(bf16[128,768]{1,0:T(8,128)(2,1)S(1)} %get-tuple-element.79.di_ref, bf16[128,768]{1,0:T(8,128)(2,1)S(1)} %get-tuple-element.80.dt_ref, bf16[1536,768]{1,0:T(8,128)(2,1)S(1)} %copy-done), custom_call_target="tpu_custom_call" | custom-call | flops 603979776 | bytes 3932160 | tf_op jit(solution)/shard_map/pallas_call | solution.py:59
  90.8 15.3 %all-to-all-done.2.parts_ref = bf16[8,208,384]{2,1,0:T(8,128)(2,1)} async-done(((bf16[8,208,384]{2,1,0:T(8,128)(2,1)}), bf16[8,208,384]{2,1,0:T(8,128)(2,1)}, u32[]{:S(2)}, u32[]{:S(2)}) %all-to-all-start.2) | async-done | bytes 1277984 | tf_op jit(solution)/shard_map/all_to_all | solution.py:506
  106.1 1.5 %shard_map.111 = bf16[8,32,384]{2,1,0:T(8,128)(2,1)S(1)} custom-call(bf16[8,208,384]{2,1,0:T(8,128)(2,1)} %all-to-all-done.2.parts_ref, f32[8,128]{1,0:T(8,128)S(1)} %get-tuple-element.81._), custom_call_target="tpu_custom_call" | custom-call | flops 6389760 | bytes 1277952 | tf_op jit(solution)/shard_map/pallas_call | solution.py:59
  107.5 13.5 %all_to_all.32 = bf16[8,32,384]{2,1,0:T(8,128)(2,1)S(1)} all-to-all(bf16[8,32,384]{2,1,0:T(8,128)(2,1)S(1)} %shard_map.111), channel_id=1, replica_groups=mesh['xl'=2,'z'=8,'y'=4,'xh'=2,'c'=2] {'z'}, dimensions={0} | all-to-all | bytes 393216 | tf_op jit(solution)/shard_map/all_to_all | solution.py:507
  122.0 4.8 %collective-permute-done.17.r_ref = f32[32,384]{1,0:T(8,128)S(1)} collective-permute-done((f32[32,384]{1,0:T(8,128)S(1)}, f32[32,384]{1,0:T(8,128)S(1)}, u32[]{:S(2)}, u32[]{:S(2)}) %collective-permute-start.17) | collective-permute-done | bytes 49184 | tf_op jit(solution)/shard_map/ppermute | solution.py:446
  126.9 1.2 collective-permute-done.18.o_ref
  (66 shorter events, 7.4 us)
Async XLA Ops:
  4.5 32.1 %all-to-all-start = ((bf16[8,128,768]{2,1,0:T(8,128)(2,1)}), bf16[8,128,768]{2,1,0:T(8,128)(2,1)S(1)}, u32[]{:S(2)}, u32[]{:S(2)}) async-start(bf16[8,128,768]{2,1,0:T(8,128)(2,1)} %bitcast.29), calls=%async_computation | async-start | bytes 3145728 | tf_op jit(solution)/shard_map/all_to_all | solution.py:478
  9.6 10.5 %collective-permute-start.3 = (bf16[128,768]{1,0:T(8,128)(2,1)S(1)}, bf16[128,768]{1,0:T(8,128)(2,1)S(1)}, u32[]{:S(2)}, u32[]{:S(2)}) collective-permute-start(bf16[128,768]{1,0:T(8,128)(2,1)S(1)} %get-tuple-element.58.refs_0_.refs_2_), channel_id=1, source_target_pairs={{0,112},{16,32},{32,16},{48,64},{64,48},{80,96},{96,80},{112,0},{1... | collective-permute-start | bytes 589832 | tf_op jit(solution)/shard_map/ppermute | solution.py:452
  15.4 6.1 %collective-permute-start.2 = (bf16[128,768]{1,0:T(8,128)(2,1)S(1)}, bf16[128,768]{1,0:T(8,128)(2,1)S(1)}, u32[]{:S(2)}, u32[]{:S(2)}) collective-permute-start(bf16[128,768]{1,0:T(8,128)(2,1)S(1)} %get-tuple-element.58.refs_0_.refs_2_), channel_id=1, source_target_pairs={{0,16},{16,0},{32,48},{48,32},{64,80},{80,64},{96,112},{112,96},{1... | collective-permute-start | bytes 589832 | tf_op jit(solution)/shard_map/ppermute | solution.py:452
  20.0 5.8 %collective-permute-start.4 = (bf16[128,768]{1,0:T(8,128)(2,1)S(1)}, bf16[128,768]{1,0:T(8,128)(2,1)S(1)}, u32[]{:S(2)}, u32[]{:S(2)}) collective-permute-start(bf16[128,768]{1,0:T(8,128)(2,1)S(1)} %collective-permute-done.3.refs_2_.refs_4_), channel_id=1, source_target_pairs={{0,16},{16,0},{32,48},{48,32},{64,80},{80,64},{96,112},{112,96},{1... | collective-permute-start | bytes 589832 | tf_op jit(solution)/shard_map/ppermute | solution.py:452
  21.5 7.6 %collective-permute-start.5 = (bf16[128,768]{1,0:T(8,128)(2,1)S(1)}, bf16[128,768]{1,0:T(8,128)(2,1)S(1)}, u32[]{:S(2)}, u32[]{:S(2)}) collective-permute-start(bf16[128,768]{1,0:T(8,128)(2,1)S(1)} %collective-permute-done.2.refs_1_.refs_3_), channel_id=1, source_target_pairs={{0,112},{16,32},{32,16},{48,64},{64,48},{80,96},{96,80},{112,0},{1... | collective-permute-start | bytes 589832 | tf_op jit(solution)/shard_map/ppermute | solution.py:452
  25.8 6.9 %collective-permute-start.7 = (bf16[128,768]{1,0:T(8,128)(2,1)S(1)}, bf16[128,768]{1,0:T(8,128)(2,1)S(1)}, u32[]{:S(2)}, u32[]{:S(2)}) collective-permute-start(bf16[128,768]{1,0:T(8,128)(2,1)S(1)} %collective-permute-done.4.refs_3_.refs_5_), channel_id=1, source_target_pairs={{0,112},{16,32},{32,16},{48,64},{64,48},{80,96},{96,80},{112,0},{1... | collective-permute-start | bytes 589832 | tf_op jit(solution)/shard_map/ppermute | solution.py:452
  29.1 7.5 %collective-permute-start.6 = (bf16[128,768]{1,0:T(8,128)(2,1)S(1)}, bf16[128,768]{1,0:T(8,128)(2,1)S(1)}, u32[]{:S(2)}, u32[]{:S(2)}) collective-permute-start(bf16[128,768]{1,0:T(8,128)(2,1)S(1)} %collective-permute-done.5.refs_4_.refs_6_), channel_id=1, source_target_pairs={{0,16},{16,0},{32,48},{48,32},{64,80},{80,64},{96,112},{112,96},{1... | collective-permute-start | bytes 589832 | tf_op jit(solution)/shard_map/ppermute | solution.py:452
  32.7 10.7 %collective-permute-start.8 = (bf16[128,768]{1,0:T(8,128)(2,1)S(1)}, bf16[128,768]{1,0:T(8,128)(2,1)S(1)}, u32[]{:S(2)}, u32[]{:S(2)}) collective-permute-start(bf16[128,768]{1,0:T(8,128)(2,1)S(1)} %collective-permute-done.7.refs_6_.refs_8_), channel_id=1, source_target_pairs={{0,16},{16,0},{32,48},{48,32},{64,80},{80,64},{96,112},{112,96},{1... | collective-permute-start | bytes 589832 | tf_op jit(solution)/shard_map/ppermute | solution.py:452
  36.6 5.4 %copy-start.1 = (bf16[128,768]{1,0:T(8,128)(2,1)}, bf16[128,768]{1,0:T(8,128)(2,1)S(1)}, u32[]{:S(2)}) copy-start(bf16[128,768]{1,0:T(8,128)(2,1)S(1)} %collective-permute-done.6.refs_5_.refs_7_) | copy-start | bytes 589828
  43.3 1.7 %copy-start.5 = (bf16[128,768]{1,0:T(8,128)(2,1)}, bf16[128,768]{1,0:T(8,128)(2,1)S(1)}, u32[]{:S(2)}) copy-start(bf16[128,768]{1,0:T(8,128)(2,1)S(1)} %get-tuple-element.64.refs_0_) | copy-start | bytes 589828
  43.3 3.7 %copy-start.2 = (bf16[128,768]{1,0:T(8,128)(2,1)S(1)}, bf16[128,768]{1,0:T(8,128)(2,1)}, u32[]{:S(2)}) copy-start(bf16[128,768]{1,0:T(8,128)(2,1)} %copy-done.1) | copy-start | bytes 589828
  44.9 5.8 %collective-permute-start.9 = (bf16[128,768]{1,0:T(8,128)(2,1)S(1)}, bf16[128,768]{1,0:T(8,128)(2,1)S(1)}, u32[]{:S(2)}, u32[]{:S(2)}) collective-permute-start(bf16[128,768]{1,0:T(8,128)(2,1)S(1)} %get-tuple-element.69), channel_id=1, source_target_pairs={{0,16},{16,0},{32,48},{48,32},{64,80},{80,64},{96,112},{112,96},{1... | collective-permute-start | bytes 589832 | tf_op jit(solution)/shard_map/ppermute | solution.py:452
  45.0 13.0 %collective-permute-start.11 = (bf16[128,768]{1,0:T(8,128)(2,1)}, bf16[128,768]{1,0:T(8,128)(2,1)S(1)}, u32[]{:S(2)}, u32[]{:S(2)}) collective-permute-start(bf16[128,768]{1,0:T(8,128)(2,1)} %get-tuple-element.71), channel_id=1, source_target_pairs={{0,16},{16,0},{32,48},{48,32},{64,80},{80,64},{96,112},{112,96},{1... | collective-permute-start | bytes 589832 | tf_op jit(solution)/shard_map/ppermute | solution.py:452
  50.7 7.3 %collective-permute-start.10 = (bf16[128,768]{1,0:T(8,128)(2,1)S(1)}, bf16[128,768]{1,0:T(8,128)(2,1)S(1)}, u32[]{:S(2)}, u32[]{:S(2)}) collective-permute-start(bf16[128,768]{1,0:T(8,128)(2,1)S(1)} %shard_map.105), channel_id=1, source_target_pairs={{0,112},{16,32},{32,16},{48,64},{64,48},{80,96},{96,80},{112,0},{1... | collective-permute-start | bytes 589832 | tf_op jit(solution)/shard_map/ppermute | solution.py:452
  53.0 5.0 %copy-start.8 = (bf16[128,768]{1,0:T(8,128)(2,1)S(1)}, bf16[128,768]{1,0:T(8,128)(2,1)}, u32[]{:S(2)}) copy-start(bf16[128,768]{1,0:T(8,128)(2,1)} %copy-done.7) | copy-start | bytes 589828
  53.0 5.1 %copy-start.10 = (bf16[128,768]{1,0:T(8,128)(2,1)S(1)}, bf16[128,768]{1,0:T(8,128)(2,1)}, u32[]{:S(2)}) copy-start(bf16[128,768]{1,0:T(8,128)(2,1)} %copy-done.9) | copy-start | bytes 589828
  53.0 22.7 %all-to-all-start.1 = ((bf16[8,128,768]{2,1,0:T(8,128)(2,1)}), bf16[8,128,768]{2,1,0:T(8,128)(2,1)}, u32[]{:S(2)}, u32[]{:S(2)}) async-start(bf16[8,128,768]{2,1,0:T(8,128)(2,1)} %bitcast.28), calls=%async_computation.1 | async-start | bytes 3145728 | tf_op jit(solution)/shard_map/all_to_all | solution.py:492
  58.0 3.1 %copy-start.11 = (bf16[1,128,1536]{2,1,0:T(8,128)(2,1)S(1)}, bf16[1,128,1536]{2,1,0:T(8,128)(2,1)}, u32[]{:S(2)}) copy-start(bf16[1,128,1536]{2,1,0:T(8,128)(2,1)} %param.7) | copy-start | bytes 1179652
  58.1 3.1 %copy-start.12 = (bf16[1,128,1536]{2,1,0:T(8,128)(2,1)S(1)}, bf16[1,128,1536]{2,1,0:T(8,128)(2,1)}, u32[]{:S(2)}) copy-start(bf16[1,128,1536]{2,1,0:T(8,128)(2,1)} %param.8) | copy-start | bytes 1179652
  58.1 8.0 %copy-start.4 = (bf16[128,768]{1,0:T(8,128)(2,1)S(1)}, bf16[128,768]{1,0:T(8,128)(2,1)}, u32[]{:S(2)}) copy-start(bf16[128,768]{1,0:T(8,128)(2,1)} %copy-done.3) | copy-start | bytes 589828
  58.1 8.0 %copy-start.6 = (bf16[128,768]{1,0:T(8,128)(2,1)S(1)}, bf16[128,768]{1,0:T(8,128)(2,1)}, u32[]{:S(2)}) copy-start(bf16[128,768]{1,0:T(8,128)(2,1)} %copy-done.5) | copy-start | bytes 589828
  58.2 5.8 %collective-permute-start.12 = (bf16[128,768]{1,0:T(8,128)(2,1)S(1)}, bf16[128,768]{1,0:T(8,128)(2,1)S(1)}, u32[]{:S(2)}, u32[]{:S(2)}) collective-permute-start(bf16[128,768]{1,0:T(8,128)(2,1)S(1)} %get-tuple-element.72), channel_id=1, source_target_pairs={{0,16},{16,0},{32,48},{48,32},{64,80},{80,64},{96,112},{112,96},{1... | collective-permute-start | bytes 589832 | tf_op jit(solution)/shard_map/ppermute | solution.py:452
  58.4 7.6 %collective-permute-start.13 = (bf16[128,768]{1,0:T(8,128)(2,1)S(1)}, bf16[128,768]{1,0:T(8,128)(2,1)S(1)}, u32[]{:S(2)}, u32[]{:S(2)}) collective-permute-start(bf16[128,768]{1,0:T(8,128)(2,1)S(1)} %get-tuple-element.73), channel_id=1, source_target_pairs={{0,112},{16,32},{32,16},{48,64},{64,48},{80,96},{96,80},{112,0},{1... | collective-permute-start | bytes 589832 | tf_op jit(solution)/shard_map/ppermute | solution.py:452
  61.2 8.9 %collective-permute-start = (bf16[128,1536]{1,0:T(8,128)(2,1)S(1)}, bf16[128,1536]{1,0:T(8,128)(2,1)S(1)}, u32[]{:S(2)}, u32[]{:S(2)}) collective-permute-start(bf16[128,1536]{1,0:T(8,128)(2,1)S(1)} %bitcast.24), channel_id=1, source_target_pairs={{0,1},{1,0},{2,3},{3,2},{4,5},{5,4},{6,7},{7,6},{8,9},{9,8},{10,11... | collective-permute-start | bytes 1179656 | tf_op jit(solution)/shard_map/ppermute | solution.py:446
  61.2 9.6 %collective-permute-start.1 = (bf16[128,1536]{1,0:T(8,128)(2,1)S(1)}, bf16[128,1536]{1,0:T(8,128)(2,1)}, u32[]{:S(2)}, u32[]{:S(2)}) collective-permute-start(bf16[128,1536]{1,0:T(8,128)(2,1)S(1)} %bitcast.27), channel_id=1, source_target_pairs={{0,1},{1,0},{2,3},{3,2},{4,5},{5,4},{6,7},{7,6},{8,9},{9,8},{10,11... | collective-permute-start | bytes 1179656 | tf_op jit(solution)/shard_map/ppermute | solution.py:446
  66.2 7.4 %collective-permute-start.14 = (bf16[128,768]{1,0:T(8,128)(2,1)S(1)}, bf16[128,768]{1,0:T(8,128)(2,1)S(1)}, u32[]{:S(2)}, u32[]{:S(2)}) collective-permute-start(bf16[128,768]{1,0:T(8,128)(2,1)S(1)} %get-tuple-element.74), channel_id=1, source_target_pairs={{0,112},{16,32},{32,16},{48,64},{64,48},{80,96},{96,80},{112,0},{1... | collective-permute-start | bytes 589832 | tf_op jit(solution)/shard_map/ppermute | solution.py:452
  70.0 5.7 %collective-permute-start.15 = (bf16[128,768]{1,0:T(8,128)(2,1)S(1)}, bf16[128,768]{1,0:T(8,128)(2,1)S(1)}, u32[]{:S(2)}, u32[]{:S(2)}) collective-permute-start(bf16[128,768]{1,0:T(8,128)(2,1)S(1)} %get-tuple-element.75), channel_id=1, source_target_pairs={{0,16},{16,0},{32,48},{48,32},{64,80},{80,64},{96,112},{112,96},{1... | collective-permute-start | bytes 589832 | tf_op jit(solution)/shard_map/ppermute | solution.py:452
  78.3 1.5 %collective-permute-start.16 = (bf16[256,384]{1,0:T(8,128)(2,1)S(1)}, bf16[256,384]{1,0:T(8,128)(2,1)S(1)}, u32[]{:S(2)}, u32[]{:S(2)}) collective-permute-start(bf16[256,384]{1,0:T(8,128)(2,1)S(1)} %get-tuple-element.77), channel_id=1, source_target_pairs={{0,1},{1,0},{2,3},{3,2},{4,5},{5,4},{6,7},{7,6},{8,9},{9,8},{10,11... | collective-permute-start | bytes 589832 | tf_op jit(solution)/shard_map/ppermute | solution.py:446
  81.7 6.7 %copy-start = (bf16[1536,768]{1,0:T(8,128)(2,1)S(1)}, bf16[1536,768]{1,0:T(8,128)(2,1)}, u32[]{:S(2)}) copy-start(bf16[1536,768]{1,0:T(8,128)(2,1)} %head_ref.1) | copy-start | bytes 7077892
  81.7 24.3 %all-to-all-start.2 = ((bf16[8,208,384]{2,1,0:T(8,128)(2,1)}), bf16[8,208,384]{2,1,0:T(8,128)(2,1)}, u32[]{:S(2)}, u32[]{:S(2)}) async-start(bf16[8,208,384]{2,1,0:T(8,128)(2,1)} %shard_map.109), calls=%async_computation.2 | async-start | bytes 2555904 | tf_op jit(solution)/shard_map/all_to_all | solution.py:506
  121.1 5.7 %collective-permute-start.17 = (f32[32,384]{1,0:T(8,128)S(1)}, f32[32,384]{1,0:T(8,128)S(1)}, u32[]{:S(2)}, u32[]{:S(2)}) collective-permute-start(f32[32,384]{1,0:T(8,128)S(1)} %convert_reduce_fusion.s_ref), channel_id=1, source_target_pairs={{0,2},{2,0},{1,3},{3,1},{4,6},{6,4},{5,7},{7,5},{8,10},{10,8},{9,1... | collective-permute-start | bytes 147464 | tf_op jit(solution)/shard_map/ppermute | solution.py:446
  126.8 1.3 %collective-permute-start.18 = (f32[32,384]{1,0:T(8,128)S(1)}, f32[32,384]{1,0:T(8,128)S(1)}, u32[]{:S(2)}, u32[]{:S(2)}) collective-permute-start(f32[32,384]{1,0:T(8,128)S(1)} %add.11), channel_id=1, source_target_pairs={{0,1},{1,0},{2,3},{3,2},{4,5},{5,4},{6,7},{7,6},{8,9},{9,8},{10,11... | collective-permute-start | bytes 147464 | tf_op jit(solution)/shard_map/ppermute | solution.py:446
  (4 other events, 3.8 us)

commit v4 on v3

--- a/solution.py
+++ b/solution.py
@@ -227,20 +227,24 @@
     )(scal, at, v, *before, *us)
 
 
-def cols_kernel(*refs):
-    n = len(refs) - 7
-    g1_ref, g2_ref, u_refs, (dv_hbm, done_ref, u_all, dv_ref, sem) = refs[0], refs[1], refs[2 : 2 + n], refs[-5:]
+def cols_kernel(n, *refs):
+    g_refs, u_refs, (dv_hbm, done_ref, u_all, dv_ref, sem) = refs[:n], refs[n:-5], refs[-5:]
     done_ref[...] = jnp.zeros(done_ref.shape, F32)
     at = 0
     for ref in u_refs:
-        u_all[at : at + ref.shape[0]] = ref[...]
-        at += ref.shape[0]
-    k = g1_ref.shape[0]
+        u_all[at : at + R] = ref[...]
+        at += R
     cols = dv_ref.shape[0] // 2
     put = []
     for i in range(2):
         at = pl.ds(i * cols, cols)
-        dv = dot(g1_ref[:, at], u_all[:k], TN) + dot(g2_ref[:, at], u_all[k:], TN)
+        dv = None
+        row = 0
+        for g in g_refs:
+            k = g.shape[0]
+            part = dot(g[:, at], u_all[row : row + k], TN)
+            dv = part if dv is None else dv + part
+            row += k
         dv_ref[at] = dv.astype(BF16)
         put.append(pltpu.make_async_copy(dv_ref.at[at], dv_hbm.at[at], sem.at[i]))
         put[i].start()
@@ -248,15 +252,16 @@
         c.wait()
 
 
-def pair_cols(g1, g2, us):
-    rows = g1.shape[0] + g2.shape[0]
-    cols = g1.shape[1]
-    return vmem_call(
-        cols_kernel, (jax.ShapeDtypeStruct((cols, E), BF16), jax.ShapeDtypeStruct((8, 128), F32)),
+def pair_cols(gs, us):
+    rows = sum(g.shape[0] for g in gs)
+    cols = gs[0].shape[1]
+    return vmem_call(
+        functools.partial(cols_kernel, len(gs)),
+        (jax.ShapeDtypeStruct((cols, E), BF16), jax.ShapeDtypeStruct((8, 128), F32)),
         scratch=(pltpu.VMEM((rows, E), BF16), pltpu.VMEM((cols, E), BF16), pltpu.SemaphoreType.DMA((2,))),
-        specs=[VP, VP] + [VM] * len(us), out_specs=(HB, VM),
+        specs=[VP] * len(gs) + [VM] * len(us), out_specs=(HB, VM),
         flops=2 * rows * cols * E, nbytes=2 * (rows * cols + rows * E + cols * E),
-    )(g1, g2, *us)
+    )(*gs, *us)
 
 
 def step_kernel(n, *refs):
@@ -282,29 +287,32 @@
     get = [
         pltpu.make_async_copy(src, dst, sem.at[k])
         for k, (src, dst) in enumerate(
-            ((dv_hbm, dv_ref), (ui_hbm, ui_ref), (ni_hbm, ni_ref), (ut_hbm, ut_ref), (nt_hbm, nt_ref))
+            ((ui_hbm, ui_ref), (ni_hbm, ni_ref), (ut_hbm, ut_ref), (nt_hbm, nt_ref), (dv_hbm, dv_ref))
         )
     ]
     for c in get:
         c.start()
     scale = scal_ref[0, 0]
     low = scal_ref[0, 1] == 0.0
-    du = scale * (du_ref[...].astype(F32) + qa_ref[...].astype(F32) + qb_ref[...].astype(F32))
-    for c in get:
-        c.wait()
-    dv = dv_ref[:R].astype(F32)
-    for j in range(1, 8):
-        dv = dv + dv_ref[j * R : (j + 1) * R].astype(F32)
-    dv = scale * dv
-    for k, (unit_ref, norm_ref, grad, out_ref) in enumerate(
-        ((ui_ref, ni_ref, du, di_ref), (ut_ref, nt_ref, dv, dt_ref))
-    ):
+
+    def finish(k, unit_ref, norm_ref, grad, out_ref):
         unit = unit_ref[...]
         d = (grad - unit * jnp.sum(unit * grad, axis=1, keepdims=True)) / norm_ref[:, :1]
         out_ref[...] = d.astype(BF16)
         left, right = d[:, :H], d[:, H:]
         keep_ref[k * R : (k + 1) * R] = jnp.where(low, left, right).astype(BF16)
         send_ref[k * R : (k + 1) * R] = jnp.where(low, right, left).astype(BF16)
+
+    du = scale * (du_ref[...].astype(F32) + qa_ref[...].astype(F32) + qb_ref[...].astype(F32))
+    get[0].wait()
+    get[1].wait()
+    finish(0, ui_ref, ni_ref, du, di_ref)
+    for c in get[2:]:
+        c.wait()
+    dv = dv_ref[:R].astype(F32)
+    for j in range(1, 8):
+        dv = dv + dv_ref[j * R : (j + 1) * R].astype(F32)
+    finish(1, ut_ref, nt_ref, scale * dv, dt_ref)
 
 
 def back(scal, *args):
@@ -396,10 +404,16 @@
     )(xt, keep, got, extra)
 
 
-def sum_kernel(parts_ref, _, out_ref):
-    s = parts_ref[0].astype(F32)
-    for j in range(1, 8):
-        s = s + parts_ref[j].astype(F32)
+def sum_kernel(parts_hbm, _, out_ref, parts_v, sem):
+    get = [pltpu.make_async_copy(parts_hbm.at[j], parts_v.at[j], sem.at[j]) for j in range(8)]
+    for c in get:
+        c.start()
+    s = None
+    for j in range(0, 8, 2):
+        get[j].wait()
+        get[j + 1].wait()
+        pair_sum = parts_v[j].astype(F32) + parts_v[j + 1].astype(F32)
+        s = pair_sum if s is None else s + pair_sum
     t = jnp.sum(s[8 * ZROWS : 8 * ZROWS + 3], axis=0, keepdims=True)
     hi = t.astype(BF16).astype(F32)
     mid = (t - hi).astype(BF16).astype(F32)
@@ -412,7 +426,8 @@
 
 def sum_parts(parts, after):
     return vmem_call(
-        sum_kernel, jax.ShapeDtypeStruct((8, ZROWS + 8, H), BF16), n_in=2,
+        sum_kernel, jax.ShapeDtypeStruct((8, ZROWS + 8, H), BF16), specs=[HB, VM],
+        scratch=(pltpu.VMEM(parts.shape, BF16), pltpu.SemaphoreType.DMA((8,))),
         flops=10 * parts.size, nbytes=2 * parts.size,
     )(parts, after)
 
@@ -484,10 +499,11 @@
     scal = jnp.stack([scale * LOG2E, bias * LOG2E]).reshape(1, 2)
     at = (lax.axis_index(near) * R).reshape(1, 1)
     us = (u, a1, b1, a2, b2, a3, b3)
-    p0, pa1, pb1, pa2, pb2, pa3, pb3, g1, sums = pair(((0,), (1, 2), (3, 4), (5, 6)), True, scal, at, vs, us)
-    pf, g2, sums = pair(((0,),), False, scal, at, vs, (far,), (sums,))
-
-    dv, done = pair_cols(g1, g2, (*us, far))
+    p0, pa1, pb1, pa2, pb2, g1, sums = pair(((0,), (1, 2), (3, 4)), True, scal, at, vs, us[:5])
+    pa3, pb3, g2, sums = pair(((0, 1),), False, scal, at, vs, us[5:], (sums,))
+    pf, g3, sums = pair(((0,),), False, scal, at, vs, (far,), (sums,))
+
+    dv, done = pair_cols((g1, g2, g3), (*us, far))
     (qa,) = ring_step((pb3,), (z1(pf),), (done,))
     dv = lax.all_to_all(dv, near, 0, 0, tiled=True)
     qa, qb = ring_step((pa2, pb2), (z2(qa), z1(pa3)))

time: 131 us -> 128 us (0.977)
  waiting for transfers between devices: 45.4 us -> 42.7 us
  local copies, waits for them, and re-layouts: 2.23 us -> 0.9 us
    ppermute x8, waiting for transfers between devices: 12.5 us -> 10 us  [ring(): lax.ppermute(v, axis, even)]
    ppermute x6, starting transfers between devices: 19 us -> 21 us  [ring(): lax.ppermute(v, axis, odd)]
    all_to_all x1, starting transfers between devices: 6.68 us -> 4.63 us  [per_device(): parts = lax.all_to_all(parts, ('xl', 'y'), 0, 0, tiled=True)]
    unnamed x28, local copies, waits for them, and re-layouts: 2.14 us -> 0.81 us
    pallas_call x13 -> x14, Pallas kernels: 25.9 us -> 26.6 us  [call(): pl.pallas_call(kernel, out_shape=jax.tree.map(place_out, out_shape, out_s...]
  transfers between devices with their start and end apart: 22 -> 22, of which waited for: 15 -> 15; matrix products, arithmetic and copies ran while one was open for 0% -> 0% of each run, Pallas kernels for 10% -> 11%
where the time goes in v4:
time: 128 us; the launch traced here: 126 us
  waiting for transfers between devices  42.7 us (33%)
  starting transfers between devices  39.5 us (31%)
  Pallas kernels  26.6 us (21%)
  blocking collectives  14 us (11%)
  between operations  2.27 us (2%)
    pallas_call x14, Pallas kernels, call(): pl.pallas_call(kernel, out_shape=jax.tree.map(place_out, out_shape, out_s...  26.6 us
    ppermute x6, starting transfers between devices, ring(): lax.ppermute(v, axis, odd)  21 us
    all_to_all x1, waiting for transfers between devices, per_device(): parts = lax.all_to_all(parts, ('xl', 'y'), 0, 0, tiled=True)  15.3 us
    all_to_all x1, blocking collectives, per_device(): parts = lax.all_to_all(sum_parts(parts, done), 'z', 0, 0, tiled=True)  14 us
    ppermute x8, waiting for transfers between devices, ring(): lax.ppermute(v, axis, even)  10 us
    ppermute x6, waiting for transfers between devices, ring(): lax.ppermute(v, axis, odd)  9.34 us
    ppermute x5, waiting for transfers between devices, swap(): return lambda v: lax.ppermute(v, axis, [(0, 1), (1, 0)])  7.37 us
    all_to_all x1, starting transfers between devices, per_device(): vs = lax.all_to_all(v, near, 0, 0, tiled=True)  5.11 us
  transfers between devices with their start and end apart: 22, of which 15 were waited for; matrix products, arithmetic and copies ran while one was open for 0% of the time, Pallas kernels for 11%

profile of v4, /device:TPU:4, one launch (start us, length us, event | category | flops | bytes accessed | tf_op | source)
XLA Modules:
  0.0 126.3 jit_solution(17469620343747721702)
XLA Ops:
  0.6 3.8 %shard_map.101 = (bf16[128,768]{1,0:T(8,128)(2,1)S(1)}, bf16[1024,768]{1,0:T(8,128)(2,1)}, f32[128,768]{1,0:T(8,128)}, f32[128,128]{1,0:T(8,128)}, f32[128,768]{1,0:T(8,128)}, /*index=5*/f32[128,128]{1,0:T(8,128)}) custom-call(bf16[128,1536]{1,0:T(8,128)(2,1)} %bitcast.23, bf16[128,1536]{1,0:T(8,128)(2,1)} %bitcast.26, bf16[1536,768]{1,0:T(8,128)(2,1)} %head_ref.1), custom_call_target="tpu_custom_call" | custom-call | flops 603979776 | bytes 3145728 | tf_op jit(solution)/shard_map/pallas_call | solution.py:59
  4.5 5.1 %all-to-all-start = ((bf16[8,128,768]{2,1,0:T(8,128)(2,1)}), bf16[8,128,768]{2,1,0:T(8,128)(2,1)S(1)}, u32[]{:S(2)}, u32[]{:S(2)}) async-start(bf16[8,128,768]{2,1,0:T(8,128)(2,1)} %bitcast.30), calls=%async_computation | async-start | bytes 3145728 | tf_op jit(solution)/shard_map/all_to_all | solution.py:493
  9.6 5.9 %collective-permute-start.3 = (bf16[128,768]{1,0:T(8,128)(2,1)S(1)}, bf16[128,768]{1,0:T(8,128)(2,1)S(1)}, u32[]{:S(2)}, u32[]{:S(2)}) collective-permute-start(bf16[128,768]{1,0:T(8,128)(2,1)S(1)} %get-tuple-element.60.refs_0_.refs_3_), channel_id=1, source_target_pairs={{0,112},{16,32},{32,16},{48,64},{64,48},{80,96},{96,80},{112,0},{1... | collective-permute-start | bytes 589832 | tf_op jit(solution)/shard_map/ppermute | solution.py:467
  15.4 4.6 %collective-permute-done.3.refs_2_.refs_5_ = bf16[128,768]{1,0:T(8,128)(2,1)S(1)} collective-permute-done((bf16[128,768]{1,0:T(8,128)(2,1)S(1)}, bf16[128,768]{1,0:T(8,128)(2,1)S(1)}, u32[]{:S(2)}, u32[]{:S(2)}) %collective-permute-start.3) | collective-permute-done | bytes 196640 | tf_op jit(solution)/shard_map/ppermute | solution.py:467
  20.0 1.5 %collective-permute-done.2.refs_1_.refs_4_ = bf16[128,768]{1,0:T(8,128)(2,1)S(1)} collective-permute-done((bf16[128,768]{1,0:T(8,128)(2,1)S(1)}, bf16[128,768]{1,0:T(8,128)(2,1)S(1)}, u32[]{:S(2)}, u32[]{:S(2)}) %collective-permute-start.2) | collective-permute-done | bytes 196640 | tf_op jit(solution)/shard_map/ppermute | solution.py:467
  21.5 1.5 %collective-permute-start.5 = (bf16[128,768]{1,0:T(8,128)(2,1)S(1)}, bf16[128,768]{1,0:T(8,128)(2,1)S(1)}, u32[]{:S(2)}, u32[]{:S(2)}) collective-permute-start(bf16[128,768]{1,0:T(8,128)(2,1)S(1)} %collective-permute-done.2.refs_1_.refs_4_), channel_id=1, source_target_pairs={{0,112},{16,32},{32,16},{48,64},{64,48},{80,96},{96,80},{112,0},{1... | collective-permute-start | bytes 589832 | tf_op jit(solution)/shard_map/ppermute | solution.py:467
  23.0 2.8 %collective-permute-done.4.refs_3_.refs_6_ = bf16[128,768]{1,0:T(8,128)(2,1)S(1)} collective-permute-done((bf16[128,768]{1,0:T(8,128)(2,1)S(1)}, bf16[128,768]{1,0:T(8,128)(2,1)S(1)}, u32[]{:S(2)}, u32[]{:S(2)}) %collective-permute-start.4) | collective-permute-done | bytes 196640 | tf_op jit(solution)/shard_map/ppermute | solution.py:467
  25.8 2.9 %collective-permute-start.7 = (bf16[128,768]{1,0:T(8,128)(2,1)S(1)}, bf16[128,768]{1,0:T(8,128)(2,1)S(1)}, u32[]{:S(2)}, u32[]{:S(2)}) collective-permute-start(bf16[128,768]{1,0:T(8,128)(2,1)S(1)} %collective-permute-done.4.refs_3_.refs_6_), channel_id=1, source_target_pairs={{0,112},{16,32},{32,16},{48,64},{64,48},{80,96},{96,80},{112,0},{1... | collective-permute-start | bytes 589832 | tf_op jit(solution)/shard_map/ppermute | solution.py:467
  30.2 2.5 %collective-permute-done.7.refs_2_.refs_9_ = bf16[128,768]{1,0:T(8,128)(2,1)S(1)} collective-permute-done((bf16[128,768]{1,0:T(8,128)(2,1)S(1)}, bf16[128,768]{1,0:T(8,128)(2,1)S(1)}, u32[]{:S(2)}, u32[]{:S(2)}) %collective-permute-start.7) | collective-permute-done | bytes 196640 | tf_op jit(solution)/shard_map/ppermute | solution.py:467
  32.7 3.7 %shard_map.102 = (bf16[128,768]{1,0:T(8,128)(2,1)S(1)}, bf16[128,768]{1,0:T(8,128)(2,1)S(1)}, bf16[128,768]{1,0:T(8,128)(2,1)S(1)}, bf16[128,768]{1,0:T(8,128)(2...) custom-call(f32[1,2]{1,0:T(1,128)S(1)} %maximum_bitcast_fusion.1.scal_ref, ...), custom_call_target="tpu_custom_call" | custom-call | flops 2013265920 | bytes 5111808 | tf_op jit(solution)/shard_map/pallas_call | solution.py:59
  37.1 2.5 %shard_map.103 = (bf16[128,768]{1,0:T(8,128)(2,1)}, bf16[128,768]{1,0:T(8,128)(2,1)S(1)}, bf16[256,1024]{1,0:T(8,128)(2,1)S(1)}, f32[3,8,256]{2,1,0:T(8,128)S(1)}) custom-call(f32[1,2]{1,0:T(1,128)S(1)} %maximum_bitcast_fusion.1.scal_ref, s32[1,1]{1,0:T(1,128)} %bitcast.8.at_ref, bf16[1024,768]{1,0:T(8,128)(2,1)S(1)} %bitcast.21, ...), custom_call_target="tpu_custom_call" | custom-call | flops 805306368 | bytes 3932160 | tf_op jit(solution)/shard_map/pallas_call | solution.py:59
  39.7 1.6 %shard_map.104 = (bf16[128,768]{1,0:T(8,128)(2,1)S(1)}, bf16[128,1024]{1,0:T(8,128)(2,1)S(1)}, f32[3,8,256]{2,1,0:T(8,128)S(1)}) custom-call(f32[1,2]{1,0:T(1,128)S(1)} %maximum_bitcast_fusion.1.scal_ref, s32[1,1]{1,0:T(1,128)} %bitcast.8.at_ref, bf16[1024,768]{1,0:T(8,128)(2,1)S(1)} %bitcast.22, f32[3,8,256]{2,1,0:T(8,128)S(1)} %get-tuple-element.64.refs_0_, ...), custom_call_target="tpu_custom_call" | custom-call | flops 402653184 | bytes 3538944 | tf_op jit(solution)/shard_map/pallas_call | solution.py:59
  41.3 1.5 %collective-permute-start.9 = (bf16[128,768]{1,0:T(8,128)(2,1)S(1)}, bf16[128,768]{1,0:T(8,128)(2,1)S(1)}, u32[]{:S(2)}, u32[]{:S(2)}) collective-permute-start(bf16[128,768]{1,0:T(8,128)(2,1)S(1)} %get-tuple-element.73), channel_id=1, source_target_pairs={{0,16},{16,0},{32,48},{48,32},{64,80},{80,64},{96,112},{112,96},{1... | collective-permute-start | bytes 589832 | tf_op jit(solution)/shard_map/ppermute | solution.py:467
  43.4 3.3 %shard_map.105 = (bf16[1024,768]{1,0:T(8,128)(2,1)}, f32[8,128]{1,0:T(8,128)S(1)}) custom-call(bf16[640,1024]{1,0:T(8,128)(2,1)S(1)} %get-tuple-element.61.refs_0_, bf16[256,1024]{1,0:T(8,128)(2,1)S(1)} %get-tuple-element.63.refs_1_, bf16[128,1024]{1,0:T(8,128)(2,1)S(1)} %get-tuple-element.65.refs_2_, ...), custom_call_target="tpu_custom_call" | custom-call | flops 1610612736 | bytes 5242880 | tf_op jit(solution)/shard_map/pallas_call | solution.py:59
  47.3 4.5 %collective-permute-start.10 = (bf16[128,768]{1,0:T(8,128)(2,1)S(1)}, bf16[128,768]{1,0:T(8,128)(2,1)S(1)}, u32[]{:S(2)}, u32[]{:S(2)}) collective-permute-start(bf16[128,768]{1,0:T(8,128)(2,1)S(1)} %shard_map.106), channel_id=1, source_target_pairs={{0,112},{16,32},{32,16},{48,64},{64,48},{80,96},{96,80},{112,0},{1... | collective-permute-start | bytes 589832 | tf_op jit(solution)/shard_map/ppermute | solution.py:467
  51.9 4.8 %all-to-all-start.1 = ((bf16[8,128,768]{2,1,0:T(8,128)(2,1)}), bf16[8,128,768]{2,1,0:T(8,128)(2,1)}, u32[]{:S(2)}, u32[]{:S(2)}) async-start(bf16[8,128,768]{2,1,0:T(8,128)(2,1)} %bitcast.29), calls=%async_computation.1 | async-start | bytes 3145728 | tf_op jit(solution)/shard_map/all_to_all | solution.py:508
  57.0 2.5 %collective-permute-start.13 = (bf16[128,768]{1,0:T(8,128)(2,1)S(1)}, bf16[128,768]{1,0:T(8,128)(2,1)S(1)}, u32[]{:S(2)}, u32[]{:S(2)}) collective-permute-start(bf16[128,768]{1,0:T(8,128)(2,1)S(1)} %get-tuple-element.77), channel_id=1, source_target_pairs={{0,112},{16,32},{32,16},{48,64},{64,48},{80,96},{96,80},{112,0},{1... | collective-permute-start | bytes 589832 | tf_op jit(solution)/shard_map/ppermute | solution.py:467
  60.1 2.6 %collective-permute-done.12.refs_2_ = bf16[128,768]{1,0:T(8,128)(2,1)S(1)} collective-permute-done((bf16[128,768]{1,0:T(8,128)(2,1)S(1)}, bf16[128,768]{1,0:T(8,128)(2,1)S(1)}, u32[]{:S(2)}, u32[]{:S(2)}) %collective-permute-start.12) | collective-permute-done | bytes 196640 | tf_op jit(solution)/shard_map/ppermute | solution.py:467
  62.6 1.4 %collective-permute-done.13.refs_3_ = bf16[128,768]{1,0:T(8,128)(2,1)S(1)} collective-permute-done((bf16[128,768]{1,0:T(8,128)(2,1)S(1)}, bf16[128,768]{1,0:T(8,128)(2,1)S(1)}, u32[]{:S(2)}, u32[]{:S(2)}) %collective-permute-start.13) | collective-permute-done | bytes 196640 | tf_op jit(solution)/shard_map/ppermute | solution.py:467
  64.1 3.8 %collective-permute-start.14 = (bf16[128,768]{1,0:T(8,128)(2,1)S(1)}, bf16[128,768]{1,0:T(8,128)(2,1)S(1)}, u32[]{:S(2)}, u32[]{:S(2)}) collective-permute-start(bf16[128,768]{1,0:T(8,128)(2,1)S(1)} %get-tuple-element.78), channel_id=1, source_target_pairs={{0,112},{16,32},{32,16},{48,64},{64,48},{80,96},{96,80},{112,0},{1... | collective-permute-start | bytes 589832 | tf_op jit(solution)/shard_map/ppermute | solution.py:467
  68.7 1.8 %shard_map.100.xt_ref = bf16[1536,512]{1,0:T(8,128)(2,1)S(1)} custom-call(bf16[128,1536]{1,0:T(8,128)(2,1)} %bitcast.24, bf16[128,1536]{1,0:T(8,128)(2,1)} %bitcast.27, bf16[128,1536]{1,0:T(8,128)(2,1)} %copy-done.13, bf16[128,1536]{1,0:T(8,128)(2,1)} %collective-permute-done.1.refs_3_), custom_call_target="tpu_custom_call" | custom-call | flops 786432 | bytes 3145728 | tf_op jit(solution)/shard_map/pallas_call | solution.py:59
  71.6 2.0 %collective-permute-done.15.qb_ref = bf16[128,768]{1,0:T(8,128)(2,1)S(1)} collective-permute-done((bf16[128,768]{1,0:T(8,128)(2,1)S(1)}, bf16[128,768]{1,0:T(8,128)(2,1)S(1)}, u32[]{:S(2)}, u32[]{:S(2)}) %collective-permute-start.15) | collective-permute-done | bytes 196640 | tf_op jit(solution)/shard_map/ppermute | solution.py:467
  74.2 2.7 %shard_map.109 = (bf16[128,768]{1,0:T(8,128)(2,1)S(1)}, bf16[128,768]{1,0:T(8,128)(2,1)S(1)}, bf16[256,384]{1,0:T(8,128)(2,1)S(1)}, bf16[256,384]{1,0:T(8,128)(2,1)S(1)}) custom-call(f32[1,2]{1,0:T(1,128)S(1)} %maximum_bitcast_fusion.scal_ref, f32[128,768]{1,0:T(8,128)} %get-tuple-element.55.ui_hbm, f32[128,128]{1,0:T(8,128)} %get-tuple-element.56.ni_hbm, ...), custom_call_target="tpu_custom_call" | custom-call | flops 1966080 | bytes 2949120 | tf_op jit(solution)/shard_map/pallas_call | solution.py:59
  77.1 1.4 %collective-permute-done.16.got_ref = bf16[256,384]{1,0:T(8,128)(2,1)S(1)} collective-permute-done((bf16[256,384]{1,0:T(8,128)(2,1)S(1)}, bf16[256,384]{1,0:T(8,128)(2,1)S(1)}, u32[]{:S(2)}, u32[]{:S(2)}) %collective-permute-start.16) | collective-permute-done | bytes 196640 | tf_op jit(solution)/shard_map/ppermute | solution.py:461
  78.4 1.9 %shard_map.110 = bf16[8,208,384]{2,1,0:T(8,128)(2,1)} custom-call(bf16[1536,512]{1,0:T(8,128)(2,1)S(1)} %shard_map.100.xt_ref, bf16[256,384]{1,0:T(8,128)(2,1)S(1)} %get-tuple-element.80.keep_ref, bf16[256,384]{1,0:T(8,128)(2,1)S(1)} %collective-permute-done.16.got_ref, bf16[16,384]{1,0:T(8,128)(2,1)S(1)} %maximum_maximum_fusion.extra_ref), custom_call_target="tpu_custom_call" | custom-call | flops 603979776 | bytes 2752512 | tf_op jit(solution)/shard_map/pallas_call | solution.py:59
  80.3 4.6 %all-to-all-start.2 = ((bf16[8,208,384]{2,1,0:T(8,128)(2,1)}), bf16[8,208,384]{2,1,0:T(8,128)(2,1)}, u32[]{:S(2)}, u32[]{:S(2)}) async-start(bf16[8,208,384]{2,1,0:T(8,128)(2,1)} %shard_map.110), calls=%async_computation.2 | async-start | bytes 2555904 | tf_op jit(solution)/shard_map/all_to_all | solution.py:522
  84.9 2.4 %shard_map.111 = (bf16[128,1536]{1,0:T(8,128)(2,1)}, bf16[128,1536]{1,0:T(8,128)(2,1)}, f32[8,128]{1,0:T(8,128)S(1)}) custom-call(bf16[128,768]{1,0:T(8,128)(2,1)S(1)} %get-tuple-element.83.di_ref, bf16[128,768]{1,0:T(8,128)(2,1)S(1)} %get-tuple-element.84.dt_ref, bf16[1536,768]{1,0:T(8,128)(2,1)S(1)} %copy-done), custom_call_target="tpu_custom_call" | custom-call | flops 603979776 | bytes 3932160 | tf_op jit(solution)/shard_map/pallas_call | solution.py:59
  87.3 15.3 %all-to-all-done.2.parts_hbm = bf16[8,208,384]{2,1,0:T(8,128)(2,1)} async-done(((bf16[8,208,384]{2,1,0:T(8,128)(2,1)}), bf16[8,208,384]{2,1,0:T(8,128)(2,1)}, u32[]{:S(2)}, u32[]{:S(2)}) %all-to-all-start.2) | async-done | bytes 1277984 | tf_op jit(solution)/shard_map/all_to_all | solution.py:522
  102.6 1.5 %shard_map.112 = bf16[8,32,384]{2,1,0:T(8,128)(2,1)S(1)} custom-call(bf16[8,208,384]{2,1,0:T(8,128)(2,1)} %all-to-all-done.2.parts_hbm, f32[8,128]{1,0:T(8,128)S(1)} %get-tuple-element.85._), custom_call_target="tpu_custom_call" | custom-call | flops 6389760 | bytes 1277952 | tf_op jit(solution)/shard_map/pallas_call | solution.py:59
  104.1 14.0 %all_to_all.32 = bf16[8,32,384]{2,1,0:T(8,128)(2,1)S(1)} all-to-all(bf16[8,32,384]{2,1,0:T(8,128)(2,1)S(1)} %shard_map.112), channel_id=1, replica_groups=mesh['xl'=2,'z'=8,'y'=4,'xh'=2,'c'=2] {'z'}, dimensions={0} | all-to-all | bytes 393216 | tf_op jit(solution)/shard_map/all_to_all | solution.py:523
  119.0 4.8 %collective-permute-done.17.r_ref = f32[32,384]{1,0:T(8,128)S(1)} collective-permute-done((f32[32,384]{1,0:T(8,128)S(1)}, f32[32,384]{1,0:T(8,128)S(1)}, u32[]{:S(2)}, u32[]{:S(2)}) %collective-permute-start.17) | collective-permute-done | bytes 49184 | tf_op jit(solution)/shard_map/ppermute | solution.py:461
  123.9 1.2 collective-permute-done.18.o_ref
  (67 shorter events, 7.8 us)
Async XLA Ops:
  4.5 28.2 %all-to-all-start = ((bf16[8,128,768]{2,1,0:T(8,128)(2,1)}), bf16[8,128,768]{2,1,0:T(8,128)(2,1)S(1)}, u32[]{:S(2)}, u32[]{:S(2)}) async-start(bf16[8,128,768]{2,1,0:T(8,128)(2,1)} %bitcast.30), calls=%async_computation | async-start | bytes 3145728 | tf_op jit(solution)/shard_map/all_to_all | solution.py:493
  9.6 10.5 %collective-permute-start.3 = (bf16[128,768]{1,0:T(8,128)(2,1)S(1)}, bf16[128,768]{1,0:T(8,128)(2,1)S(1)}, u32[]{:S(2)}, u32[]{:S(2)}) collective-permute-start(bf16[128,768]{1,0:T(8,128)(2,1)S(1)} %get-tuple-element.60.refs_0_.refs_3_), channel_id=1, source_target_pairs={{0,112},{16,32},{32,16},{48,64},{64,48},{80,96},{96,80},{112,0},{1... | collective-permute-start | bytes 589832 | tf_op jit(solution)/shard_map/ppermute | solution.py:467
  15.4 6.1 %collective-permute-start.2 = (bf16[128,768]{1,0:T(8,128)(2,1)S(1)}, bf16[128,768]{1,0:T(8,128)(2,1)S(1)}, u32[]{:S(2)}, u32[]{:S(2)}) collective-permute-start(bf16[128,768]{1,0:T(8,128)(2,1)S(1)} %get-tuple-element.60.refs_0_.refs_3_), channel_id=1, source_target_pairs={{0,16},{16,0},{32,48},{48,32},{64,80},{80,64},{96,112},{112,96},{1... | collective-permute-start | bytes 589832 | tf_op jit(solution)/shard_map/ppermute | solution.py:467
  20.0 5.8 %collective-permute-start.4 = (bf16[128,768]{1,0:T(8,128)(2,1)S(1)}, bf16[128,768]{1,0:T(8,128)(2,1)S(1)}, u32[]{:S(2)}, u32[]{:S(2)}) collective-permute-start(bf16[128,768]{1,0:T(8,128)(2,1)S(1)} %collective-permute-done.3.refs_2_.refs_5_), channel_id=1, source_target_pairs={{0,16},{16,0},{32,48},{48,32},{64,80},{80,64},{96,112},{112,96},{1... | collective-permute-start | bytes 589832 | tf_op jit(solution)/shard_map/ppermute | solution.py:467
  21.5 8.5 %collective-permute-start.5 = (bf16[128,768]{1,0:T(8,128)(2,1)S(1)}, bf16[128,768]{1,0:T(8,128)(2,1)S(1)}, u32[]{:S(2)}, u32[]{:S(2)}) collective-permute-start(bf16[128,768]{1,0:T(8,128)(2,1)S(1)} %collective-permute-done.2.refs_1_.refs_4_), channel_id=1, source_target_pairs={{0,112},{16,32},{32,16},{48,64},{64,48},{80,96},{96,80},{112,0},{1... | collective-permute-start | bytes 589832 | tf_op jit(solution)/shard_map/ppermute | solution.py:467
  25.8 6.9 %collective-permute-start.7 = (bf16[128,768]{1,0:T(8,128)(2,1)S(1)}, bf16[128,768]{1,0:T(8,128)(2,1)S(1)}, u32[]{:S(2)}, u32[]{:S(2)}) collective-permute-start(bf16[128,768]{1,0:T(8,128)(2,1)S(1)} %collective-permute-done.4.refs_3_.refs_6_), channel_id=1, source_target_pairs={{0,112},{16,32},{32,16},{48,64},{64,48},{80,96},{96,80},{112,0},{1... | collective-permute-start | bytes 589832 | tf_op jit(solution)/shard_map/ppermute | solution.py:467
  30.0 7.1 %collective-permute-start.6 = (bf16[128,768]{1,0:T(8,128)(2,1)S(1)}, bf16[128,768]{1,0:T(8,128)(2,1)S(1)}, u32[]{:S(2)}, u32[]{:S(2)}) collective-permute-start(bf16[128,768]{1,0:T(8,128)(2,1)S(1)} %collective-permute-done.5.refs_4_.refs_7_), channel_id=1, source_target_pairs={{0,16},{16,0},{32,48},{48,32},{64,80},{80,64},{96,112},{112,96},{1... | collective-permute-start | bytes 589832 | tf_op jit(solution)/shard_map/ppermute | solution.py:467
  32.7 7.0 %collective-permute-start.8 = (bf16[128,768]{1,0:T(8,128)(2,1)S(1)}, bf16[128,768]{1,0:T(8,128)(2,1)S(1)}, u32[]{:S(2)}, u32[]{:S(2)}) collective-permute-start(bf16[128,768]{1,0:T(8,128)(2,1)S(1)} %collective-permute-done.7.refs_2_.refs_9_), channel_id=1, source_target_pairs={{0,16},{16,0},{32,48},{48,32},{64,80},{80,64},{96,112},{112,96},{1... | collective-permute-start | bytes 589832 | tf_op jit(solution)/shard_map/ppermute | solution.py:467
  36.4 4.8 %copy-start.3 = (bf16[128,768]{1,0:T(8,128)(2,1)}, bf16[128,768]{1,0:T(8,128)(2,1)S(1)}, u32[]{:S(2)}) copy-start(bf16[128,768]{1,0:T(8,128)(2,1)S(1)} %get-tuple-element.69.refs_1_) | copy-start | bytes 589828
  36.4 4.8 %copy-start.5 = (bf16[128,768]{1,0:T(8,128)(2,1)}, bf16[128,768]{1,0:T(8,128)(2,1)S(1)}, u32[]{:S(2)}) copy-start(bf16[128,768]{1,0:T(8,128)(2,1)S(1)} %get-tuple-element.68.refs_0_) | copy-start | bytes 589828
  36.4 4.8 %copy-start.7 = (bf16[128,768]{1,0:T(8,128)(2,1)}, bf16[128,768]{1,0:T(8,128)(2,1)S(1)}, u32[]{:S(2)}) copy-start(bf16[128,768]{1,0:T(8,128)(2,1)S(1)} %get-tuple-element.70.refs_0_) | copy-start | bytes 589828
  36.5 4.8 %copy-start.9 = (bf16[128,768]{1,0:T(8,128)(2,1)}, bf16[128,768]{1,0:T(8,128)(2,1)S(1)}, u32[]{:S(2)}) copy-start(bf16[128,768]{1,0:T(8,128)(2,1)S(1)} %get-tuple-element.71.refs_1_) | copy-start | bytes 589828
  39.6 3.7 %copy-start.2 = (bf16[128,768]{1,0:T(8,128)(2,1)S(1)}, bf16[128,768]{1,0:T(8,128)(2,1)}, u32[]{:S(2)}) copy-start(bf16[128,768]{1,0:T(8,128)(2,1)} %copy-done.1) | copy-start | bytes 589828
  41.3 6.0 %collective-permute-start.9 = (bf16[128,768]{1,0:T(8,128)(2,1)S(1)}, bf16[128,768]{1,0:T(8,128)(2,1)S(1)}, u32[]{:S(2)}, u32[]{:S(2)}) collective-permute-start(bf16[128,768]{1,0:T(8,128)(2,1)S(1)} %get-tuple-element.73), channel_id=1, source_target_pairs={{0,16},{16,0},{32,48},{48,32},{64,80},{80,64},{96,112},{112,96},{1... | collective-permute-start | bytes 589832 | tf_op jit(solution)/shard_map/ppermute | solution.py:467
  42.7 14.0 %collective-permute-start.11 = (bf16[128,768]{1,0:T(8,128)(2,1)}, bf16[128,768]{1,0:T(8,128)(2,1)S(1)}, u32[]{:S(2)}, u32[]{:S(2)}) collective-permute-start(bf16[128,768]{1,0:T(8,128)(2,1)} %get-tuple-element.75), channel_id=1, source_target_pairs={{0,16},{16,0},{32,48},{48,32},{64,80},{80,64},{96,112},{112,96},{1... | collective-permute-start | bytes 589832 | tf_op jit(solution)/shard_map/ppermute | solution.py:467
  47.3 9.4 %collective-permute-start.10 = (bf16[128,768]{1,0:T(8,128)(2,1)S(1)}, bf16[128,768]{1,0:T(8,128)(2,1)S(1)}, u32[]{:S(2)}, u32[]{:S(2)}) collective-permute-start(bf16[128,768]{1,0:T(8,128)(2,1)S(1)} %shard_map.106), channel_id=1, source_target_pairs={{0,112},{16,32},{32,16},{48,64},{64,48},{80,96},{96,80},{112,0},{1... | collective-permute-start | bytes 589832 | tf_op jit(solution)/shard_map/ppermute | solution.py:467
  51.8 4.9 %copy-start.8 = (bf16[128,768]{1,0:T(8,128)(2,1)S(1)}, bf16[128,768]{1,0:T(8,128)(2,1)}, u32[]{:S(2)}) copy-start(bf16[128,768]{1,0:T(8,128)(2,1)} %copy-done.7) | copy-start | bytes 589828
  51.9 4.9 %copy-start.10 = (bf16[128,768]{1,0:T(8,128)(2,1)S(1)}, bf16[128,768]{1,0:T(8,128)(2,1)}, u32[]{:S(2)}) copy-start(bf16[128,768]{1,0:T(8,128)(2,1)} %copy-done.9) | copy-start | bytes 589828
  51.9 22.4 %all-to-all-start.1 = ((bf16[8,128,768]{2,1,0:T(8,128)(2,1)}), bf16[8,128,768]{2,1,0:T(8,128)(2,1)}, u32[]{:S(2)}, u32[]{:S(2)}) async-start(bf16[8,128,768]{2,1,0:T(8,128)(2,1)} %bitcast.29), calls=%async_computation.1 | async-start | bytes 3145728 | tf_op jit(solution)/shard_map/all_to_all | solution.py:508
  56.7 7.3 %copy-start.4 = (bf16[128,768]{1,0:T(8,128)(2,1)S(1)}, bf16[128,768]{1,0:T(8,128)(2,1)}, u32[]{:S(2)}) copy-start(bf16[128,768]{1,0:T(8,128)(2,1)} %copy-done.3) | copy-start | bytes 589828
  56.8 7.3 %copy-start.6 = (bf16[128,768]{1,0:T(8,128)(2,1)S(1)}, bf16[128,768]{1,0:T(8,128)(2,1)}, u32[]{:S(2)}) copy-start(bf16[128,768]{1,0:T(8,128)(2,1)} %copy-done.5) | copy-start | bytes 589828
  56.9 5.8 %collective-permute-start.12 = (bf16[128,768]{1,0:T(8,128)(2,1)S(1)}, bf16[128,768]{1,0:T(8,128)(2,1)S(1)}, u32[]{:S(2)}, u32[]{:S(2)}) collective-permute-start(bf16[128,768]{1,0:T(8,128)(2,1)S(1)} %get-tuple-element.76), channel_id=1, source_target_pairs={{0,16},{16,0},{32,48},{48,32},{64,80},{80,64},{96,112},{112,96},{1... | collective-permute-start | bytes 589832 | tf_op jit(solution)/shard_map/ppermute | solution.py:467
  57.0 7.1 %collective-permute-start.13 = (bf16[128,768]{1,0:T(8,128)(2,1)S(1)}, bf16[128,768]{1,0:T(8,128)(2,1)S(1)}, u32[]{:S(2)}, u32[]{:S(2)}) collective-permute-start(bf16[128,768]{1,0:T(8,128)(2,1)S(1)} %get-tuple-element.77), channel_id=1, source_target_pairs={{0,112},{16,32},{32,16},{48,64},{64,48},{80,96},{96,80},{112,0},{1... | collective-permute-start | bytes 589832 | tf_op jit(solution)/shard_map/ppermute | solution.py:467
  59.5 8.5 %collective-permute-start = (bf16[128,1536]{1,0:T(8,128)(2,1)S(1)}, bf16[128,1536]{1,0:T(8,128)(2,1)S(1)}, u32[]{:S(2)}, u32[]{:S(2)}) collective-permute-start(bf16[128,1536]{1,0:T(8,128)(2,1)S(1)} %bitcast.25), channel_id=1, source_target_pairs={{0,1},{1,0},{2,3},{3,2},{4,5},{5,4},{6,7},{7,6},{8,9},{9,8},{10,11... | collective-permute-start | bytes 1179656 | tf_op jit(solution)/shard_map/ppermute | solution.py:461
  59.5 9.3 %collective-permute-start.1 = (bf16[128,1536]{1,0:T(8,128)(2,1)S(1)}, bf16[128,1536]{1,0:T(8,128)(2,1)}, u32[]{:S(2)}, u32[]{:S(2)}) collective-permute-start(bf16[128,1536]{1,0:T(8,128)(2,1)S(1)} %bitcast.28), channel_id=1, source_target_pairs={{0,1},{1,0},{2,3},{3,2},{4,5},{5,4},{6,7},{7,6},{8,9},{9,8},{10,11... | collective-permute-start | bytes 1179656 | tf_op jit(solution)/shard_map/ppermute | solution.py:461
  64.1 7.4 %collective-permute-start.14 = (bf16[128,768]{1,0:T(8,128)(2,1)S(1)}, bf16[128,768]{1,0:T(8,128)(2,1)S(1)}, u32[]{:S(2)}, u32[]{:S(2)}) collective-permute-start(bf16[128,768]{1,0:T(8,128)(2,1)S(1)} %get-tuple-element.78), channel_id=1, source_target_pairs={{0,112},{16,32},{32,16},{48,64},{64,48},{80,96},{96,80},{112,0},{1... | collective-permute-start | bytes 589832 | tf_op jit(solution)/shard_map/ppermute | solution.py:467
  67.9 5.7 %collective-permute-start.15 = (bf16[128,768]{1,0:T(8,128)(2,1)S(1)}, bf16[128,768]{1,0:T(8,128)(2,1)S(1)}, u32[]{:S(2)}, u32[]{:S(2)}) collective-permute-start(bf16[128,768]{1,0:T(8,128)(2,1)S(1)} %get-tuple-element.79), channel_id=1, source_target_pairs={{0,16},{16,0},{32,48},{48,32},{64,80},{80,64},{96,112},{112,96},{1... | collective-permute-start | bytes 589832 | tf_op jit(solution)/shard_map/ppermute | solution.py:467
  76.9 1.5 %collective-permute-start.16 = (bf16[256,384]{1,0:T(8,128)(2,1)S(1)}, bf16[256,384]{1,0:T(8,128)(2,1)S(1)}, u32[]{:S(2)}, u32[]{:S(2)}) collective-permute-start(bf16[256,384]{1,0:T(8,128)(2,1)S(1)} %get-tuple-element.81), channel_id=1, source_target_pairs={{0,1},{1,0},{2,3},{3,2},{4,5},{5,4},{6,7},{7,6},{8,9},{9,8},{10,11... | collective-permute-start | bytes 589832 | tf_op jit(solution)/shard_map/ppermute | solution.py:461
  80.3 4.6 %copy-start = (bf16[1536,768]{1,0:T(8,128)(2,1)S(1)}, bf16[1536,768]{1,0:T(8,128)(2,1)}, u32[]{:S(2)}) copy-start(bf16[1536,768]{1,0:T(8,128)(2,1)} %head_ref.1) | copy-start | bytes 7077892
  80.3 22.3 %all-to-all-start.2 = ((bf16[8,208,384]{2,1,0:T(8,128)(2,1)}), bf16[8,208,384]{2,1,0:T(8,128)(2,1)}, u32[]{:S(2)}, u32[]{:S(2)}) async-start(bf16[8,208,384]{2,1,0:T(8,128)(2,1)} %shard_map.110), calls=%async_computation.2 | async-start | bytes 2555904 | tf_op jit(solution)/shard_map/all_to_all | solution.py:522
  118.1 5.7 %collective-permute-start.17 = (f32[32,384]{1,0:T(8,128)S(1)}, f32[32,384]{1,0:T(8,128)S(1)}, u32[]{:S(2)}, u32[]{:S(2)}) collective-permute-start(f32[32,384]{1,0:T(8,128)S(1)} %convert_reduce_fusion.s_ref), channel_id=1, source_target_pairs={{0,2},{2,0},{1,3},{3,1},{4,6},{6,4},{5,7},{7,5},{8,10},{10,8},{9,1... | collective-permute-start | bytes 147464 | tf_op jit(solution)/shard_map/ppermute | solution.py:461
  123.8 1.3 %collective-permute-start.18 = (f32[32,384]{1,0:T(8,128)S(1)}, f32[32,384]{1,0:T(8,128)S(1)}, u32[]{:S(2)}, u32[]{:S(2)}) collective-permute-start(f32[32,384]{1,0:T(8,128)S(1)} %add.11), channel_id=1, source_target_pairs={{0,1},{1,0},{2,3},{3,2},{4,5},{5,4},{6,7},{7,6},{8,9},{9,8},{10,11... | collective-permute-start | bytes 147464 | tf_op jit(solution)/shard_map/ppermute | solution.py:461
  (4 other events, 8.7 us)

commit v5 on v4

--- a/solution.py
+++ b/solution.py
@@ -369,15 +369,25 @@
     )(*data)
 
 
-def head_grad_kernel(xt_ref, keep_ref, got_ref, extra_ref, out_hbm, d_all, out_v, out_sem):
-    d_all[: 2 * R] = keep_ref[...]
-    d_all[2 * R :] = got_ref[...]
+def own_head_kernel(xt_ref, keep_ref, out_ref):
+    out_ref[...] = dot(xt_ref[:, : 2 * R], keep_ref[...], NN)
+
+
+def own_head(xt, keep):
+    return vmem_call(
+        own_head_kernel, jax.ShapeDtypeStruct((D, H), F32), specs=[VP, VM], out_specs=VP,
+        flops=4 * R * D * H, nbytes=4 * R * D + 4 * D * H,
+    )(xt, keep)
+
+
+def head_grad_kernel(xt_ref, own_ref, got_ref, extra_ref, out_hbm, out_v, out_sem):
     for j in range(8):
         out_v[j, 8 * ZROWS :] = extra_ref[...]
-    d = d_all[...]
+    d = got_ref[...]
     put = []
     for xl in range(2):
-        full = dot(xt_ref[xl * E : (xl + 1) * E], d, NN)
+        rows = slice(xl * E, (xl + 1) * E)
+        full = own_ref[rows] + dot(xt_ref[rows, 2 * R :], d, NN)
         for y in range(4):
             for z in range(0, 8, 2):
                 a = (z * 4 + y) * ZROWS
@@ -391,17 +401,13 @@
         c.wait()
 
 
-def head_grad_parts(xt, keep, got, extra):
+def head_grad_parts(xt, own, got, extra):
     shape = (8, 8 * ZROWS + PAD, H)
     return vmem_call(
         head_grad_kernel, jax.ShapeDtypeStruct(shape, BF16),
-        scratch=(
-            pltpu.VMEM((4 * R, H), BF16),
-            pltpu.VMEM(shape, BF16),
-            pltpu.SemaphoreType.DMA((2,)),
-        ),
-        specs=[VP] + [VM] * 3, out_specs=HB, flops=8 * R * D * H, nbytes=2 * (4 * R * D + D * H),
-    )(xt, keep, got, extra)
+        scratch=(pltpu.VMEM(shape, BF16), pltpu.SemaphoreType.DMA((2,))),
+        specs=[VP, VP, VM, VM], out_specs=HB, flops=4 * R * D * H, nbytes=2 * (4 * R * D + D * H),
+    )(xt, own, got, extra)
 
 
 def sum_kernel(parts_hbm, _, out_ref, parts_v, sem):
@@ -518,7 +524,7 @@
     got = cc(send)
     gi, gt, done = input_grad(di, dt, head)
 
-    parts = head_grad_parts(xt, keep, got, extra)
+    parts = head_grad_parts(xt, own_head(xt, keep), got, extra)
     parts = lax.all_to_all(parts, ("xl", "y"), 0, 0, tiled=True)
     parts = lax.all_to_all(sum_parts(parts, done), "z", 0, 0, tiled=True)
     s = jnp.sum(parts.astype(F32), axis=0)

time: 128 us -> 128 us (level)
    pallas_call x14 -> x15, Pallas kernels: 26.6 us -> 26.8 us  [call(): pl.pallas_call(kernel, out_shape=jax.tree.map(place_out, out_shape, out_s...]
  transfers between devices with their start and end apart: 22 -> 22, of which waited for: 15 -> 15; matrix products, arithmetic and copies ran while one was open for 0% -> 0% of each run, Pallas kernels for 11% -> 12%
where the time goes in v5:
time: 128 us; the launch traced here: 126 us
  waiting for transfers between devices  42.1 us (33%)
  starting transfers between devices  39.5 us (31%)
  Pallas kernels  26.8 us (21%)
  blocking collectives  14 us (11%)
  between operations  2.28 us (2%)
    pallas_call x15, Pallas kernels, call(): pl.pallas_call(kernel, out_shape=jax.tree.map(place_out, out_shape, out_s...  26.8 us
    ppermute x6, starting transfers between devices, ring(): lax.ppermute(v, axis, odd)  21 us
    all_to_all x1, waiting for transfers between devices, per_device(): parts = lax.all_to_all(parts, ('xl', 'y'), 0, 0, tiled=True)  15.3 us
    all_to_all x1, blocking collectives, per_device(): parts = lax.all_to_all(sum_parts(parts, done), 'z', 0, 0, tiled=True)  14 us
    ppermute x8, waiting for transfers between devices, ring(): lax.ppermute(v, axis, even)  10 us
    ppermute x6, waiting for transfers between devices, ring(): lax.ppermute(v, axis, odd)  9.34 us
    ppermute x5, waiting for transfers between devices, swap(): return lambda v: lax.ppermute(v, axis, [(0, 1), (1, 0)])  6.81 us
    all_to_all x1, starting transfers between devices, per_device(): vs = lax.all_to_all(v, near, 0, 0, tiled=True)  5.11 us
  transfers between devices with their start and end apart: 22, of which 15 were waited for; matrix products, arithmetic and copies ran while one was open for 0% of the time, Pallas kernels for 12%

profile of v5, /device:TPU:4, one launch (start us, length us, event | category | flops | bytes accessed | tf_op | source)
XLA Modules:
  0.0 125.9 jit_solution(15716732666974721804)
XLA Ops:
  0.6 3.8 %shard_map.101 = (bf16[128,768]{1,0:T(8,128)(2,1)S(1)}, bf16[1024,768]{1,0:T(8,128)(2,1)}, f32[128,768]{1,0:T(8,128)}, f32[128,128]{1,0:T(8,128)}, f32[128,768]{1,0:T(8,128)}, /*index=5*/f32[128,128]{1,0:T(8,128)}) custom-call(bf16[128,1536]{1,0:T(8,128)(2,1)} %bitcast.23, bf16[128,1536]{1,0:T(8,128)(2,1)} %bitcast.26, bf16[1536,768]{1,0:T(8,128)(2,1)} %head_ref.1), custom_call_target="tpu_custom_call" | custom-call | flops 603979776 | bytes 3145728 | tf_op jit(solution)/shard_map/pallas_call | solution.py:59
  4.5 5.1 %all-to-all-start = ((bf16[8,128,768]{2,1,0:T(8,128)(2,1)}), bf16[8,128,768]{2,1,0:T(8,128)(2,1)S(1)}, u32[]{:S(2)}, u32[]{:S(2)}) async-start(bf16[8,128,768]{2,1,0:T(8,128)(2,1)} %bitcast.30), calls=%async_computation | async-start | bytes 3145728 | tf_op jit(solution)/shard_map/all_to_all | solution.py:499
  9.6 5.9 %collective-permute-start.3 = (bf16[128,768]{1,0:T(8,128)(2,1)S(1)}, bf16[128,768]{1,0:T(8,128)(2,1)S(1)}, u32[]{:S(2)}, u32[]{:S(2)}) collective-permute-start(bf16[128,768]{1,0:T(8,128)(2,1)S(1)} %get-tuple-element.60.refs_0_.refs_3_), channel_id=1, source_target_pairs={{0,112},{16,32},{32,16},{48,64},{64,48},{80,96},{96,80},{112,0},{1... | collective-permute-start | bytes 589832 | tf_op jit(solution)/shard_map/ppermute | solution.py:473
  15.4 4.6 %collective-permute-done.3.refs_2_.refs_5_ = bf16[128,768]{1,0:T(8,128)(2,1)S(1)} collective-permute-done((bf16[128,768]{1,0:T(8,128)(2,1)S(1)}, bf16[128,768]{1,0:T(8,128)(2,1)S(1)}, u32[]{:S(2)}, u32[]{:S(2)}) %collective-permute-start.3) | collective-permute-done | bytes 196640 | tf_op jit(solution)/shard_map/ppermute | solution.py:473
  20.0 1.5 %collective-permute-done.2.refs_1_.refs_4_ = bf16[128,768]{1,0:T(8,128)(2,1)S(1)} collective-permute-done((bf16[128,768]{1,0:T(8,128)(2,1)S(1)}, bf16[128,768]{1,0:T(8,128)(2,1)S(1)}, u32[]{:S(2)}, u32[]{:S(2)}) %collective-permute-start.2) | collective-permute-done | bytes 196640 | tf_op jit(solution)/shard_map/ppermute | solution.py:473
  21.5 1.5 %collective-permute-start.5 = (bf16[128,768]{1,0:T(8,128)(2,1)S(1)}, bf16[128,768]{1,0:T(8,128)(2,1)S(1)}, u32[]{:S(2)}, u32[]{:S(2)}) collective-permute-start(bf16[128,768]{1,0:T(8,128)(2,1)S(1)} %collective-permute-done.2.refs_1_.refs_4_), channel_id=1, source_target_pairs={{0,112},{16,32},{32,16},{48,64},{64,48},{80,96},{96,80},{112,0},{1... | collective-permute-start | bytes 589832 | tf_op jit(solution)/shard_map/ppermute | solution.py:473
  23.0 2.8 %collective-permute-done.4.refs_3_.refs_6_ = bf16[128,768]{1,0:T(8,128)(2,1)S(1)} collective-permute-done((bf16[128,768]{1,0:T(8,128)(2,1)S(1)}, bf16[128,768]{1,0:T(8,128)(2,1)S(1)}, u32[]{:S(2)}, u32[]{:S(2)}) %collective-permute-start.4) | collective-permute-done | bytes 196640 | tf_op jit(solution)/shard_map/ppermute | solution.py:473
  25.8 2.9 %collective-permute-start.7 = (bf16[128,768]{1,0:T(8,128)(2,1)S(1)}, bf16[128,768]{1,0:T(8,128)(2,1)S(1)}, u32[]{:S(2)}, u32[]{:S(2)}) collective-permute-start(bf16[128,768]{1,0:T(8,128)(2,1)S(1)} %collective-permute-done.4.refs_3_.refs_6_), channel_id=1, source_target_pairs={{0,112},{16,32},{32,16},{48,64},{64,48},{80,96},{96,80},{112,0},{1... | collective-permute-start | bytes 589832 | tf_op jit(solution)/shard_map/ppermute | solution.py:473
  30.2 2.5 %collective-permute-done.7.refs_2_.refs_9_ = bf16[128,768]{1,0:T(8,128)(2,1)S(1)} collective-permute-done((bf16[128,768]{1,0:T(8,128)(2,1)S(1)}, bf16[128,768]{1,0:T(8,128)(2,1)S(1)}, u32[]{:S(2)}, u32[]{:S(2)}) %collective-permute-start.7) | collective-permute-done | bytes 196640 | tf_op jit(solution)/shard_map/ppermute | solution.py:473
  32.7 3.7 %shard_map.102 = (bf16[128,768]{1,0:T(8,128)(2,1)S(1)}, bf16[128,768]{1,0:T(8,128)(2,1)S(1)}, bf16[128,768]{1,0:T(8,128)(2,1)S(1)}, bf16[128,768]{1,0:T(8,128)(2...) custom-call(f32[1,2]{1,0:T(1,128)S(1)} %maximum_bitcast_fusion.1.scal_ref, ...), custom_call_target="tpu_custom_call" | custom-call | flops 2013265920 | bytes 5111808 | tf_op jit(solution)/shard_map/pallas_call | solution.py:59
  37.1 2.5 %shard_map.103 = (bf16[128,768]{1,0:T(8,128)(2,1)}, bf16[128,768]{1,0:T(8,128)(2,1)S(1)}, bf16[256,1024]{1,0:T(8,128)(2,1)S(1)}, f32[3,8,256]{2,1,0:T(8,128)S(1)}) custom-call(f32[1,2]{1,0:T(1,128)S(1)} %maximum_bitcast_fusion.1.scal_ref, s32[1,1]{1,0:T(1,128)} %bitcast.8.at_ref, bf16[1024,768]{1,0:T(8,128)(2,1)S(1)} %bitcast.21, ...), custom_call_target="tpu_custom_call" | custom-call | flops 805306368 | bytes 3932160 | tf_op jit(solution)/shard_map/pallas_call | solution.py:59
  39.7 1.6 %shard_map.104 = (bf16[128,768]{1,0:T(8,128)(2,1)S(1)}, bf16[128,1024]{1,0:T(8,128)(2,1)S(1)}, f32[3,8,256]{2,1,0:T(8,128)S(1)}) custom-call(f32[1,2]{1,0:T(1,128)S(1)} %maximum_bitcast_fusion.1.scal_ref, s32[1,1]{1,0:T(1,128)} %bitcast.8.at_ref, bf16[1024,768]{1,0:T(8,128)(2,1)S(1)} %bitcast.22, f32[3,8,256]{2,1,0:T(8,128)S(1)} %get-tuple-element.64.refs_0_, ...), custom_call_target="tpu_custom_call" | custom-call | flops 402653184 | bytes 3538944 | tf_op jit(solution)/shard_map/pallas_call | solution.py:59
  41.3 1.5 %collective-permute-start.9 = (bf16[128,768]{1,0:T(8,128)(2,1)S(1)}, bf16[128,768]{1,0:T(8,128)(2,1)S(1)}, u32[]{:S(2)}, u32[]{:S(2)}) collective-permute-start(bf16[128,768]{1,0:T(8,128)(2,1)S(1)} %get-tuple-element.73), channel_id=1, source_target_pairs={{0,16},{16,0},{32,48},{48,32},{64,80},{80,64},{96,112},{112,96},{1... | collective-permute-start | bytes 589832 | tf_op jit(solution)/shard_map/ppermute | solution.py:473
  43.4 3.3 %shard_map.105 = (bf16[1024,768]{1,0:T(8,128)(2,1)}, f32[8,128]{1,0:T(8,128)S(1)}) custom-call(bf16[640,1024]{1,0:T(8,128)(2,1)S(1)} %get-tuple-element.61.refs_0_, bf16[256,1024]{1,0:T(8,128)(2,1)S(1)} %get-tuple-element.63.refs_1_, bf16[128,1024]{1,0:T(8,128)(2,1)S(1)} %get-tuple-element.65.refs_2_, ...), custom_call_target="tpu_custom_call" | custom-call | flops 1610612736 | bytes 5242880 | tf_op jit(solution)/shard_map/pallas_call | solution.py:59
  47.3 4.5 %collective-permute-start.10 = (bf16[128,768]{1,0:T(8,128)(2,1)S(1)}, bf16[128,768]{1,0:T(8,128)(2,1)S(1)}, u32[]{:S(2)}, u32[]{:S(2)}) collective-permute-start(bf16[128,768]{1,0:T(8,128)(2,1)S(1)} %shard_map.106), channel_id=1, source_target_pairs={{0,112},{16,32},{32,16},{48,64},{64,48},{80,96},{96,80},{112,0},{1... | collective-permute-start | bytes 589832 | tf_op jit(solution)/shard_map/ppermute | solution.py:473
  51.9 4.8 %all-to-all-start.1 = ((bf16[8,128,768]{2,1,0:T(8,128)(2,1)}), bf16[8,128,768]{2,1,0:T(8,128)(2,1)}, u32[]{:S(2)}, u32[]{:S(2)}) async-start(bf16[8,128,768]{2,1,0:T(8,128)(2,1)} %bitcast.29), calls=%async_computation.1 | async-start | bytes 3145728 | tf_op jit(solution)/shard_map/all_to_all | solution.py:514
  57.0 2.5 %collective-permute-start.13 = (bf16[128,768]{1,0:T(8,128)(2,1)S(1)}, bf16[128,768]{1,0:T(8,128)(2,1)S(1)}, u32[]{:S(2)}, u32[]{:S(2)}) collective-permute-start(bf16[128,768]{1,0:T(8,128)(2,1)S(1)} %get-tuple-element.77), channel_id=1, source_target_pairs={{0,112},{16,32},{32,16},{48,64},{64,48},{80,96},{96,80},{112,0},{1... | collective-permute-start | bytes 589832 | tf_op jit(solution)/shard_map/ppermute | solution.py:473
  60.1 2.6 %collective-permute-done.12.refs_2_ = bf16[128,768]{1,0:T(8,128)(2,1)S(1)} collective-permute-done((bf16[128,768]{1,0:T(8,128)(2,1)S(1)}, bf16[128,768]{1,0:T(8,128)(2,1)S(1)}, u32[]{:S(2)}, u32[]{:S(2)}) %collective-permute-start.12) | collective-permute-done | bytes 196640 | tf_op jit(solution)/shard_map/ppermute | solution.py:473
  62.6 1.4 %collective-permute-done.13.refs_3_ = bf16[128,768]{1,0:T(8,128)(2,1)S(1)} collective-permute-done((bf16[128,768]{1,0:T(8,128)(2,1)S(1)}, bf16[128,768]{1,0:T(8,128)(2,1)S(1)}, u32[]{:S(2)}, u32[]{:S(2)}) %collective-permute-start.13) | collective-permute-done | bytes 196640 | tf_op jit(solution)/shard_map/ppermute | solution.py:473
  64.1 3.8 %collective-permute-start.14 = (bf16[128,768]{1,0:T(8,128)(2,1)S(1)}, bf16[128,768]{1,0:T(8,128)(2,1)S(1)}, u32[]{:S(2)}, u32[]{:S(2)}) collective-permute-start(bf16[128,768]{1,0:T(8,128)(2,1)S(1)} %get-tuple-element.78), channel_id=1, source_target_pairs={{0,112},{16,32},{32,16},{48,64},{64,48},{80,96},{96,80},{112,0},{1... | collective-permute-start | bytes 589832 | tf_op jit(solution)/shard_map/ppermute | solution.py:473
  68.7 1.8 %shard_map.100.xt_ref = bf16[1536,512]{1,0:T(8,128)(2,1)S(1)} custom-call(bf16[128,1536]{1,0:T(8,128)(2,1)} %bitcast.24, bf16[128,1536]{1,0:T(8,128)(2,1)} %bitcast.27, bf16[128,1536]{1,0:T(8,128)(2,1)} %copy-done.13, bf16[128,1536]{1,0:T(8,128)(2,1)} %collective-permute-done.1.refs_3_), custom_call_target="tpu_custom_call" | custom-call | flops 786432 | bytes 3145728 | tf_op jit(solution)/shard_map/pallas_call | solution.py:59
  71.6 2.0 %collective-permute-done.15.qb_ref = bf16[128,768]{1,0:T(8,128)(2,1)S(1)} collective-permute-done((bf16[128,768]{1,0:T(8,128)(2,1)S(1)}, bf16[128,768]{1,0:T(8,128)(2,1)S(1)}, u32[]{:S(2)}, u32[]{:S(2)}) %collective-permute-start.15) | collective-permute-done | bytes 196640 | tf_op jit(solution)/shard_map/ppermute | solution.py:473
  74.2 2.7 %shard_map.109 = (bf16[128,768]{1,0:T(8,128)(2,1)S(1)}, bf16[128,768]{1,0:T(8,128)(2,1)S(1)}, bf16[256,384]{1,0:T(8,128)(2,1)S(1)}, bf16[256,384]{1,0:T(8,128)(2,1)S(1)}) custom-call(f32[1,2]{1,0:T(1,128)S(1)} %maximum_bitcast_fusion.scal_ref, f32[128,768]{1,0:T(8,128)} %get-tuple-element.55.ui_hbm, f32[128,128]{1,0:T(8,128)} %get-tuple-element.56.ni_hbm, ...), custom_call_target="tpu_custom_call" | custom-call | flops 1966080 | bytes 2949120 | tf_op jit(solution)/shard_map/pallas_call | solution.py:59
  78.4 1.5 %shard_map.111 = bf16[8,208,384]{2,1,0:T(8,128)(2,1)} custom-call(bf16[1536,512]{1,0:T(8,128)(2,1)S(1)} %shard_map.100.xt_ref, f32[1536,384]{1,0:T(8,128)S(1)} %shard_map.110.own_ref, bf16[256,384]{1,0:T(8,128)(2,1)S(1)} %collective-permute-done.16.got_ref, bf16[16,384]{1,0:T(8,128)(2,1)S(1)} %maximum_maximum_fusion.extra_ref), custom_call_target="tpu_custom_call" | custom-call | flops 301989888 | bytes 2752512 | tf_op jit(solution)/shard_map/pallas_call | solution.py:59
  79.9 4.6 %all-to-all-start.2 = ((bf16[8,208,384]{2,1,0:T(8,128)(2,1)}), bf16[8,208,384]{2,1,0:T(8,128)(2,1)}, u32[]{:S(2)}, u32[]{:S(2)}) async-start(bf16[8,208,384]{2,1,0:T(8,128)(2,1)} %shard_map.111), calls=%async_computation.2 | async-start | bytes 2555904 | tf_op jit(solution)/shard_map/all_to_all | solution.py:528
  84.5 2.4 %shard_map.112 = (bf16[128,1536]{1,0:T(8,128)(2,1)}, bf16[128,1536]{1,0:T(8,128)(2,1)}, f32[8,128]{1,0:T(8,128)S(1)}) custom-call(bf16[128,768]{1,0:T(8,128)(2,1)S(1)} %get-tuple-element.83.di_ref, bf16[128,768]{1,0:T(8,128)(2,1)S(1)} %get-tuple-element.84.dt_ref, bf16[1536,768]{1,0:T(8,128)(2,1)S(1)} %copy-done), custom_call_target="tpu_custom_call" | custom-call | flops 603979776 | bytes 3932160 | tf_op jit(solution)/shard_map/pallas_call | solution.py:59
  86.9 15.3 %all-to-all-done.2.parts_hbm = bf16[8,208,384]{2,1,0:T(8,128)(2,1)} async-done(((bf16[8,208,384]{2,1,0:T(8,128)(2,1)}), bf16[8,208,384]{2,1,0:T(8,128)(2,1)}, u32[]{:S(2)}, u32[]{:S(2)}) %all-to-all-start.2) | async-done | bytes 1277984 | tf_op jit(solution)/shard_map/all_to_all | solution.py:528
  102.2 1.5 %shard_map.113 = bf16[8,32,384]{2,1,0:T(8,128)(2,1)S(1)} custom-call(bf16[8,208,384]{2,1,0:T(8,128)(2,1)} %all-to-all-done.2.parts_hbm, f32[8,128]{1,0:T(8,128)S(1)} %get-tuple-element.85._), custom_call_target="tpu_custom_call" | custom-call | flops 6389760 | bytes 1277952 | tf_op jit(solution)/shard_map/pallas_call | solution.py:59
  103.7 14.0 %all_to_all.32 = bf16[8,32,384]{2,1,0:T(8,128)(2,1)S(1)} all-to-all(bf16[8,32,384]{2,1,0:T(8,128)(2,1)S(1)} %shard_map.113), channel_id=1, replica_groups=mesh['xl'=2,'z'=8,'y'=4,'xh'=2,'c'=2] {'z'}, dimensions={0} | all-to-all | bytes 393216 | tf_op jit(solution)/shard_map/all_to_all | solution.py:529
  118.6 4.8 %collective-permute-done.17.r_ref = f32[32,384]{1,0:T(8,128)S(1)} collective-permute-done((f32[32,384]{1,0:T(8,128)S(1)}, f32[32,384]{1,0:T(8,128)S(1)}, u32[]{:S(2)}, u32[]{:S(2)}) %collective-permute-start.17) | collective-permute-done | bytes 49184 | tf_op jit(solution)/shard_map/ppermute | solution.py:467
  123.5 1.2 collective-permute-done.18.o_ref
  124.7 1.2 shard_map.114
  (68 shorter events, 7.9 us)
Async XLA Ops:
  4.5 28.2 %all-to-all-start = ((bf16[8,128,768]{2,1,0:T(8,128)(2,1)}), bf16[8,128,768]{2,1,0:T(8,128)(2,1)S(1)}, u32[]{:S(2)}, u32[]{:S(2)}) async-start(bf16[8,128,768]{2,1,0:T(8,128)(2,1)} %bitcast.30), calls=%async_computation | async-start | bytes 3145728 | tf_op jit(solution)/shard_map/all_to_all | solution.py:499
  9.6 10.5 %collective-permute-start.3 = (bf16[128,768]{1,0:T(8,128)(2,1)S(1)}, bf16[128,768]{1,0:T(8,128)(2,1)S(1)}, u32[]{:S(2)}, u32[]{:S(2)}) collective-permute-start(bf16[128,768]{1,0:T(8,128)(2,1)S(1)} %get-tuple-element.60.refs_0_.refs_3_), channel_id=1, source_target_pairs={{0,112},{16,32},{32,16},{48,64},{64,48},{80,96},{96,80},{112,0},{1... | collective-permute-start | bytes 589832 | tf_op jit(solution)/shard_map/ppermute | solution.py:473
  15.4 6.1 %collective-permute-start.2 = (bf16[128,768]{1,0:T(8,128)(2,1)S(1)}, bf16[128,768]{1,0:T(8,128)(2,1)S(1)}, u32[]{:S(2)}, u32[]{:S(2)}) collective-permute-start(bf16[128,768]{1,0:T(8,128)(2,1)S(1)} %get-tuple-element.60.refs_0_.refs_3_), channel_id=1, source_target_pairs={{0,16},{16,0},{32,48},{48,32},{64,80},{80,64},{96,112},{112,96},{1... | collective-permute-start | bytes 589832 | tf_op jit(solution)/shard_map/ppermute | solution.py:473
  20.0 5.8 %collective-permute-start.4 = (bf16[128,768]{1,0:T(8,128)(2,1)S(1)}, bf16[128,768]{1,0:T(8,128)(2,1)S(1)}, u32[]{:S(2)}, u32[]{:S(2)}) collective-permute-start(bf16[128,768]{1,0:T(8,128)(2,1)S(1)} %collective-permute-done.3.refs_2_.refs_5_), channel_id=1, source_target_pairs={{0,16},{16,0},{32,48},{48,32},{64,80},{80,64},{96,112},{112,96},{1... | collective-permute-start | bytes 589832 | tf_op jit(solution)/shard_map/ppermute | solution.py:473
  21.5 8.5 %collective-permute-start.5 = (bf16[128,768]{1,0:T(8,128)(2,1)S(1)}, bf16[128,768]{1,0:T(8,128)(2,1)S(1)}, u32[]{:S(2)}, u32[]{:S(2)}) collective-permute-start(bf16[128,768]{1,0:T(8,128)(2,1)S(1)} %collective-permute-done.2.refs_1_.refs_4_), channel_id=1, source_target_pairs={{0,112},{16,32},{32,16},{48,64},{64,48},{80,96},{96,80},{112,0},{1... | collective-permute-start | bytes 589832 | tf_op jit(solution)/shard_map/ppermute | solution.py:473
  25.8 6.9 %collective-permute-start.7 = (bf16[128,768]{1,0:T(8,128)(2,1)S(1)}, bf16[128,768]{1,0:T(8,128)(2,1)S(1)}, u32[]{:S(2)}, u32[]{:S(2)}) collective-permute-start(bf16[128,768]{1,0:T(8,128)(2,1)S(1)} %collective-permute-done.4.refs_3_.refs_6_), channel_id=1, source_target_pairs={{0,112},{16,32},{32,16},{48,64},{64,48},{80,96},{96,80},{112,0},{1... | collective-permute-start | bytes 589832 | tf_op jit(solution)/shard_map/ppermute | solution.py:473
  30.0 7.1 %collective-permute-start.6 = (bf16[128,768]{1,0:T(8,128)(2,1)S(1)}, bf16[128,768]{1,0:T(8,128)(2,1)S(1)}, u32[]{:S(2)}, u32[]{:S(2)}) collective-permute-start(bf16[128,768]{1,0:T(8,128)(2,1)S(1)} %collective-permute-done.5.refs_4_.refs_7_), channel_id=1, source_target_pairs={{0,16},{16,0},{32,48},{48,32},{64,80},{80,64},{96,112},{112,96},{1... | collective-permute-start | bytes 589832 | tf_op jit(solution)/shard_map/ppermute | solution.py:473
  32.7 7.0 %collective-permute-start.8 = (bf16[128,768]{1,0:T(8,128)(2,1)S(1)}, bf16[128,768]{1,0:T(8,128)(2,1)S(1)}, u32[]{:S(2)}, u32[]{:S(2)}) collective-permute-start(bf16[128,768]{1,0:T(8,128)(2,1)S(1)} %collective-permute-done.7.refs_2_.refs_9_), channel_id=1, source_target_pairs={{0,16},{16,0},{32,48},{48,32},{64,80},{80,64},{96,112},{112,96},{1... | collective-permute-start | bytes 589832 | tf_op jit(solution)/shard_map/ppermute | solution.py:473
  36.4 4.8 %copy-start.3 = (bf16[128,768]{1,0:T(8,128)(2,1)}, bf16[128,768]{1,0:T(8,128)(2,1)S(1)}, u32[]{:S(2)}) copy-start(bf16[128,768]{1,0:T(8,128)(2,1)S(1)} %get-tuple-element.69.refs_1_) | copy-start | bytes 589828
  36.4 4.8 %copy-start.5 = (bf16[128,768]{1,0:T(8,128)(2,1)}, bf16[128,768]{1,0:T(8,128)(2,1)S(1)}, u32[]{:S(2)}) copy-start(bf16[128,768]{1,0:T(8,128)(2,1)S(1)} %get-tuple-element.68.refs_0_) | copy-start | bytes 589828
  36.4 4.8 %copy-start.7 = (bf16[128,768]{1,0:T(8,128)(2,1)}, bf16[128,768]{1,0:T(8,128)(2,1)S(1)}, u32[]{:S(2)}) copy-start(bf16[128,768]{1,0:T(8,128)(2,1)S(1)} %get-tuple-element.70.refs_0_) | copy-start | bytes 589828
  36.5 4.8 %copy-start.9 = (bf16[128,768]{1,0:T(8,128)(2,1)}, bf16[128,768]{1,0:T(8,128)(2,1)S(1)}, u32[]{:S(2)}) copy-start(bf16[128,768]{1,0:T(8,128)(2,1)S(1)} %get-tuple-element.71.refs_1_) | copy-start | bytes 589828
  39.6 3.7 %copy-start.2 = (bf16[128,768]{1,0:T(8,128)(2,1)S(1)}, bf16[128,768]{1,0:T(8,128)(2,1)}, u32[]{:S(2)}) copy-start(bf16[128,768]{1,0:T(8,128)(2,1)} %copy-done.1) | copy-start | bytes 589828
  41.3 6.0 %collective-permute-start.9 = (bf16[128,768]{1,0:T(8,128)(2,1)S(1)}, bf16[128,768]{1,0:T(8,128)(2,1)S(1)}, u32[]{:S(2)}, u32[]{:S(2)}) collective-permute-start(bf16[128,768]{1,0:T(8,128)(2,1)S(1)} %get-tuple-element.73), channel_id=1, source_target_pairs={{0,16},{16,0},{32,48},{48,32},{64,80},{80,64},{96,112},{112,96},{1... | collective-permute-start | bytes 589832 | tf_op jit(solution)/shard_map/ppermute | solution.py:473
  42.7 14.0 %collective-permute-start.11 = (bf16[128,768]{1,0:T(8,128)(2,1)}, bf16[128,768]{1,0:T(8,128)(2,1)S(1)}, u32[]{:S(2)}, u32[]{:S(2)}) collective-permute-start(bf16[128,768]{1,0:T(8,128)(2,1)} %get-tuple-element.75), channel_id=1, source_target_pairs={{0,16},{16,0},{32,48},{48,32},{64,80},{80,64},{96,112},{112,96},{1... | collective-permute-start | bytes 589832 | tf_op jit(solution)/shard_map/ppermute | solution.py:473
  47.3 9.4 %collective-permute-start.10 = (bf16[128,768]{1,0:T(8,128)(2,1)S(1)}, bf16[128,768]{1,0:T(8,128)(2,1)S(1)}, u32[]{:S(2)}, u32[]{:S(2)}) collective-permute-start(bf16[128,768]{1,0:T(8,128)(2,1)S(1)} %shard_map.106), channel_id=1, source_target_pairs={{0,112},{16,32},{32,16},{48,64},{64,48},{80,96},{96,80},{112,0},{1... | collective-permute-start | bytes 589832 | tf_op jit(solution)/shard_map/ppermute | solution.py:473
  51.8 4.9 %copy-start.8 = (bf16[128,768]{1,0:T(8,128)(2,1)S(1)}, bf16[128,768]{1,0:T(8,128)(2,1)}, u32[]{:S(2)}) copy-start(bf16[128,768]{1,0:T(8,128)(2,1)} %copy-done.7) | copy-start | bytes 589828
  51.9 4.9 %copy-start.10 = (bf16[128,768]{1,0:T(8,128)(2,1)S(1)}, bf16[128,768]{1,0:T(8,128)(2,1)}, u32[]{:S(2)}) copy-start(bf16[128,768]{1,0:T(8,128)(2,1)} %copy-done.9) | copy-start | bytes 589828
  51.9 22.4 %all-to-all-start.1 = ((bf16[8,128,768]{2,1,0:T(8,128)(2,1)}), bf16[8,128,768]{2,1,0:T(8,128)(2,1)}, u32[]{:S(2)}, u32[]{:S(2)}) async-start(bf16[8,128,768]{2,1,0:T(8,128)(2,1)} %bitcast.29), calls=%async_computation.1 | async-start | bytes 3145728 | tf_op jit(solution)/shard_map/all_to_all | solution.py:514
  56.7 7.3 %copy-start.4 = (bf16[128,768]{1,0:T(8,128)(2,1)S(1)}, bf16[128,768]{1,0:T(8,128)(2,1)}, u32[]{:S(2)}) copy-start(bf16[128,768]{1,0:T(8,128)(2,1)} %copy-done.3) | copy-start | bytes 589828
  56.8 7.3 %copy-start.6 = (bf16[128,768]{1,0:T(8,128)(2,1)S(1)}, bf16[128,768]{1,0:T(8,128)(2,1)}, u32[]{:S(2)}) copy-start(bf16[128,768]{1,0:T(8,128)(2,1)} %copy-done.5) | copy-start | bytes 589828
  56.9 5.8 %collective-permute-start.12 = (bf16[128,768]{1,0:T(8,128)(2,1)S(1)}, bf16[128,768]{1,0:T(8,128)(2,1)S(1)}, u32[]{:S(2)}, u32[]{:S(2)}) collective-permute-start(bf16[128,768]{1,0:T(8,128)(2,1)S(1)} %get-tuple-element.76), channel_id=1, source_target_pairs={{0,16},{16,0},{32,48},{48,32},{64,80},{80,64},{96,112},{112,96},{1... | collective-permute-start | bytes 589832 | tf_op jit(solution)/shard_map/ppermute | solution.py:473
  57.0 7.1 %collective-permute-start.13 = (bf16[128,768]{1,0:T(8,128)(2,1)S(1)}, bf16[128,768]{1,0:T(8,128)(2,1)S(1)}, u32[]{:S(2)}, u32[]{:S(2)}) collective-permute-start(bf16[128,768]{1,0:T(8,128)(2,1)S(1)} %get-tuple-element.77), channel_id=1, source_target_pairs={{0,112},{16,32},{32,16},{48,64},{64,48},{80,96},{96,80},{112,0},{1... | collective-permute-start | bytes 589832 | tf_op jit(solution)/shard_map/ppermute | solution.py:473
  59.5 8.5 %collective-permute-start = (bf16[128,1536]{1,0:T(8,128)(2,1)S(1)}, bf16[128,1536]{1,0:T(8,128)(2,1)S(1)}, u32[]{:S(2)}, u32[]{:S(2)}) collective-permute-start(bf16[128,1536]{1,0:T(8,128)(2,1)S(1)} %bitcast.25), channel_id=1, source_target_pairs={{0,1},{1,0},{2,3},{3,2},{4,5},{5,4},{6,7},{7,6},{8,9},{9,8},{10,11... | collective-permute-start | bytes 1179656 | tf_op jit(solution)/shard_map/ppermute | solution.py:467
  59.5 9.3 %collective-permute-start.1 = (bf16[128,1536]{1,0:T(8,128)(2,1)S(1)}, bf16[128,1536]{1,0:T(8,128)(2,1)}, u32[]{:S(2)}, u32[]{:S(2)}) collective-permute-start(bf16[128,1536]{1,0:T(8,128)(2,1)S(1)} %bitcast.28), channel_id=1, source_target_pairs={{0,1},{1,0},{2,3},{3,2},{4,5},{5,4},{6,7},{7,6},{8,9},{9,8},{10,11... | collective-permute-start | bytes 1179656 | tf_op jit(solution)/shard_map/ppermute | solution.py:467
  64.1 7.4 %collective-permute-start.14 = (bf16[128,768]{1,0:T(8,128)(2,1)S(1)}, bf16[128,768]{1,0:T(8,128)(2,1)S(1)}, u32[]{:S(2)}, u32[]{:S(2)}) collective-permute-start(bf16[128,768]{1,0:T(8,128)(2,1)S(1)} %get-tuple-element.78), channel_id=1, source_target_pairs={{0,112},{16,32},{32,16},{48,64},{64,48},{80,96},{96,80},{112,0},{1... | collective-permute-start | bytes 589832 | tf_op jit(solution)/shard_map/ppermute | solution.py:473
  67.9 5.7 %collective-permute-start.15 = (bf16[128,768]{1,0:T(8,128)(2,1)S(1)}, bf16[128,768]{1,0:T(8,128)(2,1)S(1)}, u32[]{:S(2)}, u32[]{:S(2)}) collective-permute-start(bf16[128,768]{1,0:T(8,128)(2,1)S(1)} %get-tuple-element.79), channel_id=1, source_target_pairs={{0,16},{16,0},{32,48},{48,32},{64,80},{80,64},{96,112},{112,96},{1... | collective-permute-start | bytes 589832 | tf_op jit(solution)/shard_map/ppermute | solution.py:473
  76.9 1.5 %collective-permute-start.16 = (bf16[256,384]{1,0:T(8,128)(2,1)S(1)}, bf16[256,384]{1,0:T(8,128)(2,1)S(1)}, u32[]{:S(2)}, u32[]{:S(2)}) collective-permute-start(bf16[256,384]{1,0:T(8,128)(2,1)S(1)} %get-tuple-element.81), channel_id=1, source_target_pairs={{0,1},{1,0},{2,3},{3,2},{4,5},{5,4},{6,7},{7,6},{8,9},{9,8},{10,11... | collective-permute-start | bytes 589832 | tf_op jit(solution)/shard_map/ppermute | solution.py:467
  79.9 4.6 %copy-start = (bf16[1536,768]{1,0:T(8,128)(2,1)S(1)}, bf16[1536,768]{1,0:T(8,128)(2,1)}, u32[]{:S(2)}) copy-start(bf16[1536,768]{1,0:T(8,128)(2,1)} %head_ref.1) | copy-start | bytes 7077892
  79.9 22.3 %all-to-all-start.2 = ((bf16[8,208,384]{2,1,0:T(8,128)(2,1)}), bf16[8,208,384]{2,1,0:T(8,128)(2,1)}, u32[]{:S(2)}, u32[]{:S(2)}) async-start(bf16[8,208,384]{2,1,0:T(8,128)(2,1)} %shard_map.111), calls=%async_computation.2 | async-start | bytes 2555904 | tf_op jit(solution)/shard_map/all_to_all | solution.py:528
  117.7 5.7 %collective-permute-start.17 = (f32[32,384]{1,0:T(8,128)S(1)}, f32[32,384]{1,0:T(8,128)S(1)}, u32[]{:S(2)}, u32[]{:S(2)}) collective-permute-start(f32[32,384]{1,0:T(8,128)S(1)} %convert_reduce_fusion.s_ref), channel_id=1, source_target_pairs={{0,2},{2,0},{1,3},{3,1},{4,6},{6,4},{5,7},{7,5},{8,10},{10,8},{9,1... | collective-permute-start | bytes 147464 | tf_op jit(solution)/shard_map/ppermute | solution.py:467
  123.4 1.3 %collective-permute-start.18 = (f32[32,384]{1,0:T(8,128)S(1)}, f32[32,384]{1,0:T(8,128)S(1)}, u32[]{:S(2)}, u32[]{:S(2)}) collective-permute-start(f32[32,384]{1,0:T(8,128)S(1)} %add.11), channel_id=1, source_target_pairs={{0,1},{1,0},{2,3},{3,2},{4,5},{5,4},{6,7},{7,6},{8,9},{9,8},{10,11... | collective-permute-start | bytes 147464 | tf_op jit(solution)/shard_map/ppermute | solution.py:467
  (4 other events, 8.7 us)

commit v6 on v5

--- a/solution.py
+++ b/solution.py
@@ -69,24 +69,23 @@
     return call
 
 
-PARTS = 3
+PARTS = 6
 
 
 def proj_kernel(
     x_hbm, y_hbm, head_hbm, u_ref, v_hbm, ui_hbm, ni_hbm, ut_hbm, nt_hbm,
-    x_v, y_v, head_v, unit_v, norm_v, low_v, in_sem, out_sem,
+    xy_v, head_v, unit_v, norm_v, low_v, in_sem, out_sem,
 ):
     deep = D // PARTS
-    get_x = pltpu.make_async_copy(x_hbm, x_v, in_sem.at[PARTS])
-    get_y = pltpu.make_async_copy(y_hbm, y_v, in_sem.at[PARTS + 1])
     get = [
+        pltpu.make_async_copy(y_hbm, xy_v.at[pl.ds(0, R)], in_sem.at[PARTS]),
+        pltpu.make_async_copy(x_hbm, xy_v.at[pl.ds(R, R)], in_sem.at[PARTS + 1]),
+    ] + [
         pltpu.make_async_copy(head_hbm.at[pl.ds(k * deep, deep)], head_v.at[pl.ds(k * deep, deep)], in_sem.at[k])
         for k in range(PARTS)
     ]
-    get_y.start()
     for c in get:
         c.start()
-    get_x.start()
     put = []
 
     def send(src, dst):
@@ -102,17 +101,17 @@
         send(norm_v.at[k], norm_hbm)
         return unit.astype(BF16)
 
-    get_y.wait()
+    get[0].wait()
+    get[1].wait()
     proj = None
-    for k, c in enumerate(get):
-        c.wait()
-        part = dot(y_v[:, k * deep : (k + 1) * deep], head_v[k * deep : (k + 1) * deep], NN)
+    for k in range(PARTS):
+        get[2 + k].wait()
+        part = dot(xy_v[:, k * deep : (k + 1) * deep], head_v[k * deep : (k + 1) * deep], NN)
         proj = part if proj is None else proj + part
-    low_v[...] = finish(0, proj, ut_hbm, nt_hbm)
+    low_v[...] = finish(0, proj[:R], ut_hbm, nt_hbm)
     for k in range(8):
         send(low_v, v_hbm.at[pl.ds(k * R, R)])
-    get_x.wait()
-    u_ref[...] = finish(1, dot(x_v[...], head_v[...], NN), ui_hbm, ni_hbm)
+    u_ref[...] = finish(1, proj[R:], ui_hbm, ni_hbm)
     for c in put:
         c.wait()
 
@@ -124,8 +123,7 @@
         proj_kernel,
         (jax.ShapeDtypeStruct((R, E), BF16), jax.ShapeDtypeStruct((8 * R, E), BF16), unit, norm, unit, norm),
         scratch=(
-            pltpu.VMEM((R, D), BF16),
-            pltpu.VMEM((R, D), BF16),
+            pltpu.VMEM((2 * R, D), BF16),
             pltpu.VMEM((D, E), BF16),
             pltpu.VMEM((2, R, E), F32),
             pltpu.VMEM((2, R, 128), F32),

time: 128 us -> 128 us (level)
  no operation moved by 1% of the time
where the time goes in v6:
time: 128 us; the launch traced here: 126 us
  waiting for transfers between devices  42.1 us (33%)
  starting transfers between devices  39.5 us (31%)
  Pallas kernels  27.2 us (21%)
  blocking collectives  14 us (11%)
  between operations  2.28 us (2%)
    pallas_call x15, Pallas kernels, call(): pl.pallas_call(kernel, out_shape=jax.tree.map(place_out, out_shape, out_s...  27.2 us
    ppermute x6, starting transfers between devices, ring(): lax.ppermute(v, axis, odd)  21 us
    all_to_all x1, waiting for transfers between devices, per_device(): parts = lax.all_to_all(parts, ('xl', 'y'), 0, 0, tiled=True)  15.3 us
    all_to_all x1, blocking collectives, per_device(): parts = lax.all_to_all(sum_parts(parts, done), 'z', 0, 0, tiled=True)  14 us
    ppermute x8, waiting for transfers between devices, ring(): lax.ppermute(v, axis, even)  10 us
    ppermute x6, waiting for transfers between devices, ring(): lax.ppermute(v, axis, odd)  9.31 us
    ppermute x5, waiting for transfers between devices, swap(): return lambda v: lax.ppermute(v, axis, [(0, 1), (1, 0)])  6.77 us
    all_to_all x1, starting transfers between devices, per_device(): vs = lax.all_to_all(v, near, 0, 0, tiled=True)  5.11 us
  transfers between devices with their start and end apart: 22, of which 15 were waited for; matrix products, arithmetic and copies ran while one was open for 0% of the time, Pallas kernels for 12%

profile of v6, /device:TPU:4, one launch (start us, length us, event | category | flops | bytes accessed | tf_op | source)
XLA Modules:
  0.0 126.4 jit_solution(7362659740374306276)
XLA Ops:
  0.6 4.3 %shard_map.101 = (bf16[128,768]{1,0:T(8,128)(2,1)S(1)}, bf16[1024,768]{1,0:T(8,128)(2,1)}, f32[128,768]{1,0:T(8,128)}, f32[128,128]{1,0:T(8,128)}, f32[128,768]{1,0:T(8,128)}, /*index=5*/f32[128,128]{1,0:T(8,128)}) custom-call(bf16[128,1536]{1,0:T(8,128)(2,1)} %bitcast.23, bf16[128,1536]{1,0:T(8,128)(2,1)} %bitcast.26, bf16[1536,768]{1,0:T(8,128)(2,1)} %head_ref.1), custom_call_target="tpu_custom_call" | custom-call | flops 603979776 | bytes 3145728 | tf_op jit(solution)/shard_map/pallas_call | solution.py:59
  4.9 5.1 %all-to-all-start = ((bf16[8,128,768]{2,1,0:T(8,128)(2,1)}), bf16[8,128,768]{2,1,0:T(8,128)(2,1)S(1)}, u32[]{:S(2)}, u32[]{:S(2)}) async-start(bf16[8,128,768]{2,1,0:T(8,128)(2,1)} %bitcast.30), calls=%async_computation | async-start | bytes 3145728 | tf_op jit(solution)/shard_map/all_to_all | solution.py:497
  10.0 5.9 %collective-permute-start.3 = (bf16[128,768]{1,0:T(8,128)(2,1)S(1)}, bf16[128,768]{1,0:T(8,128)(2,1)S(1)}, u32[]{:S(2)}, u32[]{:S(2)}) collective-permute-start(bf16[128,768]{1,0:T(8,128)(2,1)S(1)} %get-tuple-element.60.refs_0_.refs_3_), channel_id=1, source_target_pairs={{0,112},{16,32},{32,16},{48,64},{64,48},{80,96},{96,80},{112,0},{1... | collective-permute-start | bytes 589832 | tf_op jit(solution)/shard_map/ppermute | solution.py:471
  15.9 4.6 %collective-permute-done.3.refs_2_.refs_5_ = bf16[128,768]{1,0:T(8,128)(2,1)S(1)} collective-permute-done((bf16[128,768]{1,0:T(8,128)(2,1)S(1)}, bf16[128,768]{1,0:T(8,128)(2,1)S(1)}, u32[]{:S(2)}, u32[]{:S(2)}) %collective-permute-start.3) | collective-permute-done | bytes 196640 | tf_op jit(solution)/shard_map/ppermute | solution.py:471
  20.5 1.5 %collective-permute-done.2.refs_1_.refs_4_ = bf16[128,768]{1,0:T(8,128)(2,1)S(1)} collective-permute-done((bf16[128,768]{1,0:T(8,128)(2,1)S(1)}, bf16[128,768]{1,0:T(8,128)(2,1)S(1)}, u32[]{:S(2)}, u32[]{:S(2)}) %collective-permute-start.2) | collective-permute-done | bytes 196640 | tf_op jit(solution)/shard_map/ppermute | solution.py:471
  22.0 1.5 %collective-permute-start.5 = (bf16[128,768]{1,0:T(8,128)(2,1)S(1)}, bf16[128,768]{1,0:T(8,128)(2,1)S(1)}, u32[]{:S(2)}, u32[]{:S(2)}) collective-permute-start(bf16[128,768]{1,0:T(8,128)(2,1)S(1)} %collective-permute-done.2.refs_1_.refs_4_), channel_id=1, source_target_pairs={{0,112},{16,32},{32,16},{48,64},{64,48},{80,96},{96,80},{112,0},{1... | collective-permute-start | bytes 589832 | tf_op jit(solution)/shard_map/ppermute | solution.py:471
  23.5 2.8 %collective-permute-done.4.refs_3_.refs_6_ = bf16[128,768]{1,0:T(8,128)(2,1)S(1)} collective-permute-done((bf16[128,768]{1,0:T(8,128)(2,1)S(1)}, bf16[128,768]{1,0:T(8,128)(2,1)S(1)}, u32[]{:S(2)}, u32[]{:S(2)}) %collective-permute-start.4) | collective-permute-done | bytes 196640 | tf_op jit(solution)/shard_map/ppermute | solution.py:471
  26.3 2.9 %collective-permute-start.7 = (bf16[128,768]{1,0:T(8,128)(2,1)S(1)}, bf16[128,768]{1,0:T(8,128)(2,1)S(1)}, u32[]{:S(2)}, u32[]{:S(2)}) collective-permute-start(bf16[128,768]{1,0:T(8,128)(2,1)S(1)} %collective-permute-done.4.refs_3_.refs_6_), channel_id=1, source_target_pairs={{0,112},{16,32},{32,16},{48,64},{64,48},{80,96},{96,80},{112,0},{1... | collective-permute-start | bytes 589832 | tf_op jit(solution)/shard_map/ppermute | solution.py:471
  30.6 2.5 %collective-permute-done.7.refs_2_.refs_9_ = bf16[128,768]{1,0:T(8,128)(2,1)S(1)} collective-permute-done((bf16[128,768]{1,0:T(8,128)(2,1)S(1)}, bf16[128,768]{1,0:T(8,128)(2,1)S(1)}, u32[]{:S(2)}, u32[]{:S(2)}) %collective-permute-start.7) | collective-permute-done | bytes 196640 | tf_op jit(solution)/shard_map/ppermute | solution.py:471
  33.1 3.7 %shard_map.102 = (bf16[128,768]{1,0:T(8,128)(2,1)S(1)}, bf16[128,768]{1,0:T(8,128)(2,1)S(1)}, bf16[128,768]{1,0:T(8,128)(2,1)S(1)}, bf16[128,768]{1,0:T(8,128)(2...) custom-call(f32[1,2]{1,0:T(1,128)S(1)} %maximum_bitcast_fusion.1.scal_ref, ...), custom_call_target="tpu_custom_call" | custom-call | flops 2013265920 | bytes 5111808 | tf_op jit(solution)/shard_map/pallas_call | solution.py:59
  37.6 2.5 %shard_map.103 = (bf16[128,768]{1,0:T(8,128)(2,1)}, bf16[128,768]{1,0:T(8,128)(2,1)S(1)}, bf16[256,1024]{1,0:T(8,128)(2,1)S(1)}, f32[3,8,256]{2,1,0:T(8,128)S(1)}) custom-call(f32[1,2]{1,0:T(1,128)S(1)} %maximum_bitcast_fusion.1.scal_ref, s32[1,1]{1,0:T(1,128)} %bitcast.8.at_ref, bf16[1024,768]{1,0:T(8,128)(2,1)S(1)} %bitcast.21, ...), custom_call_target="tpu_custom_call" | custom-call | flops 805306368 | bytes 3932160 | tf_op jit(solution)/shard_map/pallas_call | solution.py:59
  40.1 1.6 %shard_map.104 = (bf16[128,768]{1,0:T(8,128)(2,1)S(1)}, bf16[128,1024]{1,0:T(8,128)(2,1)S(1)}, f32[3,8,256]{2,1,0:T(8,128)S(1)}) custom-call(f32[1,2]{1,0:T(1,128)S(1)} %maximum_bitcast_fusion.1.scal_ref, s32[1,1]{1,0:T(1,128)} %bitcast.8.at_ref, bf16[1024,768]{1,0:T(8,128)(2,1)S(1)} %bitcast.22, f32[3,8,256]{2,1,0:T(8,128)S(1)} %get-tuple-element.64.refs_0_, ...), custom_call_target="tpu_custom_call" | custom-call | flops 402653184 | bytes 3538944 | tf_op jit(solution)/shard_map/pallas_call | solution.py:59
  41.7 1.5 %collective-permute-start.9 = (bf16[128,768]{1,0:T(8,128)(2,1)S(1)}, bf16[128,768]{1,0:T(8,128)(2,1)S(1)}, u32[]{:S(2)}, u32[]{:S(2)}) collective-permute-start(bf16[128,768]{1,0:T(8,128)(2,1)S(1)} %get-tuple-element.73), channel_id=1, source_target_pairs={{0,16},{16,0},{32,48},{48,32},{64,80},{80,64},{96,112},{112,96},{1... | collective-permute-start | bytes 589832 | tf_op jit(solution)/shard_map/ppermute | solution.py:471
  43.8 3.3 %shard_map.105 = (bf16[1024,768]{1,0:T(8,128)(2,1)}, f32[8,128]{1,0:T(8,128)S(1)}) custom-call(bf16[640,1024]{1,0:T(8,128)(2,1)S(1)} %get-tuple-element.61.refs_0_, bf16[256,1024]{1,0:T(8,128)(2,1)S(1)} %get-tuple-element.63.refs_1_, bf16[128,1024]{1,0:T(8,128)(2,1)S(1)} %get-tuple-element.65.refs_2_, ...), custom_call_target="tpu_custom_call" | custom-call | flops 1610612736 | bytes 5242880 | tf_op jit(solution)/shard_map/pallas_call | solution.py:59
  47.8 4.5 %collective-permute-start.10 = (bf16[128,768]{1,0:T(8,128)(2,1)S(1)}, bf16[128,768]{1,0:T(8,128)(2,1)S(1)}, u32[]{:S(2)}, u32[]{:S(2)}) collective-permute-start(bf16[128,768]{1,0:T(8,128)(2,1)S(1)} %shard_map.106), channel_id=1, source_target_pairs={{0,112},{16,32},{32,16},{48,64},{64,48},{80,96},{96,80},{112,0},{1... | collective-permute-start | bytes 589832 | tf_op jit(solution)/shard_map/ppermute | solution.py:471
  52.3 4.9 %all-to-all-start.1 = ((bf16[8,128,768]{2,1,0:T(8,128)(2,1)}), bf16[8,128,768]{2,1,0:T(8,128)(2,1)}, u32[]{:S(2)}, u32[]{:S(2)}) async-start(bf16[8,128,768]{2,1,0:T(8,128)(2,1)} %bitcast.29), calls=%async_computation.1 | async-start | bytes 3145728 | tf_op jit(solution)/shard_map/all_to_all | solution.py:512
  57.4 2.5 %collective-permute-start.13 = (bf16[128,768]{1,0:T(8,128)(2,1)S(1)}, bf16[128,768]{1,0:T(8,128)(2,1)S(1)}, u32[]{:S(2)}, u32[]{:S(2)}) collective-permute-start(bf16[128,768]{1,0:T(8,128)(2,1)S(1)} %get-tuple-element.77), channel_id=1, source_target_pairs={{0,112},{16,32},{32,16},{48,64},{64,48},{80,96},{96,80},{112,0},{1... | collective-permute-start | bytes 589832 | tf_op jit(solution)/shard_map/ppermute | solution.py:471
  60.5 2.6 %collective-permute-done.12.refs_2_ = bf16[128,768]{1,0:T(8,128)(2,1)S(1)} collective-permute-done((bf16[128,768]{1,0:T(8,128)(2,1)S(1)}, bf16[128,768]{1,0:T(8,128)(2,1)S(1)}, u32[]{:S(2)}, u32[]{:S(2)}) %collective-permute-start.12) | collective-permute-done | bytes 196640 | tf_op jit(solution)/shard_map/ppermute | solution.py:471
  63.1 1.4 %collective-permute-done.13.refs_3_ = bf16[128,768]{1,0:T(8,128)(2,1)S(1)} collective-permute-done((bf16[128,768]{1,0:T(8,128)(2,1)S(1)}, bf16[128,768]{1,0:T(8,128)(2,1)S(1)}, u32[]{:S(2)}, u32[]{:S(2)}) %collective-permute-start.13) | collective-permute-done | bytes 196640 | tf_op jit(solution)/shard_map/ppermute | solution.py:471
  64.6 3.8 %collective-permute-start.14 = (bf16[128,768]{1,0:T(8,128)(2,1)S(1)}, bf16[128,768]{1,0:T(8,128)(2,1)S(1)}, u32[]{:S(2)}, u32[]{:S(2)}) collective-permute-start(bf16[128,768]{1,0:T(8,128)(2,1)S(1)} %get-tuple-element.78), channel_id=1, source_target_pairs={{0,112},{16,32},{32,16},{48,64},{64,48},{80,96},{96,80},{112,0},{1... | collective-permute-start | bytes 589832 | tf_op jit(solution)/shard_map/ppermute | solution.py:471
  69.2 1.8 %shard_map.100.xt_ref = bf16[1536,512]{1,0:T(8,128)(2,1)S(1)} custom-call(bf16[128,1536]{1,0:T(8,128)(2,1)} %bitcast.24, bf16[128,1536]{1,0:T(8,128)(2,1)} %bitcast.27, bf16[128,1536]{1,0:T(8,128)(2,1)} %copy-done.13, bf16[128,1536]{1,0:T(8,128)(2,1)} %collective-permute-done.1.refs_3_), custom_call_target="tpu_custom_call" | custom-call | flops 786432 | bytes 3145728 | tf_op jit(solution)/shard_map/pallas_call | solution.py:59
  72.0 2.0 %collective-permute-done.15.qb_ref = bf16[128,768]{1,0:T(8,128)(2,1)S(1)} collective-permute-done((bf16[128,768]{1,0:T(8,128)(2,1)S(1)}, bf16[128,768]{1,0:T(8,128)(2,1)S(1)}, u32[]{:S(2)}, u32[]{:S(2)}) %collective-permute-start.15) | collective-permute-done | bytes 196640 | tf_op jit(solution)/shard_map/ppermute | solution.py:471
  74.7 2.7 %shard_map.109 = (bf16[128,768]{1,0:T(8,128)(2,1)S(1)}, bf16[128,768]{1,0:T(8,128)(2,1)S(1)}, bf16[256,384]{1,0:T(8,128)(2,1)S(1)}, bf16[256,384]{1,0:T(8,128)(2,1)S(1)}) custom-call(f32[1,2]{1,0:T(1,128)S(1)} %maximum_bitcast_fusion.scal_ref, f32[128,768]{1,0:T(8,128)} %get-tuple-element.55.ui_hbm, f32[128,128]{1,0:T(8,128)} %get-tuple-element.56.ni_hbm, ...), custom_call_target="tpu_custom_call" | custom-call | flops 1966080 | bytes 2949120 | tf_op jit(solution)/shard_map/pallas_call | solution.py:59
  78.9 1.5 %shard_map.111 = bf16[8,208,384]{2,1,0:T(8,128)(2,1)} custom-call(bf16[1536,512]{1,0:T(8,128)(2,1)S(1)} %shard_map.100.xt_ref, f32[1536,384]{1,0:T(8,128)S(1)} %shard_map.110.own_ref, bf16[256,384]{1,0:T(8,128)(2,1)S(1)} %collective-permute-done.16.got_ref, bf16[16,384]{1,0:T(8,128)(2,1)S(1)} %maximum_maximum_fusion.extra_ref), custom_call_target="tpu_custom_call" | custom-call | flops 301989888 | bytes 2752512 | tf_op jit(solution)/shard_map/pallas_call | solution.py:59
  80.4 4.6 %all-to-all-start.2 = ((bf16[8,208,384]{2,1,0:T(8,128)(2,1)}), bf16[8,208,384]{2,1,0:T(8,128)(2,1)}, u32[]{:S(2)}, u32[]{:S(2)}) async-start(bf16[8,208,384]{2,1,0:T(8,128)(2,1)} %shard_map.111), calls=%async_computation.2 | async-start | bytes 2555904 | tf_op jit(solution)/shard_map/all_to_all | solution.py:526
  84.9 2.4 %shard_map.112 = (bf16[128,1536]{1,0:T(8,128)(2,1)}, bf16[128,1536]{1,0:T(8,128)(2,1)}, f32[8,128]{1,0:T(8,128)S(1)}) custom-call(bf16[128,768]{1,0:T(8,128)(2,1)S(1)} %get-tuple-element.83.di_ref, bf16[128,768]{1,0:T(8,128)(2,1)S(1)} %get-tuple-element.84.dt_ref, bf16[1536,768]{1,0:T(8,128)(2,1)S(1)} %copy-done), custom_call_target="tpu_custom_call" | custom-call | flops 603979776 | bytes 3932160 | tf_op jit(solution)/shard_map/pallas_call | solution.py:59
  87.3 15.3 %all-to-all-done.2.parts_hbm = bf16[8,208,384]{2,1,0:T(8,128)(2,1)} async-done(((bf16[8,208,384]{2,1,0:T(8,128)(2,1)}), bf16[8,208,384]{2,1,0:T(8,128)(2,1)}, u32[]{:S(2)}, u32[]{:S(2)}) %all-to-all-start.2) | async-done | bytes 1277984 | tf_op jit(solution)/shard_map/all_to_all | solution.py:526
  102.6 1.5 %shard_map.113 = bf16[8,32,384]{2,1,0:T(8,128)(2,1)S(1)} custom-call(bf16[8,208,384]{2,1,0:T(8,128)(2,1)} %all-to-all-done.2.parts_hbm, f32[8,128]{1,0:T(8,128)S(1)} %get-tuple-element.85._), custom_call_target="tpu_custom_call" | custom-call | flops 6389760 | bytes 1277952 | tf_op jit(solution)/shard_map/pallas_call | solution.py:59
  104.1 14.0 %all_to_all.32 = bf16[8,32,384]{2,1,0:T(8,128)(2,1)S(1)} all-to-all(bf16[8,32,384]{2,1,0:T(8,128)(2,1)S(1)} %shard_map.113), channel_id=1, replica_groups=mesh['xl'=2,'z'=8,'y'=4,'xh'=2,'c'=2] {'z'}, dimensions={0} | all-to-all | bytes 393216 | tf_op jit(solution)/shard_map/all_to_all | solution.py:527
  119.1 4.8 %collective-permute-done.17.r_ref = f32[32,384]{1,0:T(8,128)S(1)} collective-permute-done((f32[32,384]{1,0:T(8,128)S(1)}, f32[32,384]{1,0:T(8,128)S(1)}, u32[]{:S(2)}, u32[]{:S(2)}) %collective-permute-start.17) | collective-permute-done | bytes 49184 | tf_op jit(solution)/shard_map/ppermute | solution.py:465
  124.0 1.2 collective-permute-done.18.o_ref
  125.2 1.2 shard_map.114
  (68 shorter events, 8.0 us)
Async XLA Ops:
  4.9 28.2 %all-to-all-start = ((bf16[8,128,768]{2,1,0:T(8,128)(2,1)}), bf16[8,128,768]{2,1,0:T(8,128)(2,1)S(1)}, u32[]{:S(2)}, u32[]{:S(2)}) async-start(bf16[8,128,768]{2,1,0:T(8,128)(2,1)} %bitcast.30), calls=%async_computation | async-start | bytes 3145728 | tf_op jit(solution)/shard_map/all_to_all | solution.py:497
  10.0 10.5 %collective-permute-start.3 = (bf16[128,768]{1,0:T(8,128)(2,1)S(1)}, bf16[128,768]{1,0:T(8,128)(2,1)S(1)}, u32[]{:S(2)}, u32[]{:S(2)}) collective-permute-start(bf16[128,768]{1,0:T(8,128)(2,1)S(1)} %get-tuple-element.60.refs_0_.refs_3_), channel_id=1, source_target_pairs={{0,112},{16,32},{32,16},{48,64},{64,48},{80,96},{96,80},{112,0},{1... | collective-permute-start | bytes 589832 | tf_op jit(solution)/shard_map/ppermute | solution.py:471
  15.9 6.1 %collective-permute-start.2 = (bf16[128,768]{1,0:T(8,128)(2,1)S(1)}, bf16[128,768]{1,0:T(8,128)(2,1)S(1)}, u32[]{:S(2)}, u32[]{:S(2)}) collective-permute-start(bf16[128,768]{1,0:T(8,128)(2,1)S(1)} %get-tuple-element.60.refs_0_.refs_3_), channel_id=1, source_target_pairs={{0,16},{16,0},{32,48},{48,32},{64,80},{80,64},{96,112},{112,96},{1... | collective-permute-start | bytes 589832 | tf_op jit(solution)/shard_map/ppermute | solution.py:471
  20.5 5.8 %collective-permute-start.4 = (bf16[128,768]{1,0:T(8,128)(2,1)S(1)}, bf16[128,768]{1,0:T(8,128)(2,1)S(1)}, u32[]{:S(2)}, u32[]{:S(2)}) collective-permute-start(bf16[128,768]{1,0:T(8,128)(2,1)S(1)} %collective-permute-done.3.refs_2_.refs_5_), channel_id=1, source_target_pairs={{0,16},{16,0},{32,48},{48,32},{64,80},{80,64},{96,112},{112,96},{1... | collective-permute-start | bytes 589832 | tf_op jit(solution)/shard_map/ppermute | solution.py:471
  22.0 8.5 %collective-permute-start.5 = (bf16[128,768]{1,0:T(8,128)(2,1)S(1)}, bf16[128,768]{1,0:T(8,128)(2,1)S(1)}, u32[]{:S(2)}, u32[]{:S(2)}) collective-permute-start(bf16[128,768]{1,0:T(8,128)(2,1)S(1)} %collective-permute-done.2.refs_1_.refs_4_), channel_id=1, source_target_pairs={{0,112},{16,32},{32,16},{48,64},{64,48},{80,96},{96,80},{112,0},{1... | collective-permute-start | bytes 589832 | tf_op jit(solution)/shard_map/ppermute | solution.py:471
  26.3 6.9 %collective-permute-start.7 = (bf16[128,768]{1,0:T(8,128)(2,1)S(1)}, bf16[128,768]{1,0:T(8,128)(2,1)S(1)}, u32[]{:S(2)}, u32[]{:S(2)}) collective-permute-start(bf16[128,768]{1,0:T(8,128)(2,1)S(1)} %collective-permute-done.4.refs_3_.refs_6_), channel_id=1, source_target_pairs={{0,112},{16,32},{32,16},{48,64},{64,48},{80,96},{96,80},{112,0},{1... | collective-permute-start | bytes 589832 | tf_op jit(solution)/shard_map/ppermute | solution.py:471
  30.5 7.1 %collective-permute-start.6 = (bf16[128,768]{1,0:T(8,128)(2,1)S(1)}, bf16[128,768]{1,0:T(8,128)(2,1)S(1)}, u32[]{:S(2)}, u32[]{:S(2)}) collective-permute-start(bf16[128,768]{1,0:T(8,128)(2,1)S(1)} %collective-permute-done.5.refs_4_.refs_7_), channel_id=1, source_target_pairs={{0,16},{16,0},{32,48},{48,32},{64,80},{80,64},{96,112},{112,96},{1... | collective-permute-start | bytes 589832 | tf_op jit(solution)/shard_map/ppermute | solution.py:471
  33.1 7.0 %collective-permute-start.8 = (bf16[128,768]{1,0:T(8,128)(2,1)S(1)}, bf16[128,768]{1,0:T(8,128)(2,1)S(1)}, u32[]{:S(2)}, u32[]{:S(2)}) collective-permute-start(bf16[128,768]{1,0:T(8,128)(2,1)S(1)} %collective-permute-done.7.refs_2_.refs_9_), channel_id=1, source_target_pairs={{0,16},{16,0},{32,48},{48,32},{64,80},{80,64},{96,112},{112,96},{1... | collective-permute-start | bytes 589832 | tf_op jit(solution)/shard_map/ppermute | solution.py:471
  36.9 4.8 %copy-start.3 = (bf16[128,768]{1,0:T(8,128)(2,1)}, bf16[128,768]{1,0:T(8,128)(2,1)S(1)}, u32[]{:S(2)}) copy-start(bf16[128,768]{1,0:T(8,128)(2,1)S(1)} %get-tuple-element.69.refs_1_) | copy-start | bytes 589828
  36.9 4.8 %copy-start.5 = (bf16[128,768]{1,0:T(8,128)(2,1)}, bf16[128,768]{1,0:T(8,128)(2,1)S(1)}, u32[]{:S(2)}) copy-start(bf16[128,768]{1,0:T(8,128)(2,1)S(1)} %get-tuple-element.68.refs_0_) | copy-start | bytes 589828
  36.9 4.8 %copy-start.7 = (bf16[128,768]{1,0:T(8,128)(2,1)}, bf16[128,768]{1,0:T(8,128)(2,1)S(1)}, u32[]{:S(2)}) copy-start(bf16[128,768]{1,0:T(8,128)(2,1)S(1)} %get-tuple-element.70.refs_0_) | copy-start | bytes 589828
  36.9 4.8 %copy-start.9 = (bf16[128,768]{1,0:T(8,128)(2,1)}, bf16[128,768]{1,0:T(8,128)(2,1)S(1)}, u32[]{:S(2)}) copy-start(bf16[128,768]{1,0:T(8,128)(2,1)S(1)} %get-tuple-element.71.refs_1_) | copy-start | bytes 589828
  40.1 3.7 %copy-start.2 = (bf16[128,768]{1,0:T(8,128)(2,1)S(1)}, bf16[128,768]{1,0:T(8,128)(2,1)}, u32[]{:S(2)}) copy-start(bf16[128,768]{1,0:T(8,128)(2,1)} %copy-done.1) | copy-start | bytes 589828
  41.7 6.0 %collective-permute-start.9 = (bf16[128,768]{1,0:T(8,128)(2,1)S(1)}, bf16[128,768]{1,0:T(8,128)(2,1)S(1)}, u32[]{:S(2)}, u32[]{:S(2)}) collective-permute-start(bf16[128,768]{1,0:T(8,128)(2,1)S(1)} %get-tuple-element.73), channel_id=1, source_target_pairs={{0,16},{16,0},{32,48},{48,32},{64,80},{80,64},{96,112},{112,96},{1... | collective-permute-start | bytes 589832 | tf_op jit(solution)/shard_map/ppermute | solution.py:471
  43.2 14.0 %collective-permute-start.11 = (bf16[128,768]{1,0:T(8,128)(2,1)}, bf16[128,768]{1,0:T(8,128)(2,1)S(1)}, u32[]{:S(2)}, u32[]{:S(2)}) collective-permute-start(bf16[128,768]{1,0:T(8,128)(2,1)} %get-tuple-element.75), channel_id=1, source_target_pairs={{0,16},{16,0},{32,48},{48,32},{64,80},{80,64},{96,112},{112,96},{1... | collective-permute-start | bytes 589832 | tf_op jit(solution)/shard_map/ppermute | solution.py:471
  47.8 9.4 %collective-permute-start.10 = (bf16[128,768]{1,0:T(8,128)(2,1)S(1)}, bf16[128,768]{1,0:T(8,128)(2,1)S(1)}, u32[]{:S(2)}, u32[]{:S(2)}) collective-permute-start(bf16[128,768]{1,0:T(8,128)(2,1)S(1)} %shard_map.106), channel_id=1, source_target_pairs={{0,112},{16,32},{32,16},{48,64},{64,48},{80,96},{96,80},{112,0},{1... | collective-permute-start | bytes 589832 | tf_op jit(solution)/shard_map/ppermute | solution.py:471
  52.3 4.9 %copy-start.8 = (bf16[128,768]{1,0:T(8,128)(2,1)S(1)}, bf16[128,768]{1,0:T(8,128)(2,1)}, u32[]{:S(2)}) copy-start(bf16[128,768]{1,0:T(8,128)(2,1)} %copy-done.7) | copy-start | bytes 589828
  52.3 4.9 %copy-start.10 = (bf16[128,768]{1,0:T(8,128)(2,1)S(1)}, bf16[128,768]{1,0:T(8,128)(2,1)}, u32[]{:S(2)}) copy-start(bf16[128,768]{1,0:T(8,128)(2,1)} %copy-done.9) | copy-start | bytes 589828
  52.3 22.4 %all-to-all-start.1 = ((bf16[8,128,768]{2,1,0:T(8,128)(2,1)}), bf16[8,128,768]{2,1,0:T(8,128)(2,1)}, u32[]{:S(2)}, u32[]{:S(2)}) async-start(bf16[8,128,768]{2,1,0:T(8,128)(2,1)} %bitcast.29), calls=%async_computation.1 | async-start | bytes 3145728 | tf_op jit(solution)/shard_map/all_to_all | solution.py:512
  57.2 7.3 %copy-start.4 = (bf16[128,768]{1,0:T(8,128)(2,1)S(1)}, bf16[128,768]{1,0:T(8,128)(2,1)}, u32[]{:S(2)}) copy-start(bf16[128,768]{1,0:T(8,128)(2,1)} %copy-done.3) | copy-start | bytes 589828
  57.2 7.2 %copy-start.6 = (bf16[128,768]{1,0:T(8,128)(2,1)S(1)}, bf16[128,768]{1,0:T(8,128)(2,1)}, u32[]{:S(2)}) copy-start(bf16[128,768]{1,0:T(8,128)(2,1)} %copy-done.5) | copy-start | bytes 589828
  57.3 5.8 %collective-permute-start.12 = (bf16[128,768]{1,0:T(8,128)(2,1)S(1)}, bf16[128,768]{1,0:T(8,128)(2,1)S(1)}, u32[]{:S(2)}, u32[]{:S(2)}) collective-permute-start(bf16[128,768]{1,0:T(8,128)(2,1)S(1)} %get-tuple-element.76), channel_id=1, source_target_pairs={{0,16},{16,0},{32,48},{48,32},{64,80},{80,64},{96,112},{112,96},{1... | collective-permute-start | bytes 589832 | tf_op jit(solution)/shard_map/ppermute | solution.py:471
  57.4 7.0 %collective-permute-start.13 = (bf16[128,768]{1,0:T(8,128)(2,1)S(1)}, bf16[128,768]{1,0:T(8,128)(2,1)S(1)}, u32[]{:S(2)}, u32[]{:S(2)}) collective-permute-start(bf16[128,768]{1,0:T(8,128)(2,1)S(1)} %get-tuple-element.77), channel_id=1, source_target_pairs={{0,112},{16,32},{32,16},{48,64},{64,48},{80,96},{96,80},{112,0},{1... | collective-permute-start | bytes 589832 | tf_op jit(solution)/shard_map/ppermute | solution.py:471
  59.9 8.5 %collective-permute-start = (bf16[128,1536]{1,0:T(8,128)(2,1)S(1)}, bf16[128,1536]{1,0:T(8,128)(2,1)S(1)}, u32[]{:S(2)}, u32[]{:S(2)}) collective-permute-start(bf16[128,1536]{1,0:T(8,128)(2,1)S(1)} %bitcast.25), channel_id=1, source_target_pairs={{0,1},{1,0},{2,3},{3,2},{4,5},{5,4},{6,7},{7,6},{8,9},{9,8},{10,11... | collective-permute-start | bytes 1179656 | tf_op jit(solution)/shard_map/ppermute | solution.py:465
  59.9 9.2 %collective-permute-start.1 = (bf16[128,1536]{1,0:T(8,128)(2,1)S(1)}, bf16[128,1536]{1,0:T(8,128)(2,1)}, u32[]{:S(2)}, u32[]{:S(2)}) collective-permute-start(bf16[128,1536]{1,0:T(8,128)(2,1)S(1)} %bitcast.28), channel_id=1, source_target_pairs={{0,1},{1,0},{2,3},{3,2},{4,5},{5,4},{6,7},{7,6},{8,9},{9,8},{10,11... | collective-permute-start | bytes 1179656 | tf_op jit(solution)/shard_map/ppermute | solution.py:465
  64.6 7.4 %collective-permute-start.14 = (bf16[128,768]{1,0:T(8,128)(2,1)S(1)}, bf16[128,768]{1,0:T(8,128)(2,1)S(1)}, u32[]{:S(2)}, u32[]{:S(2)}) collective-permute-start(bf16[128,768]{1,0:T(8,128)(2,1)S(1)} %get-tuple-element.78), channel_id=1, source_target_pairs={{0,112},{16,32},{32,16},{48,64},{64,48},{80,96},{96,80},{112,0},{1... | collective-permute-start | bytes 589832 | tf_op jit(solution)/shard_map/ppermute | solution.py:471
  68.3 5.7 %collective-permute-start.15 = (bf16[128,768]{1,0:T(8,128)(2,1)S(1)}, bf16[128,768]{1,0:T(8,128)(2,1)S(1)}, u32[]{:S(2)}, u32[]{:S(2)}) collective-permute-start(bf16[128,768]{1,0:T(8,128)(2,1)S(1)} %get-tuple-element.79), channel_id=1, source_target_pairs={{0,16},{16,0},{32,48},{48,32},{64,80},{80,64},{96,112},{112,96},{1... | collective-permute-start | bytes 589832 | tf_op jit(solution)/shard_map/ppermute | solution.py:471
  77.4 1.5 %collective-permute-start.16 = (bf16[256,384]{1,0:T(8,128)(2,1)S(1)}, bf16[256,384]{1,0:T(8,128)(2,1)S(1)}, u32[]{:S(2)}, u32[]{:S(2)}) collective-permute-start(bf16[256,384]{1,0:T(8,128)(2,1)S(1)} %get-tuple-element.81), channel_id=1, source_target_pairs={{0,1},{1,0},{2,3},{3,2},{4,5},{5,4},{6,7},{7,6},{8,9},{9,8},{10,11... | collective-permute-start | bytes 589832 | tf_op jit(solution)/shard_map/ppermute | solution.py:465
  80.4 4.6 %copy-start = (bf16[1536,768]{1,0:T(8,128)(2,1)S(1)}, bf16[1536,768]{1,0:T(8,128)(2,1)}, u32[]{:S(2)}) copy-start(bf16[1536,768]{1,0:T(8,128)(2,1)} %head_ref.1) | copy-start | bytes 7077892
  80.4 22.3 %all-to-all-start.2 = ((bf16[8,208,384]{2,1,0:T(8,128)(2,1)}), bf16[8,208,384]{2,1,0:T(8,128)(2,1)}, u32[]{:S(2)}, u32[]{:S(2)}) async-start(bf16[8,208,384]{2,1,0:T(8,128)(2,1)} %shard_map.111), calls=%async_computation.2 | async-start | bytes 2555904 | tf_op jit(solution)/shard_map/all_to_all | solution.py:526
  118.2 5.7 %collective-permute-start.17 = (f32[32,384]{1,0:T(8,128)S(1)}, f32[32,384]{1,0:T(8,128)S(1)}, u32[]{:S(2)}, u32[]{:S(2)}) collective-permute-start(f32[32,384]{1,0:T(8,128)S(1)} %convert_reduce_fusion.s_ref), channel_id=1, source_target_pairs={{0,2},{2,0},{1,3},{3,1},{4,6},{6,4},{5,7},{7,5},{8,10},{10,8},{9,1... | collective-permute-start | bytes 147464 | tf_op jit(solution)/shard_map/ppermute | solution.py:465
  123.9 1.3 %collective-permute-start.18 = (f32[32,384]{1,0:T(8,128)S(1)}, f32[32,384]{1,0:T(8,128)S(1)}, u32[]{:S(2)}, u32[]{:S(2)}) collective-permute-start(f32[32,384]{1,0:T(8,128)S(1)} %add.11), channel_id=1, source_target_pairs={{0,1},{1,0},{2,3},{3,2},{4,5},{5,4},{6,7},{7,6},{8,9},{9,8},{10,11... | collective-permute-start | bytes 147464 | tf_op jit(solution)/shard_map/ppermute | solution.py:465
  (4 other events, 8.7 us)

commit v7 on v5

--- a/solution.py
+++ b/solution.py
@@ -157,7 +157,8 @@
         for r in range(rows // RB):
             s = s_ref[r * RB : (r + 1) * RB, c * CB : (c + 1) * CB]
             z = s * scale2 + bias2
-            if diag_at is not None:
+            diag = diag_at is not None and r * RB < R
+            if diag:
                 row = r * RB + lax.broadcasted_iota(jnp.int32, (RB, CB), 0)
                 col = c * CB + lax.broadcasted_iota(jnp.int32, (RB, CB), 1)
                 mask = row + diag_at == col
@@ -166,7 +167,7 @@
             one_t = 1.0 + t
             inv = 1.0 / one_t
             g = jnp.where(z >= 0.0, inv, t * inv)
-            if diag_at is not None:
+            if diag:
                 g = jnp.where(mask, -g, g)
             g_ref[r * RB : (r + 1) * RB, c * CB : (c + 1) * CB] = g.astype(BF16)
             acc_m = acc_m + fold(jnp.maximum(z, 0.0))
@@ -505,7 +506,7 @@
     scal = jnp.stack([scale * LOG2E, bias * LOG2E]).reshape(1, 2)
     at = (lax.axis_index(near) * R).reshape(1, 1)
     us = (u, a1, b1, a2, b2, a3, b3)
-    p0, pa1, pb1, pa2, pb2, g1, sums = pair(((0,), (1, 2), (3, 4)), True, scal, at, vs, us[:5])
+    p0, pa1, pb1, pa2, pb2, g1, sums = pair(((0, 1), (2, 3, 4)), True, scal, at, vs, us[:5])
     pa3, pb3, g2, sums = pair(((0, 1),), False, scal, at, vs, us[5:], (sums,))
     pf, g3, sums = pair(((0,),), False, scal, at, vs, (far,), (sums,))
 

time: 128 us -> 128 us (level)
  transfers between devices with their start and end apart: 22 -> 22, of which waited for: 15 -> 15; matrix products, arithmetic and copies ran while one was open for 0% -> 0% of each run, Pallas kernels for 12% -> 11%
where the time goes in v7:
time: 128 us; the launch traced here: 126 us
  waiting for transfers between devices  42.1 us (33%)
  starting transfers between devices  39.5 us (31%)
  Pallas kernels  26.6 us (21%)
  blocking collectives  14 us (11%)
  between operations  2.28 us (2%)
    pallas_call x15, Pallas kernels, call(): pl.pallas_call(kernel, out_shape=jax.tree.map(place_out, out_shape, out_s...  26.6 us
    ppermute x6, starting transfers between devices, ring(): lax.ppermute(v, axis, odd)  21 us
    all_to_all x1, waiting for transfers between devices, per_device(): parts = lax.all_to_all(parts, ('xl', 'y'), 0, 0, tiled=True)  15.3 us
    all_to_all x1, blocking collectives, per_device(): parts = lax.all_to_all(sum_parts(parts, done), 'z', 0, 0, tiled=True)  14 us
    ppermute x8, waiting for transfers between devices, ring(): lax.ppermute(v, axis, even)  10.1 us
    ppermute x6, waiting for transfers between devices, ring(): lax.ppermute(v, axis, odd)  9.29 us
    ppermute x5, waiting for transfers between devices, swap(): return lambda v: lax.ppermute(v, axis, [(0, 1), (1, 0)])  6.78 us
    all_to_all x1, starting transfers between devices, per_device(): vs = lax.all_to_all(v, near, 0, 0, tiled=True)  5.11 us
  transfers between devices with their start and end apart: 22, of which 15 were waited for; matrix products, arithmetic and copies ran while one was open for 0% of the time, Pallas kernels for 11%

profile of v7, /device:TPU:4, one launch (start us, length us, event | category | flops | bytes accessed | tf_op | source)
XLA Modules:
  0.0 125.8 jit_solution(15268035744444814756)
XLA Ops:
  0.6 3.8 %shard_map.101 = (bf16[128,768]{1,0:T(8,128)(2,1)S(1)}, bf16[1024,768]{1,0:T(8,128)(2,1)}, f32[128,768]{1,0:T(8,128)}, f32[128,128]{1,0:T(8,128)}, f32[128,768]{1,0:T(8,128)}, /*index=5*/f32[128,128]{1,0:T(8,128)}) custom-call(bf16[128,1536]{1,0:T(8,128)(2,1)} %bitcast.23, bf16[128,1536]{1,0:T(8,128)(2,1)} %bitcast.26, bf16[1536,768]{1,0:T(8,128)(2,1)} %head_ref.1), custom_call_target="tpu_custom_call" | custom-call | flops 603979776 | bytes 3145728 | tf_op jit(solution)/shard_map/pallas_call | solution.py:59
  4.5 5.1 %all-to-all-start = ((bf16[8,128,768]{2,1,0:T(8,128)(2,1)}), bf16[8,128,768]{2,1,0:T(8,128)(2,1)S(1)}, u32[]{:S(2)}, u32[]{:S(2)}) async-start(bf16[8,128,768]{2,1,0:T(8,128)(2,1)} %bitcast.30), calls=%async_computation | async-start | bytes 3145728 | tf_op jit(solution)/shard_map/all_to_all | solution.py:500
  9.6 5.9 %collective-permute-start.3 = (bf16[128,768]{1,0:T(8,128)(2,1)S(1)}, bf16[128,768]{1,0:T(8,128)(2,1)S(1)}, u32[]{:S(2)}, u32[]{:S(2)}) collective-permute-start(bf16[128,768]{1,0:T(8,128)(2,1)S(1)} %get-tuple-element.60.refs_0_.refs_3_), channel_id=1, source_target_pairs={{0,112},{16,32},{32,16},{48,64},{64,48},{80,96},{96,80},{112,0},{1... | collective-permute-start | bytes 589832 | tf_op jit(solution)/shard_map/ppermute | solution.py:474
  15.4 4.6 %collective-permute-done.3.refs_2_.refs_5_ = bf16[128,768]{1,0:T(8,128)(2,1)S(1)} collective-permute-done((bf16[128,768]{1,0:T(8,128)(2,1)S(1)}, bf16[128,768]{1,0:T(8,128)(2,1)S(1)}, u32[]{:S(2)}, u32[]{:S(2)}) %collective-permute-start.3) | collective-permute-done | bytes 196640 | tf_op jit(solution)/shard_map/ppermute | solution.py:474
  20.0 1.5 %collective-permute-done.2.refs_1_.refs_4_ = bf16[128,768]{1,0:T(8,128)(2,1)S(1)} collective-permute-done((bf16[128,768]{1,0:T(8,128)(2,1)S(1)}, bf16[128,768]{1,0:T(8,128)(2,1)S(1)}, u32[]{:S(2)}, u32[]{:S(2)}) %collective-permute-start.2) | collective-permute-done | bytes 196640 | tf_op jit(solution)/shard_map/ppermute | solution.py:474
  21.5 1.5 %collective-permute-start.5 = (bf16[128,768]{1,0:T(8,128)(2,1)S(1)}, bf16[128,768]{1,0:T(8,128)(2,1)S(1)}, u32[]{:S(2)}, u32[]{:S(2)}) collective-permute-start(bf16[128,768]{1,0:T(8,128)(2,1)S(1)} %collective-permute-done.2.refs_1_.refs_4_), channel_id=1, source_target_pairs={{0,112},{16,32},{32,16},{48,64},{64,48},{80,96},{96,80},{112,0},{1... | collective-permute-start | bytes 589832 | tf_op jit(solution)/shard_map/ppermute | solution.py:474
  23.0 2.8 %collective-permute-done.4.refs_3_.refs_6_ = bf16[128,768]{1,0:T(8,128)(2,1)S(1)} collective-permute-done((bf16[128,768]{1,0:T(8,128)(2,1)S(1)}, bf16[128,768]{1,0:T(8,128)(2,1)S(1)}, u32[]{:S(2)}, u32[]{:S(2)}) %collective-permute-start.4) | collective-permute-done | bytes 196640 | tf_op jit(solution)/shard_map/ppermute | solution.py:474
  25.8 2.9 %collective-permute-start.7 = (bf16[128,768]{1,0:T(8,128)(2,1)S(1)}, bf16[128,768]{1,0:T(8,128)(2,1)S(1)}, u32[]{:S(2)}, u32[]{:S(2)}) collective-permute-start(bf16[128,768]{1,0:T(8,128)(2,1)S(1)} %collective-permute-done.4.refs_3_.refs_6_), channel_id=1, source_target_pairs={{0,112},{16,32},{32,16},{48,64},{64,48},{80,96},{96,80},{112,0},{1... | collective-permute-start | bytes 589832 | tf_op jit(solution)/shard_map/ppermute | solution.py:474
  30.2 2.5 %collective-permute-done.7.refs_2_.refs_9_ = bf16[128,768]{1,0:T(8,128)(2,1)S(1)} collective-permute-done((bf16[128,768]{1,0:T(8,128)(2,1)S(1)}, bf16[128,768]{1,0:T(8,128)(2,1)S(1)}, u32[]{:S(2)}, u32[]{:S(2)}) %collective-permute-start.7) | collective-permute-done | bytes 196640 | tf_op jit(solution)/shard_map/ppermute | solution.py:474
  32.7 3.6 %shard_map.102 = (bf16[128,768]{1,0:T(8,128)(2,1)S(1)}, bf16[128,768]{1,0:T(8,128)(2,1)S(1)}, bf16[128,768]{1,0:T(8,128)(2,1)S(1)}, bf16[128,768]{1,0:T(8,128)(2...) custom-call(f32[1,2]{1,0:T(1,128)S(1)} %maximum_bitcast_fusion.1.scal_ref, ...), custom_call_target="tpu_custom_call" | custom-call | flops 2013265920 | bytes 5111808 | tf_op jit(solution)/shard_map/pallas_call | solution.py:59
  37.1 2.5 %shard_map.103 = (bf16[128,768]{1,0:T(8,128)(2,1)}, bf16[128,768]{1,0:T(8,128)(2,1)S(1)}, bf16[256,1024]{1,0:T(8,128)(2,1)S(1)}, f32[3,8,256]{2,1,0:T(8,128)S(1)}) custom-call(f32[1,2]{1,0:T(1,128)S(1)} %maximum_bitcast_fusion.1.scal_ref, s32[1,1]{1,0:T(1,128)} %bitcast.8.at_ref, bf16[1024,768]{1,0:T(8,128)(2,1)S(1)} %bitcast.21, ...), custom_call_target="tpu_custom_call" | custom-call | flops 805306368 | bytes 3932160 | tf_op jit(solution)/shard_map/pallas_call | solution.py:59
  39.7 1.6 %shard_map.104 = (bf16[128,768]{1,0:T(8,128)(2,1)S(1)}, bf16[128,1024]{1,0:T(8,128)(2,1)S(1)}, f32[3,8,256]{2,1,0:T(8,128)S(1)}) custom-call(f32[1,2]{1,0:T(1,128)S(1)} %maximum_bitcast_fusion.1.scal_ref, s32[1,1]{1,0:T(1,128)} %bitcast.8.at_ref, bf16[1024,768]{1,0:T(8,128)(2,1)S(1)} %bitcast.22, f32[3,8,256]{2,1,0:T(8,128)S(1)} %get-tuple-element.64.refs_0_, ...), custom_call_target="tpu_custom_call" | custom-call | flops 402653184 | bytes 3538944 | tf_op jit(solution)/shard_map/pallas_call | solution.py:59
  41.3 1.4 %collective-permute-start.9 = (bf16[128,768]{1,0:T(8,128)(2,1)S(1)}, bf16[128,768]{1,0:T(8,128)(2,1)S(1)}, u32[]{:S(2)}, u32[]{:S(2)}) collective-permute-start(bf16[128,768]{1,0:T(8,128)(2,1)S(1)} %get-tuple-element.73), channel_id=1, source_target_pairs={{0,16},{16,0},{32,48},{48,32},{64,80},{80,64},{96,112},{112,96},{1... | collective-permute-start | bytes 589832 | tf_op jit(solution)/shard_map/ppermute | solution.py:474
  43.4 3.3 %shard_map.105 = (bf16[1024,768]{1,0:T(8,128)(2,1)}, f32[8,128]{1,0:T(8,128)S(1)}) custom-call(bf16[640,1024]{1,0:T(8,128)(2,1)S(1)} %get-tuple-element.61.refs_0_, bf16[256,1024]{1,0:T(8,128)(2,1)S(1)} %get-tuple-element.63.refs_1_, bf16[128,1024]{1,0:T(8,128)(2,1)S(1)} %get-tuple-element.65.refs_2_, ...), custom_call_target="tpu_custom_call" | custom-call | flops 1610612736 | bytes 5242880 | tf_op jit(solution)/shard_map/pallas_call | solution.py:59
  47.2 4.5 %collective-permute-start.10 = (bf16[128,768]{1,0:T(8,128)(2,1)S(1)}, bf16[128,768]{1,0:T(8,128)(2,1)S(1)}, u32[]{:S(2)}, u32[]{:S(2)}) collective-permute-start(bf16[128,768]{1,0:T(8,128)(2,1)S(1)} %shard_map.106), channel_id=1, source_target_pairs={{0,112},{16,32},{32,16},{48,64},{64,48},{80,96},{96,80},{112,0},{1... | collective-permute-start | bytes 589832 | tf_op jit(solution)/shard_map/ppermute | solution.py:474
  51.7 4.9 %all-to-all-start.1 = ((bf16[8,128,768]{2,1,0:T(8,128)(2,1)}), bf16[8,128,768]{2,1,0:T(8,128)(2,1)}, u32[]{:S(2)}, u32[]{:S(2)}) async-start(bf16[8,128,768]{2,1,0:T(8,128)(2,1)} %bitcast.29), calls=%async_computation.1 | async-start | bytes 3145728 | tf_op jit(solution)/shard_map/all_to_all | solution.py:515
  56.9 2.5 %collective-permute-start.13 = (bf16[128,768]{1,0:T(8,128)(2,1)S(1)}, bf16[128,768]{1,0:T(8,128)(2,1)S(1)}, u32[]{:S(2)}, u32[]{:S(2)}) collective-permute-start(bf16[128,768]{1,0:T(8,128)(2,1)S(1)} %get-tuple-element.77), channel_id=1, source_target_pairs={{0,112},{16,32},{32,16},{48,64},{64,48},{80,96},{96,80},{112,0},{1... | collective-permute-start | bytes 589832 | tf_op jit(solution)/shard_map/ppermute | solution.py:474
  59.9 2.6 %collective-permute-done.12.refs_2_ = bf16[128,768]{1,0:T(8,128)(2,1)S(1)} collective-permute-done((bf16[128,768]{1,0:T(8,128)(2,1)S(1)}, bf16[128,768]{1,0:T(8,128)(2,1)S(1)}, u32[]{:S(2)}, u32[]{:S(2)}) %collective-permute-start.12) | collective-permute-done | bytes 196640 | tf_op jit(solution)/shard_map/ppermute | solution.py:474
  62.5 1.4 %collective-permute-done.13.refs_3_ = bf16[128,768]{1,0:T(8,128)(2,1)S(1)} collective-permute-done((bf16[128,768]{1,0:T(8,128)(2,1)S(1)}, bf16[128,768]{1,0:T(8,128)(2,1)S(1)}, u32[]{:S(2)}, u32[]{:S(2)}) %collective-permute-start.13) | collective-permute-done | bytes 196640 | tf_op jit(solution)/shard_map/ppermute | solution.py:474
  64.0 3.8 %collective-permute-start.14 = (bf16[128,768]{1,0:T(8,128)(2,1)S(1)}, bf16[128,768]{1,0:T(8,128)(2,1)S(1)}, u32[]{:S(2)}, u32[]{:S(2)}) collective-permute-start(bf16[128,768]{1,0:T(8,128)(2,1)S(1)} %get-tuple-element.78), channel_id=1, source_target_pairs={{0,112},{16,32},{32,16},{48,64},{64,48},{80,96},{96,80},{112,0},{1... | collective-permute-start | bytes 589832 | tf_op jit(solution)/shard_map/ppermute | solution.py:474
  68.6 1.8 %shard_map.100.xt_ref = bf16[1536,512]{1,0:T(8,128)(2,1)S(1)} custom-call(bf16[128,1536]{1,0:T(8,128)(2,1)} %bitcast.24, bf16[128,1536]{1,0:T(8,128)(2,1)} %bitcast.27, bf16[128,1536]{1,0:T(8,128)(2,1)} %copy-done.13, bf16[128,1536]{1,0:T(8,128)(2,1)} %collective-permute-done.1.refs_3_), custom_call_target="tpu_custom_call" | custom-call | flops 786432 | bytes 3145728 | tf_op jit(solution)/shard_map/pallas_call | solution.py:59
  71.4 2.0 %collective-permute-done.15.qb_ref = bf16[128,768]{1,0:T(8,128)(2,1)S(1)} collective-permute-done((bf16[128,768]{1,0:T(8,128)(2,1)S(1)}, bf16[128,768]{1,0:T(8,128)(2,1)S(1)}, u32[]{:S(2)}, u32[]{:S(2)}) %collective-permute-start.15) | collective-permute-done | bytes 196640 | tf_op jit(solution)/shard_map/ppermute | solution.py:474
  74.1 2.7 %shard_map.109 = (bf16[128,768]{1,0:T(8,128)(2,1)S(1)}, bf16[128,768]{1,0:T(8,128)(2,1)S(1)}, bf16[256,384]{1,0:T(8,128)(2,1)S(1)}, bf16[256,384]{1,0:T(8,128)(2,1)S(1)}) custom-call(f32[1,2]{1,0:T(1,128)S(1)} %maximum_bitcast_fusion.scal_ref, f32[128,768]{1,0:T(8,128)} %get-tuple-element.55.ui_hbm, f32[128,128]{1,0:T(8,128)} %get-tuple-element.56.ni_hbm, ...), custom_call_target="tpu_custom_call" | custom-call | flops 1966080 | bytes 2949120 | tf_op jit(solution)/shard_map/pallas_call | solution.py:59
  78.3 1.5 %shard_map.111 = bf16[8,208,384]{2,1,0:T(8,128)(2,1)} custom-call(bf16[1536,512]{1,0:T(8,128)(2,1)S(1)} %shard_map.100.xt_ref, f32[1536,384]{1,0:T(8,128)S(1)} %shard_map.110.own_ref, bf16[256,384]{1,0:T(8,128)(2,1)S(1)} %collective-permute-done.16.got_ref, bf16[16,384]{1,0:T(8,128)(2,1)S(1)} %maximum_maximum_fusion.extra_ref), custom_call_target="tpu_custom_call" | custom-call | flops 301989888 | bytes 2752512 | tf_op jit(solution)/shard_map/pallas_call | solution.py:59
  79.8 4.6 %all-to-all-start.2 = ((bf16[8,208,384]{2,1,0:T(8,128)(2,1)}), bf16[8,208,384]{2,1,0:T(8,128)(2,1)}, u32[]{:S(2)}, u32[]{:S(2)}) async-start(bf16[8,208,384]{2,1,0:T(8,128)(2,1)} %shard_map.111), calls=%async_computation.2 | async-start | bytes 2555904 | tf_op jit(solution)/shard_map/all_to_all | solution.py:529
  84.4 2.4 %shard_map.112 = (bf16[128,1536]{1,0:T(8,128)(2,1)}, bf16[128,1536]{1,0:T(8,128)(2,1)}, f32[8,128]{1,0:T(8,128)S(1)}) custom-call(bf16[128,768]{1,0:T(8,128)(2,1)S(1)} %get-tuple-element.83.di_ref, bf16[128,768]{1,0:T(8,128)(2,1)S(1)} %get-tuple-element.84.dt_ref, bf16[1536,768]{1,0:T(8,128)(2,1)S(1)} %copy-done), custom_call_target="tpu_custom_call" | custom-call | flops 603979776 | bytes 3932160 | tf_op jit(solution)/shard_map/pallas_call | solution.py:59
  86.7 15.3 %all-to-all-done.2.parts_hbm = bf16[8,208,384]{2,1,0:T(8,128)(2,1)} async-done(((bf16[8,208,384]{2,1,0:T(8,128)(2,1)}), bf16[8,208,384]{2,1,0:T(8,128)(2,1)}, u32[]{:S(2)}, u32[]{:S(2)}) %all-to-all-start.2) | async-done | bytes 1277984 | tf_op jit(solution)/shard_map/all_to_all | solution.py:529
  102.0 1.5 %shard_map.113 = bf16[8,32,384]{2,1,0:T(8,128)(2,1)S(1)} custom-call(bf16[8,208,384]{2,1,0:T(8,128)(2,1)} %all-to-all-done.2.parts_hbm, f32[8,128]{1,0:T(8,128)S(1)} %get-tuple-element.85._), custom_call_target="tpu_custom_call" | custom-call | flops 6389760 | bytes 1277952 | tf_op jit(solution)/shard_map/pallas_call | solution.py:59
  103.5 14.0 %all_to_all.32 = bf16[8,32,384]{2,1,0:T(8,128)(2,1)S(1)} all-to-all(bf16[8,32,384]{2,1,0:T(8,128)(2,1)S(1)} %shard_map.113), channel_id=1, replica_groups=mesh['xl'=2,'z'=8,'y'=4,'xh'=2,'c'=2] {'z'}, dimensions={0} | all-to-all | bytes 393216 | tf_op jit(solution)/shard_map/all_to_all | solution.py:530
  118.5 4.8 %collective-permute-done.17.r_ref = f32[32,384]{1,0:T(8,128)S(1)} collective-permute-done((f32[32,384]{1,0:T(8,128)S(1)}, f32[32,384]{1,0:T(8,128)S(1)}, u32[]{:S(2)}, u32[]{:S(2)}) %collective-permute-start.17) | collective-permute-done | bytes 49184 | tf_op jit(solution)/shard_map/ppermute | solution.py:468
  123.4 1.2 collective-permute-done.18.o_ref
  124.6 1.2 shard_map.114
  (68 shorter events, 8.1 us)
Async XLA Ops:
  4.5 28.2 %all-to-all-start = ((bf16[8,128,768]{2,1,0:T(8,128)(2,1)}), bf16[8,128,768]{2,1,0:T(8,128)(2,1)S(1)}, u32[]{:S(2)}, u32[]{:S(2)}) async-start(bf16[8,128,768]{2,1,0:T(8,128)(2,1)} %bitcast.30), calls=%async_computation | async-start | bytes 3145728 | tf_op jit(solution)/shard_map/all_to_all | solution.py:500
  9.6 10.5 %collective-permute-start.3 = (bf16[128,768]{1,0:T(8,128)(2,1)S(1)}, bf16[128,768]{1,0:T(8,128)(2,1)S(1)}, u32[]{:S(2)}, u32[]{:S(2)}) collective-permute-start(bf16[128,768]{1,0:T(8,128)(2,1)S(1)} %get-tuple-element.60.refs_0_.refs_3_), channel_id=1, source_target_pairs={{0,112},{16,32},{32,16},{48,64},{64,48},{80,96},{96,80},{112,0},{1... | collective-permute-start | bytes 589832 | tf_op jit(solution)/shard_map/ppermute | solution.py:474
  15.4 6.1 %collective-permute-start.2 = (bf16[128,768]{1,0:T(8,128)(2,1)S(1)}, bf16[128,768]{1,0:T(8,128)(2,1)S(1)}, u32[]{:S(2)}, u32[]{:S(2)}) collective-permute-start(bf16[128,768]{1,0:T(8,128)(2,1)S(1)} %get-tuple-element.60.refs_0_.refs_3_), channel_id=1, source_target_pairs={{0,16},{16,0},{32,48},{48,32},{64,80},{80,64},{96,112},{112,96},{1... | collective-permute-start | bytes 589832 | tf_op jit(solution)/shard_map/ppermute | solution.py:474
  20.0 5.8 %collective-permute-start.4 = (bf16[128,768]{1,0:T(8,128)(2,1)S(1)}, bf16[128,768]{1,0:T(8,128)(2,1)S(1)}, u32[]{:S(2)}, u32[]{:S(2)}) collective-permute-start(bf16[128,768]{1,0:T(8,128)(2,1)S(1)} %collective-permute-done.3.refs_2_.refs_5_), channel_id=1, source_target_pairs={{0,16},{16,0},{32,48},{48,32},{64,80},{80,64},{96,112},{112,96},{1... | collective-permute-start | bytes 589832 | tf_op jit(solution)/shard_map/ppermute | solution.py:474
  21.5 8.5 %collective-permute-start.5 = (bf16[128,768]{1,0:T(8,128)(2,1)S(1)}, bf16[128,768]{1,0:T(8,128)(2,1)S(1)}, u32[]{:S(2)}, u32[]{:S(2)}) collective-permute-start(bf16[128,768]{1,0:T(8,128)(2,1)S(1)} %collective-permute-done.2.refs_1_.refs_4_), channel_id=1, source_target_pairs={{0,112},{16,32},{32,16},{48,64},{64,48},{80,96},{96,80},{112,0},{1... | collective-permute-start | bytes 589832 | tf_op jit(solution)/shard_map/ppermute | solution.py:474
  25.8 6.9 %collective-permute-start.7 = (bf16[128,768]{1,0:T(8,128)(2,1)S(1)}, bf16[128,768]{1,0:T(8,128)(2,1)S(1)}, u32[]{:S(2)}, u32[]{:S(2)}) collective-permute-start(bf16[128,768]{1,0:T(8,128)(2,1)S(1)} %collective-permute-done.4.refs_3_.refs_6_), channel_id=1, source_target_pairs={{0,112},{16,32},{32,16},{48,64},{64,48},{80,96},{96,80},{112,0},{1... | collective-permute-start | bytes 589832 | tf_op jit(solution)/shard_map/ppermute | solution.py:474
  30.0 7.1 %collective-permute-start.6 = (bf16[128,768]{1,0:T(8,128)(2,1)S(1)}, bf16[128,768]{1,0:T(8,128)(2,1)S(1)}, u32[]{:S(2)}, u32[]{:S(2)}) collective-permute-start(bf16[128,768]{1,0:T(8,128)(2,1)S(1)} %collective-permute-done.5.refs_4_.refs_7_), channel_id=1, source_target_pairs={{0,16},{16,0},{32,48},{48,32},{64,80},{80,64},{96,112},{112,96},{1... | collective-permute-start | bytes 589832 | tf_op jit(solution)/shard_map/ppermute | solution.py:474
  32.7 7.0 %collective-permute-start.8 = (bf16[128,768]{1,0:T(8,128)(2,1)S(1)}, bf16[128,768]{1,0:T(8,128)(2,1)S(1)}, u32[]{:S(2)}, u32[]{:S(2)}) collective-permute-start(bf16[128,768]{1,0:T(8,128)(2,1)S(1)} %collective-permute-done.7.refs_2_.refs_9_), channel_id=1, source_target_pairs={{0,16},{16,0},{32,48},{48,32},{64,80},{80,64},{96,112},{112,96},{1... | collective-permute-start | bytes 589832 | tf_op jit(solution)/shard_map/ppermute | solution.py:474
  36.3 4.9 %copy-start.3 = (bf16[128,768]{1,0:T(8,128)(2,1)}, bf16[128,768]{1,0:T(8,128)(2,1)S(1)}, u32[]{:S(2)}) copy-start(bf16[128,768]{1,0:T(8,128)(2,1)S(1)} %get-tuple-element.69.refs_1_) | copy-start | bytes 589828
  36.3 4.9 %copy-start.5 = (bf16[128,768]{1,0:T(8,128)(2,1)}, bf16[128,768]{1,0:T(8,128)(2,1)S(1)}, u32[]{:S(2)}) copy-start(bf16[128,768]{1,0:T(8,128)(2,1)S(1)} %get-tuple-element.68.refs_0_) | copy-start | bytes 589828
  36.3 4.9 %copy-start.7 = (bf16[128,768]{1,0:T(8,128)(2,1)}, bf16[128,768]{1,0:T(8,128)(2,1)S(1)}, u32[]{:S(2)}) copy-start(bf16[128,768]{1,0:T(8,128)(2,1)S(1)} %get-tuple-element.70.refs_0_) | copy-start | bytes 589828
  36.3 4.9 %copy-start.9 = (bf16[128,768]{1,0:T(8,128)(2,1)}, bf16[128,768]{1,0:T(8,128)(2,1)S(1)}, u32[]{:S(2)}) copy-start(bf16[128,768]{1,0:T(8,128)(2,1)S(1)} %get-tuple-element.71.refs_1_) | copy-start | bytes 589828
  39.6 3.7 %copy-start.2 = (bf16[128,768]{1,0:T(8,128)(2,1)S(1)}, bf16[128,768]{1,0:T(8,128)(2,1)}, u32[]{:S(2)}) copy-start(bf16[128,768]{1,0:T(8,128)(2,1)} %copy-done.1) | copy-start | bytes 589828
  41.3 5.9 %collective-permute-start.9 = (bf16[128,768]{1,0:T(8,128)(2,1)S(1)}, bf16[128,768]{1,0:T(8,128)(2,1)S(1)}, u32[]{:S(2)}, u32[]{:S(2)}) collective-permute-start(bf16[128,768]{1,0:T(8,128)(2,1)S(1)} %get-tuple-element.73), channel_id=1, source_target_pairs={{0,16},{16,0},{32,48},{48,32},{64,80},{80,64},{96,112},{112,96},{1... | collective-permute-start | bytes 589832 | tf_op jit(solution)/shard_map/ppermute | solution.py:474
  42.6 14.0 %collective-permute-start.11 = (bf16[128,768]{1,0:T(8,128)(2,1)}, bf16[128,768]{1,0:T(8,128)(2,1)S(1)}, u32[]{:S(2)}, u32[]{:S(2)}) collective-permute-start(bf16[128,768]{1,0:T(8,128)(2,1)} %get-tuple-element.75), channel_id=1, source_target_pairs={{0,16},{16,0},{32,48},{48,32},{64,80},{80,64},{96,112},{112,96},{1... | collective-permute-start | bytes 589832 | tf_op jit(solution)/shard_map/ppermute | solution.py:474
  47.2 9.4 %collective-permute-start.10 = (bf16[128,768]{1,0:T(8,128)(2,1)S(1)}, bf16[128,768]{1,0:T(8,128)(2,1)S(1)}, u32[]{:S(2)}, u32[]{:S(2)}) collective-permute-start(bf16[128,768]{1,0:T(8,128)(2,1)S(1)} %shard_map.106), channel_id=1, source_target_pairs={{0,112},{16,32},{32,16},{48,64},{64,48},{80,96},{96,80},{112,0},{1... | collective-permute-start | bytes 589832 | tf_op jit(solution)/shard_map/ppermute | solution.py:474
  51.7 4.9 %copy-start.8 = (bf16[128,768]{1,0:T(8,128)(2,1)S(1)}, bf16[128,768]{1,0:T(8,128)(2,1)}, u32[]{:S(2)}) copy-start(bf16[128,768]{1,0:T(8,128)(2,1)} %copy-done.7) | copy-start | bytes 589828
  51.7 4.9 %copy-start.10 = (bf16[128,768]{1,0:T(8,128)(2,1)S(1)}, bf16[128,768]{1,0:T(8,128)(2,1)}, u32[]{:S(2)}) copy-start(bf16[128,768]{1,0:T(8,128)(2,1)} %copy-done.9) | copy-start | bytes 589828
  51.7 22.4 %all-to-all-start.1 = ((bf16[8,128,768]{2,1,0:T(8,128)(2,1)}), bf16[8,128,768]{2,1,0:T(8,128)(2,1)}, u32[]{:S(2)}, u32[]{:S(2)}) async-start(bf16[8,128,768]{2,1,0:T(8,128)(2,1)} %bitcast.29), calls=%async_computation.1 | async-start | bytes 3145728 | tf_op jit(solution)/shard_map/all_to_all | solution.py:515
  56.6 7.2 %copy-start.4 = (bf16[128,768]{1,0:T(8,128)(2,1)S(1)}, bf16[128,768]{1,0:T(8,128)(2,1)}, u32[]{:S(2)}) copy-start(bf16[128,768]{1,0:T(8,128)(2,1)} %copy-done.3) | copy-start | bytes 589828
  56.7 7.2 %copy-start.6 = (bf16[128,768]{1,0:T(8,128)(2,1)S(1)}, bf16[128,768]{1,0:T(8,128)(2,1)}, u32[]{:S(2)}) copy-start(bf16[128,768]{1,0:T(8,128)(2,1)} %copy-done.5) | copy-start | bytes 589828
  56.8 5.8 %collective-permute-start.12 = (bf16[128,768]{1,0:T(8,128)(2,1)S(1)}, bf16[128,768]{1,0:T(8,128)(2,1)S(1)}, u32[]{:S(2)}, u32[]{:S(2)}) collective-permute-start(bf16[128,768]{1,0:T(8,128)(2,1)S(1)} %get-tuple-element.76), channel_id=1, source_target_pairs={{0,16},{16,0},{32,48},{48,32},{64,80},{80,64},{96,112},{112,96},{1... | collective-permute-start | bytes 589832 | tf_op jit(solution)/shard_map/ppermute | solution.py:474
  56.9 7.0 %collective-permute-start.13 = (bf16[128,768]{1,0:T(8,128)(2,1)S(1)}, bf16[128,768]{1,0:T(8,128)(2,1)S(1)}, u32[]{:S(2)}, u32[]{:S(2)}) collective-permute-start(bf16[128,768]{1,0:T(8,128)(2,1)S(1)} %get-tuple-element.77), channel_id=1, source_target_pairs={{0,112},{16,32},{32,16},{48,64},{64,48},{80,96},{96,80},{112,0},{1... | collective-permute-start | bytes 589832 | tf_op jit(solution)/shard_map/ppermute | solution.py:474
  59.3 8.5 %collective-permute-start = (bf16[128,1536]{1,0:T(8,128)(2,1)S(1)}, bf16[128,1536]{1,0:T(8,128)(2,1)S(1)}, u32[]{:S(2)}, u32[]{:S(2)}) collective-permute-start(bf16[128,1536]{1,0:T(8,128)(2,1)S(1)} %bitcast.25), channel_id=1, source_target_pairs={{0,1},{1,0},{2,3},{3,2},{4,5},{5,4},{6,7},{7,6},{8,9},{9,8},{10,11... | collective-permute-start | bytes 1179656 | tf_op jit(solution)/shard_map/ppermute | solution.py:468
  59.4 9.2 %collective-permute-start.1 = (bf16[128,1536]{1,0:T(8,128)(2,1)S(1)}, bf16[128,1536]{1,0:T(8,128)(2,1)}, u32[]{:S(2)}, u32[]{:S(2)}) collective-permute-start(bf16[128,1536]{1,0:T(8,128)(2,1)S(1)} %bitcast.28), channel_id=1, source_target_pairs={{0,1},{1,0},{2,3},{3,2},{4,5},{5,4},{6,7},{7,6},{8,9},{9,8},{10,11... | collective-permute-start | bytes 1179656 | tf_op jit(solution)/shard_map/ppermute | solution.py:468
  64.0 7.4 %collective-permute-start.14 = (bf16[128,768]{1,0:T(8,128)(2,1)S(1)}, bf16[128,768]{1,0:T(8,128)(2,1)S(1)}, u32[]{:S(2)}, u32[]{:S(2)}) collective-permute-start(bf16[128,768]{1,0:T(8,128)(2,1)S(1)} %get-tuple-element.78), channel_id=1, source_target_pairs={{0,112},{16,32},{32,16},{48,64},{64,48},{80,96},{96,80},{112,0},{1... | collective-permute-start | bytes 589832 | tf_op jit(solution)/shard_map/ppermute | solution.py:474
  67.8 5.7 %collective-permute-start.15 = (bf16[128,768]{1,0:T(8,128)(2,1)S(1)}, bf16[128,768]{1,0:T(8,128)(2,1)S(1)}, u32[]{:S(2)}, u32[]{:S(2)}) collective-permute-start(bf16[128,768]{1,0:T(8,128)(2,1)S(1)} %get-tuple-element.79), channel_id=1, source_target_pairs={{0,16},{16,0},{32,48},{48,32},{64,80},{80,64},{96,112},{112,96},{1... | collective-permute-start | bytes 589832 | tf_op jit(solution)/shard_map/ppermute | solution.py:474
  76.8 1.5 %collective-permute-start.16 = (bf16[256,384]{1,0:T(8,128)(2,1)S(1)}, bf16[256,384]{1,0:T(8,128)(2,1)S(1)}, u32[]{:S(2)}, u32[]{:S(2)}) collective-permute-start(bf16[256,384]{1,0:T(8,128)(2,1)S(1)} %get-tuple-element.81), channel_id=1, source_target_pairs={{0,1},{1,0},{2,3},{3,2},{4,5},{5,4},{6,7},{7,6},{8,9},{9,8},{10,11... | collective-permute-start | bytes 589832 | tf_op jit(solution)/shard_map/ppermute | solution.py:468
  79.8 4.6 %copy-start = (bf16[1536,768]{1,0:T(8,128)(2,1)S(1)}, bf16[1536,768]{1,0:T(8,128)(2,1)}, u32[]{:S(2)}) copy-start(bf16[1536,768]{1,0:T(8,128)(2,1)} %head_ref.1) | copy-start | bytes 7077892
  79.8 22.3 %all-to-all-start.2 = ((bf16[8,208,384]{2,1,0:T(8,128)(2,1)}), bf16[8,208,384]{2,1,0:T(8,128)(2,1)}, u32[]{:S(2)}, u32[]{:S(2)}) async-start(bf16[8,208,384]{2,1,0:T(8,128)(2,1)} %shard_map.111), calls=%async_computation.2 | async-start | bytes 2555904 | tf_op jit(solution)/shard_map/all_to_all | solution.py:529
  117.6 5.7 %collective-permute-start.17 = (f32[32,384]{1,0:T(8,128)S(1)}, f32[32,384]{1,0:T(8,128)S(1)}, u32[]{:S(2)}, u32[]{:S(2)}) collective-permute-start(f32[32,384]{1,0:T(8,128)S(1)} %convert_reduce_fusion.s_ref), channel_id=1, source_target_pairs={{0,2},{2,0},{1,3},{3,1},{4,6},{6,4},{5,7},{7,5},{8,10},{10,8},{9,1... | collective-permute-start | bytes 147464 | tf_op jit(solution)/shard_map/ppermute | solution.py:468
  123.3 1.3 %collective-permute-start.18 = (f32[32,384]{1,0:T(8,128)S(1)}, f32[32,384]{1,0:T(8,128)S(1)}, u32[]{:S(2)}, u32[]{:S(2)}) collective-permute-start(f32[32,384]{1,0:T(8,128)S(1)} %add.11), channel_id=1, source_target_pairs={{0,1},{1,0},{2,3},{3,2},{4,5},{5,4},{6,7},{7,6},{8,9},{9,8},{10,11... | collective-permute-start | bytes 147464 | tf_op jit(solution)/shard_map/ppermute | solution.py:468
  (4 other events, 8.7 us)
